TPU v7x, 32 devices: a whole 2x2x4 slice. The times are simulated.
32 devices in a mesh: groups: 1, seq: 32 (over z, y, x, core), dp: 1.
Axes of the slice: x: 2, y: 2, z: 4, core: 2. Of those that a mesh axis runs over, the one named last changes fastest.
Arguments:
- values: bfloat16 [1, 256, 256, 768], P(('groups', 'dp'), 'seq'), may hold values from -6 to 6
- kernel: bfloat16 [256, 256, 768], P('seq'), may hold values from -6 to 6
- cotangent: bfloat16 [1, 256, 256, 768], P(('groups', 'dp'), 'seq'), may hold values from -6 to 6
- inner_factor: bfloat16 [256, 256], replicated, may hold values from -0.375 to 0.375
- outer_factor: bfloat16 [256, 256], replicated, may hold values from -0.375 to 0.375
- return_outer: bfloat16 [256, 256], replicated, may hold values from -0.375 to 0.375
- return_inner: bfloat16 [256, 256], replicated, may hold values from -0.375 to 0.375
Outputs:
- grad_values: bfloat16 [1, 256, 256, 768], P(('groups', 'dp'), 'seq')
- grad_inner: float32 [256, 256], P('groups')
- grad_outer: float32 [256, 256], P('groups')
- grad_return_outer: float32 [256, 256], P('groups')
- grad_return_inner: float32 [256, 256], P('groups')
All inputs are finite; a program needn't handle non-finite values.
Results may differ from a plain program's by a relative error of at most 0.0064.
Values may be sent and summed in bfloat16 or wider, within the bound.
No kernel may reach another device: no remote copies, remote signals or barrier semaphores. Data moves between devices by JAX's collectives and lax.ppermute only.
A program may use at most 64 MiB of HBM per device.

v0:
```python
import math

import jax
import jax.numpy as jnp
from jax import lax
from jax.sharding import PartitionSpec as P


def per_device(values, kernel, cotangent, inner_factor, outer_factor, return_outer, return_inner):
    f32 = jnp.float32
    bf16 = jnp.bfloat16
    order_a = outer_factor.shape[0]
    order_b = inner_factor.shape[0]
    channels = kernel.shape[2]
    seq_count = values.shape[0] * lax.axis_size("dp")
    scale_a = 1.0 / math.sqrt(seq_count * order_a * channels)
    scale_b = 1.0 / math.sqrt(seq_count * order_b * channels)
    first = jnp.einsum("jb,sabc->sajc", inner_factor, values, preferred_element_type=f32).astype(
        bf16
    )
    piece = lax.all_to_all(first, "seq", split_axis=2, concat_axis=1, tiled=True)
    mixed = jnp.einsum("ia,sajc->sjic", outer_factor, piece, preferred_element_type=f32)
    first_moved = piece
    weighted = (mixed * kernel[None].astype(f32)).astype(bf16)
    returned_local = jnp.einsum(
        "ki,sjic->sjkc", return_outer, weighted, preferred_element_type=f32
    ).astype(bf16)
    returned = lax.all_to_all(returned_local, "seq", split_axis=2, concat_axis=1, tiled=True)
    grad_returned = jnp.einsum(
        "lj,sklc->skjc", return_inner, cotangent, preferred_element_type=f32
    ).astype(bf16)
    grad_gtwo = jnp.einsum("sklc,sjkc->lj", cotangent, returned, preferred_element_type=f32)
    piece = lax.all_to_all(grad_returned, "seq", split_axis=2, concat_axis=1, tiled=True)
    grad_mixed = jnp.einsum("ki,skjc->sjic", return_outer, piece, preferred_element_type=f32)
    grad_ret_moved = piece
    grad_gone = jnp.einsum("skjc,sjic->ki", grad_ret_moved, weighted, preferred_element_type=f32)
    grad_weighted = (grad_mixed * kernel[None].astype(f32)).astype(bf16)
    grad_first_moved = jnp.einsum(
        "ia,sjic->sajc", outer_factor, grad_weighted, preferred_element_type=f32
    ).astype(bf16)
    grad_ftwo = jnp.einsum("sjic,sajc->ia", grad_weighted, first_moved, preferred_element_type=f32)
    piece = lax.all_to_all(grad_first_moved, "seq", split_axis=1, concat_axis=2, tiled=True)
    grad_values = jnp.einsum(
        "jb,sajc->sabc", inner_factor, piece, preferred_element_type=f32
    ).astype(bf16)
    grad_fone = jnp.einsum("sajc,sabc->jb", piece, values, preferred_element_type=f32)
    summed = lax.psum((grad_fone, grad_ftwo, grad_gone, grad_gtwo), ("seq", "dp"))
    return (
        grad_values,
        summed[0] * scale_a,
        summed[1] * scale_b,
        summed[2] * scale_b,
        summed[3] * scale_a,
    )


def solution(mesh):
    return jax.shard_map(
        per_device,
        mesh=mesh,
        in_specs=(
            P(("groups", "dp"), "seq", None, None),
            P("seq", None, None),
            P(("groups", "dp"), "seq", None, None),
            P(),
            P(),
            P(),
            P(),
        ),
        out_specs=(
            P(("groups", "dp"), "seq", None, None),
            P("groups", None),
            P("groups", None),
            P("groups", None),
            P("groups", None),
        ),
        check_vma=False,
    )
```

profile of v0, /device:TPU:0, one launch (start us, length us, event | category | flops | bytes accessed | tf_op | source)
XLA Modules:
  0.0 470.3 jit_solution(5235010145666699886)
XLA Ops:
  7.2 0.0 copy-start
  7.2 4.7 %convert_bitcast_fusion.4 = bf16[1,8,256,768]{2,3,1,0:T(8,128)(2,1)} fusion(bf16[1,8,256,768]{3,2,1,0:T(8,128)(2,1)} %param.9, bf16[256,256]{1,0:T(8,128)(2,1)} %param.13), kind=kOutput, calls=%fused_computation.30 | convolution fusion | flops 806879232 | bytes 6422528 | tf_op jit(solution)/shard_map/lj,sklc->skjc/dot_general | solution.py:29
  11.9 5.1 %copy.46 = bf16[1,8,256,768]{3,1,0,2:T(8,128)(2,1)} copy(bf16[1,8,256,768]{2,3,1,0:T(8,128)(2,1)} %convert_bitcast_fusion.4) | data formatting | bytes 6291456 | tf_op jit(solution)/shard_map/convert_element_type | solution.py:31
  17.0 7.4 %all-to-all-start = ((bf16[1,8,256,768]{3,1,0,2:T(8,128)(2,1)}), bf16[1,8,256,768]{3,1,0,2:T(8,128)(2,1)}, u32[]{:S(2)}, u32[]{:S(2)}) async-start(bf16[1,8,256,768]{3,1,0,2:T(8,128)(2,1)} %copy.46), calls=%async_computation | async-start | bytes 6291456 | tf_op jit(solution)/shard_map/all_to_all | solution.py:33
  24.4 0.0 copy-done
  24.4 0.0 copy-done.12
  24.4 2.7 convert_bitcast_fusion.1
  27.1 5.1 %copy.55 = bf16[1,8,256,768]{3,1,0,2:T(8,128)(2,1)} copy(bf16[1,8,256,768]{2,3,1,0:T(8,128)(2,1)} %convert_bitcast_fusion.1) | data formatting | bytes 6291456 | tf_op jit(solution)/shard_map/convert_element_type | solution.py:18
  32.2 63.6 %all-to-all-done = bf16[1,8,256,768]{3,1,0,2:T(8,128)(2,1)} async-done(((bf16[1,8,256,768]{3,1,0,2:T(8,128)(2,1)}), bf16[1,8,256,768]{3,1,0,2:T(8,128)(2,1)}, u32[]{:S(2)}, u32[]{:S(2)}) %all-to-all-start) | async-done | bytes 3145760 | tf_op jit(solution)/shard_map/all_to_all | solution.py:33
  95.8 4.0 all-to-all-start.2
  99.9 4.6 copy.50
  104.5 2.5 copy.118
  107.0 0.0 copy-start.3
  107.1 0.0 copy-start.11
  107.1 0.4 copy.48
  107.5 2.6 copy-done.3
  110.1 0.0 copy-done.11
  110.1 1.7 fusion.3
  111.8 1.7 copy-done.7
  113.5 0.0 copy-done.10
  113.5 2.6 convert_bitcast_fusion.3
  116.1 5.0 %copy.51 = bf16[1,256,8,768]{3,2,0,1:T(8,128)(2,1)} copy(bf16[1,256,8,768]{1,3,2,0:T(8,128)(2,1)} %convert_bitcast_fusion.3) | data formatting | bytes 6291456 | tf_op jit(solution)/shard_map/convert_element_type | solution.py:40
  121.1 50.2 %all-to-all-done.2 = bf16[1,8,256,768]{3,1,0,2:T(8,128)(2,1)} async-done(((bf16[1,8,256,768]{3,1,0,2:T(8,128)(2,1)}), bf16[1,8,256,768]{3,1,0,2:T(8,128)(2,1)}, u32[]{:S(2)}, u32[]{:S(2)}) %all-to-all-start.2) | async-done | bytes 3145760 | tf_op jit(solution)/shard_map/all_to_all | solution.py:21
  171.4 4.2 all-to-all-start.1
  175.6 0.0 copy-start.4
  175.6 2.6 copy.117
  178.3 0.2 copy-done.4
  178.4 3.9 fusion.2
  182.3 0.0 copy-start.5
  182.3 1.7 copy-done.5
  184.0 2.7 convert_bitcast_fusion
  186.7 5.1 %copy.62 = bf16[1,8,256,768]{3,1,0,2:T(8,128)(2,1)} copy(bf16[1,8,256,768]{2,3,1,0:T(8,128)(2,1)} %convert_bitcast_fusion) | data formatting | bytes 6291456 | tf_op jit(solution)/shard_map/convert_element_type | solution.py:27
  191.8 55.1 %all-to-all-done.1 = bf16[1,256,8,768]{3,2,0,1:T(8,128)(2,1)} async-done(((bf16[1,256,8,768]{3,2,0,1:T(8,128)(2,1)}), bf16[1,256,8,768]{3,2,0,1:T(8,128)(2,1)}, u32[]{:S(2)}, u32[]{:S(2)}) %all-to-all-start.1) | async-done | bytes 3145760 | tf_op jit(solution)/shard_map/all_to_all | solution.py:42
  246.9 4.0 all-to-all-start.3
  250.9 0.3 all-reduce.3.cloned.1.call-start
  251.2 4.8 %fusion.39 = f32[256,256]{1,0:T(8,128)} fusion(bf16[8,256,768]{1,2,0:T(8,128)(2,1)} %copy-done.5, bf16[256,8,768]{2,1,0:T(8,128)(2,1)} %bitcast.136), kind=kOutput, calls=%fused_computation.39 | convolution fusion | flops 805306368 | bytes 6553600 | tf_op jit(solution)/shard_map/skjc,sjic->ki/dot_general | solution.py:36
  256.0 4.6 fusion.47
  260.6 3.6 fusion.42
  264.2 58.2 %all-to-all-done.3 = bf16[1,8,256,768]{3,1,0,2:T(8,128)(2,1)} async-done(((bf16[1,8,256,768]{3,1,0,2:T(8,128)(2,1)}), bf16[1,8,256,768]{3,1,0,2:T(8,128)(2,1)}, u32[]{:S(2)}, u32[]{:S(2)}) %all-to-all-start.3) | async-done | bytes 3145760 | tf_op jit(solution)/shard_map/all_to_all | solution.py:28
  322.4 2.6 copy.116
  325.0 0.2 copy-done.6
  325.2 4.3 fusion.50
  329.5 0.0 all-reduce.3.cloned.1.call-update
  329.6 4.6 convert_bitcast_fusion.2
  334.2 4.7 copy.66
  338.8 120.9 %all-reduce.3.cloned.1.call-done = (f32[256,256]{1,0:T(8,128)}, f32[256,256]{1,0:T(8,128)}, f32[256,256]{1,0:T(8,128)}, f32[256,256]{1,0:T(8,128)}) async-done(((f32[256,256]{1,0:T(8,128)}, f32[256,256]{1,0:T(8,128)}, f32[256,256]{1,0:T(8,128)}, f32[256,256]{1,0:T(8,128)}), (f32[256,256]{1,0:T(8,128)}, f32[256,256]{1,0:T(8,128)}, f32[256,256]{1,0:T(8,128)}, ...) | async-done | bytes 1048592 | tf_op jit(solution)/shard_map/psum | solution.py:47
  459.7 1.9 broadcast_multiply_fusion
  461.6 1.9 broadcast_multiply_fusion.2
  (12 shorter events, 0.0 us)
Async XLA Ops:
  7.2 17.2 %copy-start = (bf16[1,8,256,768]{3,2,1,0:T(8,128)(2,1)S(1)}, bf16[1,8,256,768]{3,2,1,0:T(8,128)(2,1)}, u32[]{:S(2)}) copy-start(bf16[1,8,256,768]{3,2,1,0:T(8,128)(2,1)} %param.7) | copy-start | bytes 9437188
  17.0 7.4 %copy-start.12 = (bf16[256,256]{1,0:T(8,128)(2,1)S(1)}, bf16[256,256]{1,0:T(8,128)(2,1)}, u32[]{:S(2)}) copy-start(bf16[256,256]{1,0:T(8,128)(2,1)} %param.10) | copy-start | bytes 393220
  17.0 78.9 %all-to-all-start = ((bf16[1,8,256,768]{3,1,0,2:T(8,128)(2,1)}), bf16[1,8,256,768]{3,1,0,2:T(8,128)(2,1)}, u32[]{:S(2)}, u32[]{:S(2)}) async-start(bf16[1,8,256,768]{3,1,0,2:T(8,128)(2,1)} %copy.46), calls=%async_computation | async-start | bytes 6291456 | tf_op jit(solution)/shard_map/all_to_all | solution.py:33
  95.8 75.5 %all-to-all-start.2 = ((bf16[1,8,256,768]{3,1,0,2:T(8,128)(2,1)}), bf16[1,8,256,768]{3,1,0,2:T(8,128)(2,1)}, u32[]{:S(2)}, u32[]{:S(2)}) async-start(bf16[1,8,256,768]{3,1,0,2:T(8,128)(2,1)} %copy.55), calls=%async_computation.2 | async-start | bytes 6291456 | tf_op jit(solution)/shard_map/all_to_all | solution.py:21
  107.0 3.0 copy-start.3
  107.1 3.0 copy-start.11
  107.5 4.3 copy-start.9
  110.1 3.4 copy-start.10
  111.8 1.7 copy-start.7
  171.4 75.6 %all-to-all-start.1 = ((bf16[1,256,8,768]{3,2,0,1:T(8,128)(2,1)}), bf16[1,256,8,768]{3,2,0,1:T(8,128)(2,1)}, u32[]{:S(2)}, u32[]{:S(2)}) async-start(bf16[1,256,8,768]{3,2,0,1:T(8,128)(2,1)} %copy.51), calls=%async_computation.1 | async-start | bytes 6291456 | tf_op jit(solution)/shard_map/all_to_all | solution.py:42
  175.6 2.8 copy-start.4
  178.3 4.1 copy-start.1
  182.3 1.7 copy-start.5
  246.9 75.4 %all-to-all-start.3 = ((bf16[1,8,256,768]{3,1,0,2:T(8,128)(2,1)}), bf16[1,8,256,768]{3,1,0,2:T(8,128)(2,1)}, u32[]{:S(2)}, u32[]{:S(2)}) async-start(bf16[1,8,256,768]{3,1,0,2:T(8,128)(2,1)} %copy.62), calls=%async_computation.3 | async-start | bytes 6291456 | tf_op jit(solution)/shard_map/all_to_all | solution.py:28
  250.9 208.8 %all-reduce.3.cloned.1.call-start = ((), (), s32[]{:S(2)}) async-start(), calls=%async_computation.4 | async-start | bytes 2097152 | tf_op jit(solution)/shard_map/psum | solution.py:47
  251.2 4.8 %copy-start.2 = (bf16[1,8,256,768]{3,2,1,0:T(8,128)(2,1)S(1)}, bf16[1,8,256,768]{3,2,1,0:T(8,128)(2,1)}, u32[]{:S(2)}) copy-start(bf16[1,8,256,768]{3,2,1,0:T(8,128)(2,1)} %copy-done.1) | copy-start | bytes 9437188
  251.2 4.8 %copy-start.8 = (bf16[8,256,768]{1,2,0:T(8,128)(2,1)S(1)}, bf16[8,256,768]{1,2,0:T(8,128)(2,1)}, u32[]{:S(2)}) copy-start(bf16[8,256,768]{1,2,0:T(8,128)(2,1)} %copy-done.7) | copy-start | bytes 9437188
  322.4 2.8 copy-start.6
Sparse Core Ops, SparseCore 0:
  329.7 129.9 all-reduce.2
where the time goes:
time: 471 us; the launch traced here: 470 us
  waiting for transfers between devices  348 us (74%)
  local copies, waits for them, and re-layouts  44 us (9%)
  matrix products  40.3 us (9%)
  starting transfers between devices  19.9 us (4%)
  between operations  14.2 us (3%)
    psum x1, waiting for transfers between devices, per_device(): lax.psum((grad_fone, grad_ftwo, grad_gone, grad_gtwo), ('seq', 'dp'))  121 us
    all_to_all x1, waiting for transfers between devices, per_device(): lax.all_to_all(grad_returned, 'seq', split_axis=2, concat_axis=1, tiled=T...  63.6 us
    all_to_all x1, waiting for transfers between devices, per_device(): lax.all_to_all(returned_local, 'seq', split_axis=2, concat_axis=1, tiled=...  58.2 us
    all_to_all x1, waiting for transfers between devices, per_device(): lax.all_to_all(grad_first_moved, 'seq', split_axis=1, concat_axis=2, tile...  55.1 us
    all_to_all x1, waiting for transfers between devices, per_device(): lax.all_to_all(first, 'seq', split_axis=2, concat_axis=1, tiled=True)  50.2 us
    unnamed x28, local copies, waits for them, and re-layouts  15.6 us
  transfers between devices with their start and end apart: 5, of which 5 were waited for; matrix products, arithmetic and copies ran while one was open for 13% of the time, Pallas kernels for 0%

commit v1 on v0

--- a/solution.py
+++ b/solution.py
@@ -3,12 +3,239 @@
 import jax
 import jax.numpy as jnp
 from jax import lax
+from jax.experimental import pallas as pl
+from jax.experimental.pallas import tpu as pltpu
 from jax.sharding import PartitionSpec as P
 
-
-def per_device(values, kernel, cotangent, inner_factor, outer_factor, return_outer, return_inner):
-    f32 = jnp.float32
-    bf16 = jnp.bfloat16
+F32 = jnp.float32
+BF16 = jnp.bfloat16
+LANES = 128
+VMEM = 56 * 2**20
+
+
+def dot(x, y, dims):
+    return lax.dot_general(x, y, ((dims[:1], dims[1:]), ((), ())), preferred_element_type=F32)
+
+
+def call(body, grid, ins, outs, scratch, flops, moved):
+    return pl.pallas_call(
+        body,
+        grid=grid,
+        in_specs=[spec for spec in ins],
+        out_specs=[spec for spec, _ in outs],
+        out_shape=[shape for _, shape in outs],
+        scratch_shapes=scratch,
+        compiler_params=pltpu.CompilerParams(
+            vmem_limit_bytes=VMEM, dimension_semantics=("arbitrary",) * len(grid)
+        ),
+        cost_estimate=pl.CostEstimate(flops=flops, bytes_accessed=moved, transcendentals=0),
+    )
+
+
+def square(order):
+    return pl.BlockSpec((order, order), lambda *g: (0, 0))
+
+
+def apply_inner(x, factor, side, members):
+    rows, order, channels = x.shape
+    part = order // members
+    step = max(1, rows // 4)
+
+    def body(x_ref, f_ref, o_ref):
+        for r in range(step):
+            y = dot(f_ref[...], x_ref[r], (side, 0))
+            o_ref[:, r] = y.reshape(members, part, channels).astype(BF16)
+
+    return call(
+        body,
+        (rows // step,),
+        [pl.BlockSpec((step, order, channels), lambda g: (g, 0, 0)), square(order)],
+        [
+            (
+                pl.BlockSpec((members, step, part, channels), lambda g: (0, g, 0, 0)),
+                jax.ShapeDtypeStruct((members, rows, part, channels), BF16),
+            )
+        ],
+        [],
+        2 * order * x.size,
+        4 * x.size,
+    )(x, factor)[0]
+
+
+def tile_pairs(part, width):
+    tiles = [(j, t) for j in range(part) for t in range(width // LANES)]
+    return [tiles[p : p + 2] for p in range(0, len(tiles), 2)]
+
+
+def spread(ref, value):
+    order, part, width = value.shape
+    for t in range(width // LANES):
+        ref[t] = value[:, :, t * LANES : (t + 1) * LANES].astype(F32).reshape(order * part, LANES)
+
+
+def take(ref, pair, order, part):
+    got = [ref[t, pl.ds(j, order, stride=part), :] for j, t in pair]
+    return jnp.concatenate(got, axis=1).astype(BF16)
+
+
+def put(ref, pair, order, part, value):
+    for n, (j, t) in enumerate(pair):
+        ref[t, pl.ds(j, order, stride=part), :] = value[:, n * LANES : (n + 1) * LANES]
+
+
+def gather(ref, members, part):
+    tiles = [ref[t].reshape(members, -1, part, LANES).astype(BF16) for t in range(ref.shape[0])]
+    return jnp.concatenate(tiles, axis=-1)
+
+
+def pick(ref, pair):
+    return jnp.concatenate([ref[j, :, t * LANES : (t + 1) * LANES] for j, t in pair], axis=1)
+
+
+def backward_mixed(moved, kernel, outer, back, members):
+    order, part, channels = moved.shape
+    width = min(channels, 2 * LANES)
+    local = order // members
+
+    def body(m_ref, k_ref, o_ref, b_ref, gw_ref, gf_ref, held, result):
+        spread(held, m_ref[...])
+        for pair in tile_pairs(part, width):
+            mixed = dot(b_ref[...], take(held, pair, order, part), (0, 0))
+            gw = (mixed * pick(k_ref, pair).astype(F32)).astype(BF16)
+            for n, (j, t) in enumerate(pair):
+                gw_ref[j, :, t * LANES : (t + 1) * LANES] = gw[:, n * LANES : (n + 1) * LANES]
+            put(result, pair, order, part, dot(o_ref[...], gw, (0, 0)))
+        gf_ref[...] = gather(result, members, part)
+
+    return call(
+        body,
+        (channels // width,),
+        [
+            pl.BlockSpec((order, part, width), lambda g: (0, 0, g)),
+            pl.BlockSpec((part, order, width), lambda g: (0, 0, g)),
+            square(order),
+            square(order),
+        ],
+        [
+            (
+                pl.BlockSpec((part, order, width), lambda g: (0, 0, g)),
+                jax.ShapeDtypeStruct((part, order, channels), BF16),
+            ),
+            (
+                pl.BlockSpec((members, local, part, width), lambda g: (0, 0, 0, g)),
+                jax.ShapeDtypeStruct((members, local, part, channels), BF16),
+            ),
+        ],
+        [pltpu.VMEM((width // LANES, order * part, LANES), F32)] * 2,
+        4 * order * moved.size,
+        8 * moved.size,
+    )(moved, kernel, outer, back)
+
+
+def forward_mixed(first, grad_ret, kernel, gw, outer, back, members):
+    order, part, channels = first.shape
+    width = min(channels, 2 * LANES)
+    local = order // members
+
+    def body(f_ref, g_ref, k_ref, gw_ref, o_ref, b_ref, ret_ref, go_ref, gr_ref, held, held_g, result):
+        @pl.when(pl.program_id(0) == 0)
+        def _():
+            go_ref[...] = jnp.zeros_like(go_ref)
+            gr_ref[...] = jnp.zeros_like(gr_ref)
+
+        spread(held, f_ref[...])
+        spread(held_g, g_ref[...])
+        for pair in tile_pairs(part, width):
+            first_j = take(held, pair, order, part)
+            mixed = dot(o_ref[...], first_j, (1, 0))
+            weighted = (mixed * pick(k_ref, pair).astype(F32)).astype(BF16)
+            put(result, pair, order, part, dot(b_ref[...], weighted, (1, 0)))
+            go_ref[...] += dot(pick(gw_ref, pair), first_j, (1, 1))
+            gr_ref[...] += dot(take(held_g, pair, order, part), weighted, (1, 1))
+        ret_ref[...] = gather(result, members, part)
+
+    moved = pl.BlockSpec((order, part, width), lambda g: (0, 0, g))
+    mine = pl.BlockSpec((part, order, width), lambda g: (0, 0, g))
+    small = (square(order), jax.ShapeDtypeStruct((order, order), F32))
+    return call(
+        body,
+        (channels // width,),
+        [moved, moved, mine, mine, square(order), square(order)],
+        [
+            (
+                pl.BlockSpec((members, local, part, width), lambda g: (0, 0, 0, g)),
+                jax.ShapeDtypeStruct((members, local, part, channels), BF16),
+            ),
+            small,
+            small,
+        ],
+        [pltpu.VMEM((width // LANES, order * part, LANES), F32)] * 3,
+        8 * order * first.size,
+        10 * first.size,
+    )(first, grad_ret, kernel, gw, outer, back)
+
+
+def finish_values(grad_first, values, inner):
+    members, rows, part, channels = grad_first.shape
+    order = members * part
+    step = max(1, rows // 4)
+
+    def body(g_ref, v_ref, f_ref, gv_ref, gi_ref):
+        @pl.when(pl.program_id(0) == 0)
+        def _():
+            gi_ref[...] = jnp.zeros_like(gi_ref)
+
+        for r in range(step):
+            g = g_ref[:, r].astype(F32).reshape(order, channels).astype(BF16)
+            gv_ref[r] = dot(f_ref[...], g, (0, 0)).astype(BF16)
+            gi_ref[...] += dot(g, v_ref[r], (1, 1))
+
+    rowed = pl.BlockSpec((step, order, channels), lambda g: (g, 0, 0))
+    return call(
+        body,
+        (rows // step,),
+        [pl.BlockSpec((members, step, part, channels), lambda g: (0, g, 0, 0)), rowed, square(order)],
+        [
+            (rowed, jax.ShapeDtypeStruct(values.shape, BF16)),
+            (square(order), jax.ShapeDtypeStruct((order, order), F32)),
+        ],
+        [],
+        4 * order * values.size,
+        6 * values.size,
+    )(grad_first, values, inner)
+
+
+def finish_return(returned, cotangent):
+    members, rows, part, channels = returned.shape
+    order = members * part
+    step = max(1, rows // 4)
+
+    def body(r_ref, c_ref, o_ref):
+        @pl.when(pl.program_id(0) == 0)
+        def _():
+            o_ref[...] = jnp.zeros_like(o_ref)
+
+        for r in range(step):
+            ret = r_ref[:, r].astype(F32).reshape(order, channels).astype(BF16)
+            o_ref[...] += dot(c_ref[r], ret, (1, 1))
+
+    return call(
+        body,
+        (rows // step,),
+        [
+            pl.BlockSpec((members, step, part, channels), lambda g: (0, g, 0, 0)),
+            pl.BlockSpec((step, order, channels), lambda g: (g, 0, 0)),
+        ],
+        [(square(order), jax.ShapeDtypeStruct((order, order), F32))],
+        [],
+        2 * order * cotangent.size,
+        4 * cotangent.size,
+    )(returned, cotangent)[0]
+
+
+def plain(values, kernel, cotangent, inner_factor, outer_factor, return_outer, return_inner):
+    f32 = F32
+    bf16 = BF16
     order_a = outer_factor.shape[0]
     order_b = inner_factor.shape[0]
     channels = kernel.shape[2]
@@ -54,6 +281,67 @@
     )
 
 
+def swap(x, bit):
+    size = lax.axis_size("seq")
+    return lax.ppermute(x, "seq", [(i, i ^ bit) for i in range(size)])
+
+
+def total(x):
+    size = lax.axis_size("seq")
+    plane = [[z * 8 + p for p in range(8)] for z in range(size // 8)]
+    rows, columns = x.shape
+    parts = lax.all_to_all(
+        x.astype(BF16).reshape(8, rows // 8, columns), "seq", 0, 0, axis_index_groups=plane, tiled=True
+    )
+    held = jnp.sum(parts.astype(F32), axis=0).astype(BF16)
+    sent = sum(swap(held, 8 * d).astype(F32) for d in (2,)) + held.astype(F32)
+    sent = sent.astype(BF16)
+    part = sent.astype(F32) + swap(sent, 8).astype(F32)
+    out = jnp.broadcast_to(part.astype(BF16)[None], (8, rows // 8, columns))
+    return lax.all_to_all(out, "seq", 0, 0, axis_index_groups=plane, tiled=True).reshape(rows, columns)
+
+
+def per_device(values, kernel, cotangent, inner_factor, outer_factor, return_outer, return_inner):
+    members = lax.axis_size("seq")
+    order = outer_factor.shape[0]
+    rows, channels = kernel.shape[0], kernel.shape[2]
+    if (
+        members != 32
+        or lax.axis_size("dp") != 1
+        or values.shape[0] != 1
+        or rows != 8
+        or inner_factor.shape[0] != order
+        or channels % (2 * LANES)
+    ):
+        return plain(
+            values, kernel, cotangent, inner_factor, outer_factor, return_outer, return_inner
+        )
+    scale = 1.0 / math.sqrt(order * channels)
+
+    def move(x):
+        return lax.all_to_all(x, "seq", 0, 0, tiled=True)
+
+    grad_ret = move(apply_inner(cotangent[0], return_inner, 0, members))
+    sent = apply_inner(values[0], inner_factor, 1, members)
+    sent, grad_ret = lax.optimization_barrier((sent, grad_ret))
+    first = move(sent)
+    grad_ret = grad_ret.reshape(order, rows, channels)
+    gw, sent = backward_mixed(grad_ret, kernel, outer_factor, return_outer, members)
+    sent, first = lax.optimization_barrier((sent, first))
+    grad_first = move(sent)
+    first = first.reshape(order, rows, channels)
+    sent, grad_outer, grad_back = forward_mixed(
+        first, grad_ret, kernel, gw, outer_factor, return_outer, members
+    )
+    sent, grad_first = lax.optimization_barrier((sent, grad_first))
+    returned = move(sent)
+    grad_values, grad_inner = finish_values(grad_first, values[0], inner_factor)
+    grad_last = finish_return(returned, cotangent[0])
+    grads = total(jnp.concatenate((grad_inner, grad_outer, grad_back, grad_last), axis=1))
+    grads = jnp.split(grads.astype(F32) * scale, 4, axis=1)
+    return (grad_values[None], *grads)
+
+
 def solution(mesh):
     return jax.shard_map(
         per_device,

time: 471 us -> 357 us (0.76)
  waiting for transfers between devices: 348 us -> 264 us
  matrix products: 40.3 us -> 0 us
  local copies, waits for them, and re-layouts: 44 us -> 4.42 us
  Pallas kernels: 0 us -> 39.3 us
  blocking collectives: 0 us -> 25.1 us
  between operations: 14.2 us -> 0.75 us
    psum x1 -> x0, waiting for transfers between devices: 121 us -> none  [per_device(): lax.psum((grad_fone, grad_ftwo, grad_gone, grad_gtwo), ('seq', 'dp'))]
    dot_general x11 -> x0, matrix products: 40.3 us -> none  [the longest x1 4.8 us: per_device(): jnp.einsum('skjc,sjic->ki', grad_ret_moved, weighted, preferred_element_t...]
    pallas_call x0 -> x6, Pallas kernels: none -> 39.3 us  [the longest x1 10.5 us: forward_mixed(): call(body, (channels // width,), [moved, moved, mine, mine, square(order)...]
    all_to_all x4, waiting for transfers between devices: 227 us -> 254 us  [move(): return lax.all_to_all(x, 'seq', 0, 0, tiled=True)]
    all_to_all x0 -> x2, blocking collectives: none -> 25.1 us  [the longest x1 13 us: total(): lax.all_to_all(x.astype(BF16).reshape(8, rows // 8, columns), 'seq', 0, 0...]
    convert_element_type x4 -> x0, local copies, waits for them, and re-layouts: 20.2 us -> none  [the longest x1 5.09 us: per_device(): jnp.einsum('jb,sabc->sajc', inner_factor, values, preferred_element_type=...]
    unnamed x28 -> x6, local copies, waits for them, and re-layouts: 15.6 us -> 3.38 us
    ppermute x0 -> x2, waiting for transfers between devices: none -> 9.4 us  [swap(): return lax.ppermute(x, 'seq', [(i, i ^ bit) for i in range(size)])]
  transfers between devices with their start and end apart: 5 -> 6, of which waited for: 5 -> 6; matrix products, arithmetic and copies ran while one was open for 13% -> 1% of each run, Pallas kernels for 0% -> 8%
where the time goes in v1:
time: 357 us; the launch traced here: 356 us
  waiting for transfers between devices  264 us (74%)
  Pallas kernels  39.3 us (11%)
  blocking collectives  25.1 us (7%)
  starting transfers between devices  19.5 us (5%)
  local copies, waits for them, and re-layouts  4.42 us (1%)
    all_to_all x4, waiting for transfers between devices, move(): return lax.all_to_all(x, 'seq', 0, 0, tiled=True)  254 us
    all_to_all x4, starting transfers between devices, move(): return lax.all_to_all(x, 'seq', 0, 0, tiled=True)  19.3 us
    all_to_all x1, blocking collectives, total(): lax.all_to_all(x.astype(BF16).reshape(8, rows // 8, columns), 'seq', 0, 0...  13 us
    all_to_all x1, blocking collectives, total(): lax.all_to_all(out, 'seq', 0, 0, axis_index_groups=plane, tiled=True)  12.2 us
    pallas_call x1, Pallas kernels, forward_mixed(): call(body, (channels // width,), [moved, moved, mine, mine, square(order)...  10.5 us
    pallas_call x2, Pallas kernels, apply_inner(): call(body, (rows // step,), [pl.BlockSpec((step, order, channels), lambda...  9.94 us
    ppermute x2, waiting for transfers between devices, swap(): return lax.ppermute(x, 'seq', [(i, i ^ bit) for i in range(size)])  9.4 us
    pallas_call x1, Pallas kernels, backward_mixed(): call(body, (channels // width,), [pl.BlockSpec((order, part, width), lamb...  7.81 us
  transfers between devices with their start and end apart: 6, of which 6 were waited for; matrix products, arithmetic and copies ran while one was open for 1% of the time, Pallas kernels for 8%

profile of v1, /device:TPU:0, one launch (start us, length us, event | category | flops | bytes accessed | tf_op | source)
XLA Modules:
  0.0 356.0 jit_solution(15073280065095496344)
XLA Ops:
  0.6 4.9 %shard_map.111 = bf16[32,8,8,768]{3,2,1,0:T(8,128)(2,1)} custom-call(bf16[8,256,768]{2,1,0:T(8,128)(2,1)} %bitcast.14, bf16[256,256]{1,0:T(8,128)(2,1)} %f_ref.4), custom_call_target="tpu_custom_call" | custom-call | flops 805306368 | bytes 6291456 | tf_op jit(solution)/shard_map/pallas_call | solution.py:49
  5.6 7.3 %all-to-all-start = ((bf16[32,8,8,768]{3,2,1,0:T(8,128)(2,1)}), bf16[32,8,8,768]{3,2,1,0:T(8,128)(2,1)S(1)}, u32[]{:S(2)}, u32[]{:S(2)}) async-start(bf16[32,8,8,768]{3,2,1,0:T(8,128)(2,1)} %shard_map.111), calls=%async_computation | async-start | bytes 6291456 | tf_op jit(solution)/shard_map/all_to_all | solution.py:322
  12.9 5.0 %shard_map.110 = bf16[32,8,8,768]{3,2,1,0:T(8,128)(2,1)} custom-call(bf16[8,256,768]{2,1,0:T(8,128)(2,1)} %bitcast.12, bf16[256,256]{1,0:T(8,128)(2,1)} %f_ref.5), custom_call_target="tpu_custom_call" | custom-call | flops 805306368 | bytes 6291456 | tf_op jit(solution)/shard_map/pallas_call | solution.py:49
  17.9 66.4 %all-to-all-done = bf16[32,8,8,768]{3,2,1,0:T(8,128)(2,1)S(1)} async-done(((bf16[32,8,8,768]{3,2,1,0:T(8,128)(2,1)}), bf16[32,8,8,768]{3,2,1,0:T(8,128)(2,1)S(1)}, u32[]{:S(2)}, u32[]{:S(2)}) %all-to-all-start) | async-done | bytes 3145760 | tf_op jit(solution)/shard_map/all_to_all | solution.py:322
  84.3 0.0 copy-start
  84.3 1.7 copy-done
  86.0 4.0 %all-to-all-start.1 = ((bf16[32,8,8,768]{3,2,1,0:T(8,128)(2,1)}), bf16[32,8,8,768]{3,2,1,0:T(8,128)(2,1)}, u32[]{:S(2)}, u32[]{:S(2)}) async-start(bf16[32,8,8,768]{3,2,1,0:T(8,128)(2,1)} %shard_map.110), calls=%async_computation.1 | async-start | bytes 6291456 | tf_op jit(solution)/shard_map/all_to_all | solution.py:322
  90.0 7.8 %shard_map.112 = (bf16[8,256,768]{2,1,0:T(8,128)(2,1)}, bf16[32,8,8,768]{3,2,1,0:T(8,128)(2,1)}) custom-call(bf16[256,8,768]{2,1,0:T(8,128)(2,1)} %bitcast.10, bf16[8,256,768]{2,1,0:T(8,128)(2,1)} %k_ref.3, bf16[256,256]{1,0:T(8,128)(2,1)} %o_ref.3, bf16[256,256]{1,0:T(8,128)(2,1)} %b_ref.3), custom_call_target="tpu_custom_call" | custom-call | flops 1610612736 | bytes 12582912 | tf_op jit(solution)/shard_map/pallas_call | solution.py:110
  97.8 63.6 %all-to-all-done.1 = bf16[32,8,8,768]{3,2,1,0:T(8,128)(2,1)} async-done(((bf16[32,8,8,768]{3,2,1,0:T(8,128)(2,1)}), bf16[32,8,8,768]{3,2,1,0:T(8,128)(2,1)}, u32[]{:S(2)}, u32[]{:S(2)}) %all-to-all-start.1) | async-done | bytes 3145760 | tf_op jit(solution)/shard_map/all_to_all | solution.py:322
  161.5 3.9 %all-to-all-start.2 = ((bf16[32,8,8,768]{3,2,1,0:T(8,128)(2,1)}), bf16[32,8,8,768]{3,2,1,0:T(8,128)(2,1)S(1)}, u32[]{:S(2)}, u32[]{:S(2)}) async-start(bf16[32,8,8,768]{3,2,1,0:T(8,128)(2,1)} %get-tuple-element.24), calls=%async_computation.2 | async-start | bytes 6291456 | tf_op jit(solution)/shard_map/all_to_all | solution.py:322
  165.4 10.5 %shard_map.113 = (bf16[32,8,8,768]{3,2,1,0:T(8,128)(2,1)}, f32[256,256]{1,0:T(8,128)}, f32[256,256]{1,0:T(8,128)}) custom-call(bf16[256,8,768]{2,1,0:T(8,128)(2,1)} %bitcast.3.f_ref, bf16[256,8,768]{2,1,0:T(8,128)(2,1)} %bitcast.11, bf16[8,256,768]{2,1,0:T(8,128)(2,1)} %k_ref.3, bf16[8,256,768]{2,1,0:T(8,128)(2,1)} %get-tuple-element.22.gw_ref, ...), custom_call_target="tpu_custom_call" | custom-call | flops 3221225472 | bytes 15728640 | tf_op jit(solution)/shard_map/pallas_call | solution.py:160
  176.0 60.9 %all-to-all-done.2.g_ref = bf16[32,8,8,768]{3,2,1,0:T(8,128)(2,1)S(1)} async-done(((bf16[32,8,8,768]{3,2,1,0:T(8,128)(2,1)}), bf16[32,8,8,768]{3,2,1,0:T(8,128)(2,1)S(1)}, u32[]{:S(2)}, u32[]{:S(2)}) %all-to-all-start.2) | async-done | bytes 3145760 | tf_op jit(solution)/shard_map/all_to_all | solution.py:322
  236.9 0.0 copy-start.1
  236.9 0.0 copy-start.2
  236.9 1.7 copy-done.1
  238.6 4.0 %all-to-all-start.3 = ((bf16[32,8,8,768]{3,2,1,0:T(8,128)(2,1)}), bf16[32,8,8,768]{3,2,1,0:T(8,128)(2,1)}, u32[]{:S(2)}, u32[]{:S(2)}) async-start(bf16[32,8,8,768]{3,2,1,0:T(8,128)(2,1)} %get-tuple-element.30), calls=%async_computation.3 | async-start | bytes 6291456 | tf_op jit(solution)/shard_map/all_to_all | solution.py:322
  242.7 1.0 convert.18
  243.6 0.0 copy-done.2
  243.7 6.2 %shard_map.114 = (bf16[8,256,768]{2,1,0:T(8,128)(2,1)}, f32[256,256]{1,0:T(8,128)}) custom-call(bf16[32,8,8,768]{3,2,1,0:T(8,128)(2,1)} %copy-done.1, bf16[8,256,768]{2,1,0:T(8,128)(2,1)} %bitcast.13, bf16[256,256]{1,0:T(8,128)(2,1)} %f_ref.5), custom_call_target="tpu_custom_call" | custom-call | flops 1610612736 | bytes 9437184 | tf_op jit(solution)/shard_map/pallas_call | solution.py:194
  249.8 1.0 convert.17
  250.8 63.3 %all-to-all-done.3.r_ref = bf16[32,8,8,768]{3,2,1,0:T(8,128)(2,1)} async-done(((bf16[32,8,8,768]{3,2,1,0:T(8,128)(2,1)}), bf16[32,8,8,768]{3,2,1,0:T(8,128)(2,1)}, u32[]{:S(2)}, u32[]{:S(2)}) %all-to-all-start.3) | async-done | bytes 3145760 | tf_op jit(solution)/shard_map/all_to_all | solution.py:322
  314.1 4.9 %shard_map.115 = f32[256,256]{1,0:T(8,128)} custom-call(bf16[32,8,8,768]{3,2,1,0:T(8,128)(2,1)} %all-to-all-done.3.r_ref, bf16[8,256,768]{2,1,0:T(8,128)(2,1)} %bitcast.15), custom_call_target="tpu_custom_call" | custom-call | flops 805306368 | bytes 6291456 | tf_op jit(solution)/shard_map/pallas_call | solution.py:222
  319.0 1.0 convert.20
  319.9 0.1 pad_maximum_fusion
  320.0 13.0 %all_to_all.30 = bf16[8,32,1024]{2,1,0:T(8,128)(2,1)S(1)} all-to-all(bf16[8,32,1024]{2,1,0:T(8,128)(2,1)S(1)} %pad_maximum_fusion), channel_id=1, replica_groups={{0,1,2,3,4,5,6,7},{8,9,10,11,12,13,14,15},{16,17,18,19,20,21,22,23},{24..., dimensions={0} | all-to-all | bytes 1048576 | tf_op jit(solution)/shard_map/all_to_all | solution.py:293
  333.0 0.1 reduce_sum.12
  333.1 0.1 collective-permute-start
  333.1 5.2 %collective-permute-done = bf16[32,1024]{1,0:T(8,128)(2,1)S(1)} collective-permute-done((bf16[32,1024]{1,0:T(8,128)(2,1)S(1)}, bf16[32,1024]{1,0:T(8,128)(2,1)S(1)}, u32[]{:S(2)}, u32[]{:S(2)}) %collective-permute-start) | collective-permute-done | bytes 65568 | tf_op jit(solution)/shard_map/ppermute | solution.py:286
  338.3 0.1 collective-permute-start.1
  338.4 4.3 %collective-permute-done.1 = bf16[32,1024]{1,0:T(8,128)(2,1)S(1)} collective-permute-done((bf16[32,1024]{1,0:T(8,128)(2,1)S(1)}, bf16[32,1024]{1,0:T(8,128)(2,1)S(1)}, u32[]{:S(2)}, u32[]{:S(2)}) %collective-permute-start.1) | collective-permute-done | bytes 65568 | tf_op jit(solution)/shard_map/ppermute | solution.py:286
  342.7 0.1 broadcast_in_dim.10
  342.7 12.2 %all_to_all.31 = bf16[8,32,1024]{2,1,0:T(8,128)(2,1)S(1)} all-to-all(bf16[8,32,1024]{2,1,0:T(8,128)(2,1)S(1)} %broadcast_in_dim.10), channel_id=1, replica_groups={{0,1,2,3,4,5,6,7},{8,9,10,11,12,13,14,15},{16,17,18,19,20,21,22,23},{24..., dimensions={0} | all-to-all | bytes 1048576 | tf_op jit(solution)/shard_map/all_to_all | solution.py:301
  354.9 0.1 convert_multiply_fusion
  355.0 1.0 fusion
  (3 shorter events, 0.1 us)
Async XLA Ops:
  5.6 78.8 %all-to-all-start = ((bf16[32,8,8,768]{3,2,1,0:T(8,128)(2,1)}), bf16[32,8,8,768]{3,2,1,0:T(8,128)(2,1)S(1)}, u32[]{:S(2)}, u32[]{:S(2)}) async-start(bf16[32,8,8,768]{3,2,1,0:T(8,128)(2,1)} %shard_map.111), calls=%async_computation | async-start | bytes 6291456 | tf_op jit(solution)/shard_map/all_to_all | solution.py:322
  84.3 1.7 copy-start
  86.0 75.5 %all-to-all-start.1 = ((bf16[32,8,8,768]{3,2,1,0:T(8,128)(2,1)}), bf16[32,8,8,768]{3,2,1,0:T(8,128)(2,1)}, u32[]{:S(2)}, u32[]{:S(2)}) async-start(bf16[32,8,8,768]{3,2,1,0:T(8,128)(2,1)} %shard_map.110), calls=%async_computation.1 | async-start | bytes 6291456 | tf_op jit(solution)/shard_map/all_to_all | solution.py:322
  161.5 75.4 %all-to-all-start.2 = ((bf16[32,8,8,768]{3,2,1,0:T(8,128)(2,1)}), bf16[32,8,8,768]{3,2,1,0:T(8,128)(2,1)S(1)}, u32[]{:S(2)}, u32[]{:S(2)}) async-start(bf16[32,8,8,768]{3,2,1,0:T(8,128)(2,1)} %get-tuple-element.24), calls=%async_computation.2 | async-start | bytes 6291456 | tf_op jit(solution)/shard_map/all_to_all | solution.py:322
  236.9 1.7 copy-start.1
  236.9 6.7 %copy-start.2 = (f32[256,256]{1,0:T(8,128)S(1)}, f32[256,256]{1,0:T(8,128)}, u32[]{:S(2)}) copy-start(f32[256,256]{1,0:T(8,128)} %get-tuple-element.29) | copy-start | bytes 786436
  238.6 75.5 %all-to-all-start.3 = ((bf16[32,8,8,768]{3,2,1,0:T(8,128)(2,1)}), bf16[32,8,8,768]{3,2,1,0:T(8,128)(2,1)}, u32[]{:S(2)}, u32[]{:S(2)}) async-start(bf16[32,8,8,768]{3,2,1,0:T(8,128)(2,1)} %get-tuple-element.30), calls=%async_computation.3 | async-start | bytes 6291456 | tf_op jit(solution)/shard_map/all_to_all | solution.py:322
  333.1 5.2 %collective-permute-start = (bf16[32,1024]{1,0:T(8,128)(2,1)S(1)}, bf16[32,1024]{1,0:T(8,128)(2,1)S(1)}, u32[]{:S(2)}, u32[]{:S(2)}) collective-permute-start(bf16[32,1024]{1,0:T(8,128)(2,1)S(1)} %reduce_sum.12), channel_id=1, source_target_pairs={{0,16},{1,17},{2,18},{3,19},{4,20},{5,21},{6,22},{7,23},{8,24},{9,... | collective-permute-start | bytes 196616 | tf_op jit(solution)/shard_map/ppermute | solution.py:286
  338.3 4.3 %collective-permute-start.1 = (bf16[32,1024]{1,0:T(8,128)(2,1)S(1)}, bf16[32,1024]{1,0:T(8,128)(2,1)S(1)}, u32[]{:S(2)}, u32[]{:S(2)}) collective-permute-start(bf16[32,1024]{1,0:T(8,128)(2,1)S(1)} %add_convert_fusion.1), channel_id=1, source_target_pairs={{0,8},{1,9},{2,10},{3,11},{4,12},{5,13},{6,14},{7,15},{8,0},{9,1},... | collective-permute-start | bytes 196616 | tf_op jit(solution)/shard_map/ppermute | solution.py:286

commit v2 on v1

--- a/solution.py
+++ b/solution.py
@@ -281,65 +281,112 @@
     )
 
 
-def swap(x, bit):
+def swap(x, bits):
     size = lax.axis_size("seq")
-    return lax.ppermute(x, "seq", [(i, i ^ bit) for i in range(size)])
+    return lax.ppermute(x, "seq", [(i, i ^ bits) for i in range(size)])
+
+
+def exchange(x, members):
+    size = lax.axis_size("seq")
+    groups = [list(range(g, g + members)) for g in range(0, size, members)]
+    return lax.all_to_all(x, "seq", 0, 0, axis_index_groups=groups, tiled=True)
 
 
 def total(x):
+    rows, columns = x.shape
+    parts = exchange(x.astype(BF16).reshape(8, rows // 8, columns), 8)
+    held = jnp.sum(parts.astype(F32), axis=0)
+    held = held + swap(held, 16)
+    held = held + swap(held, 8)
+    out = jnp.broadcast_to(held[None], (8, rows // 8, columns))
+    return exchange(out, 8).reshape(rows, columns)
+
+
+class Part:
+    def __init__(self, low, members):
+        self.low = low
+        self.members = members
+        self.splits = lax.axis_size("seq") // members
+        self.mine = lax.axis_index("seq") // members
+
+    def lanes(self, split):
+        return self.low + split * LANES
+
+    def bring(self, x):
+        rows, order, _ = x.shape
+        out = jnp.zeros((self.splits * rows, order, LANES), BF16)
+        for d in range(self.splits):
+            other = self.mine ^ d
+            piece = lax.dynamic_slice(x, (0, 0, self.lanes(other)), (rows, order, LANES))
+            piece = swap(piece, d * self.members) if d else piece
+            out = lax.dynamic_update_slice(out, piece, (other * rows, 0, 0))
+        return out
+
+    def give(self, out, x):
+        rows, order, _ = out.shape
+        for d in range(self.splits):
+            other = self.mine ^ d
+            piece = lax.dynamic_slice(x, (other * rows, 0, 0), (rows, order, LANES))
+            piece = swap(piece, d * self.members) if d else piece
+            out = lax.dynamic_update_slice(out, piece, (0, 0, self.lanes(other)))
+        return out
+
+    def sort(self, matrix, axis, back=False):
+        shape = matrix.shape
+        s, m = self.splits, self.members
+        cut = (m, s) if back else (s, m)
+        cut = shape[:axis] + cut + (shape[axis] // (s * m),) + shape[axis + 1 :]
+        return jnp.swapaxes(matrix.reshape(cut), axis, axis + 1).reshape(shape)
+
+
+def per_device(values, kernel, cotangent, inner_factor, outer_factor, return_outer, return_inner):
     size = lax.axis_size("seq")
-    plane = [[z * 8 + p for p in range(8)] for z in range(size // 8)]
-    rows, columns = x.shape
-    parts = lax.all_to_all(
-        x.astype(BF16).reshape(8, rows // 8, columns), "seq", 0, 0, axis_index_groups=plane, tiled=True
-    )
-    held = jnp.sum(parts.astype(F32), axis=0).astype(BF16)
-    sent = sum(swap(held, 8 * d).astype(F32) for d in (2,)) + held.astype(F32)
-    sent = sent.astype(BF16)
-    part = sent.astype(F32) + swap(sent, 8).astype(F32)
-    out = jnp.broadcast_to(part.astype(BF16)[None], (8, rows // 8, columns))
-    return lax.all_to_all(out, "seq", 0, 0, axis_index_groups=plane, tiled=True).reshape(rows, columns)
-
-
-def per_device(values, kernel, cotangent, inner_factor, outer_factor, return_outer, return_inner):
-    members = lax.axis_size("seq")
     order = outer_factor.shape[0]
     rows, channels = kernel.shape[0], kernel.shape[2]
     if (
-        members != 32
+        size != 32
         or lax.axis_size("dp") != 1
         or values.shape[0] != 1
         or rows != 8
         or inner_factor.shape[0] != order
-        or channels % (2 * LANES)
+        or channels != 6 * LANES
     ):
         return plain(
             values, kernel, cotangent, inner_factor, outer_factor, return_outer, return_inner
         )
     scale = 1.0 / math.sqrt(order * channels)
-
-    def move(x):
-        return lax.all_to_all(x, "seq", 0, 0, tiled=True)
-
-    grad_ret = move(apply_inner(cotangent[0], return_inner, 0, members))
-    sent = apply_inner(values[0], inner_factor, 1, members)
-    sent, grad_ret = lax.optimization_barrier((sent, grad_ret))
-    first = move(sent)
-    grad_ret = grad_ret.reshape(order, rows, channels)
-    gw, sent = backward_mixed(grad_ret, kernel, outer_factor, return_outer, members)
-    sent, first = lax.optimization_barrier((sent, first))
-    grad_first = move(sent)
-    first = first.reshape(order, rows, channels)
-    sent, grad_outer, grad_back = forward_mixed(
-        first, grad_ret, kernel, gw, outer_factor, return_outer, members
-    )
-    sent, grad_first = lax.optimization_barrier((sent, grad_first))
-    returned = move(sent)
-    grad_values, grad_inner = finish_values(grad_first, values[0], inner_factor)
-    grad_last = finish_return(returned, cotangent[0])
-    grads = total(jnp.concatenate((grad_inner, grad_outer, grad_back, grad_last), axis=1))
-    grads = jnp.split(grads.astype(F32) * scale, 4, axis=1)
-    return (grad_values[None], *grads)
+    grads = []
+    out = jnp.zeros(values.shape[1:], BF16)
+    for part in (Part(0, 8), Part(4 * LANES, 16)):
+        m = part.members
+        inner = part.sort(inner_factor, 0)
+        outer = part.sort(outer_factor, 1)
+        back = part.sort(return_outer, 0)
+        last = part.sort(return_inner, 1)
+
+        cot = part.bring(cotangent[0])
+        ker = part.bring(kernel)
+        val = part.bring(values[0])
+        flat = (order, cot.shape[0], LANES)
+        grad_ret = exchange(apply_inner(cot, last, 0, m), m).reshape(flat)
+        gw, sent = backward_mixed(grad_ret, ker, outer, back, m)
+        grad_first = exchange(sent, m)
+        first = exchange(apply_inner(val, inner, 1, m), m).reshape(flat)
+        sent, grad_outer, grad_back = forward_mixed(first, grad_ret, ker, gw, outer, back, m)
+        returned = exchange(sent, m)
+        grad_values, grad_inner = finish_values(grad_first, val, inner)
+        grad_last = finish_return(returned, cot)
+        out = part.give(out, grad_values)
+        grads.append(
+            (
+                part.sort(grad_inner, 0, True),
+                part.sort(grad_outer, 1, True),
+                part.sort(grad_back, 0, True),
+                part.sort(grad_last, 1, True),
+            )
+        )
+    grads = total(jnp.concatenate([sum(g) for g in zip(*grads)], axis=1)) * scale
+    return (out[None], *jnp.split(grads, 4, axis=1))
 
 
 def solution(mesh):

time: 357 us -> 481 us (1.35)
  starting transfers between devices: 19.5 us -> 91.9 us
  local copies, waits for them, and re-layouts: 4.42 us -> 56.5 us
  Pallas kernels: 39.3 us -> 69.7 us
  blocking collectives: 25.1 us -> 0 us
  waiting for transfers between devices: 264 us -> 256 us
    all_to_all x4 -> x10, waiting for transfers between devices: 254 us -> 30.4 us  [exchange(): return lax.all_to_all(x, 'seq', 0, 0, axis_index_groups=groups, tiled=True)]
    ppermute x2 -> x18, waiting for transfers between devices: 9.4 us -> 226 us  [swap(): return lax.ppermute(x, 'seq', [(i, i ^ bits) for i in range(size)])]
    ppermute x2 -> x18, starting transfers between devices: 0.14 us -> 51.1 us  [swap(): return lax.ppermute(x, 'seq', [(i, i ^ bits) for i in range(size)])]
    all_to_all x2 -> x0, blocking collectives: 25.1 us -> none  [the longest x1 13 us: total(): lax.all_to_all(x.astype(BF16).reshape(8, rows // 8, columns), 'seq', 0, 0...]
    all_to_all x4 -> x10, starting transfers between devices: 19.3 us -> 40.9 us  [exchange(): return lax.all_to_all(x, 'seq', 0, 0, axis_index_groups=groups, tiled=True)]
    dynamic_update_slice x0 -> x20, local copies, waits for them, and re-layouts: none -> 13.8 us  [the longest x6 8.11 us: give(): out = lax.dynamic_update_slice(out, piece, (0, 0, self.lanes(other)))]
    reshape x0 -> x20, local copies, waits for them, and re-layouts: none -> 13.3 us  [sort(): return jnp.swapaxes(matrix.reshape(cut), axis, axis + 1).reshape(shape)]
    pallas_call x1 -> x2, Pallas kernels: 10.5 us -> 19.3 us  [forward_mixed(): call(body, (channels // width,), [moved, moved, mine, mine, square(order)...]
  transfers between devices with their start and end apart: 6 -> 28, of which waited for: 6 -> 16; matrix products, arithmetic and copies ran while one was open for 1% -> 8% of each run, Pallas kernels for 8% -> 13%
where the time goes in v2:
time: 481 us; the launch traced here: 479 us
  waiting for transfers between devices  256 us (53%)
  starting transfers between devices  91.9 us (19%)
  Pallas kernels  69.7 us (14%)
  local copies, waits for them, and re-layouts  56.5 us (12%)
    ppermute x18, waiting for transfers between devices, swap(): return lax.ppermute(x, 'seq', [(i, i ^ bits) for i in range(size)])  226 us
    ppermute x18, starting transfers between devices, swap(): return lax.ppermute(x, 'seq', [(i, i ^ bits) for i in range(size)])  51.1 us
    all_to_all x10, starting transfers between devices, exchange(): return lax.all_to_all(x, 'seq', 0, 0, axis_index_groups=groups, tiled=True)  40.9 us
    all_to_all x10, waiting for transfers between devices, exchange(): return lax.all_to_all(x, 'seq', 0, 0, axis_index_groups=groups, tiled=True)  30.4 us
    pallas_call x2, Pallas kernels, forward_mixed(): call(body, (channels // width,), [moved, moved, mine, mine, square(order)...  19.3 us
    pallas_call x4, Pallas kernels, apply_inner(): call(body, (rows // step,), [pl.BlockSpec((step, order, channels), lambda...  17.7 us
    pallas_call x2, Pallas kernels, backward_mixed(): call(body, (channels // width,), [pl.BlockSpec((order, part, width), lamb...  14 us
    reshape x20, local copies, waits for them, and re-layouts, sort(): return jnp.swapaxes(matrix.reshape(cut), axis, axis + 1).reshape(shape)  13.3 us
  transfers between devices with their start and end apart: 28, of which 16 were waited for; matrix products, arithmetic and copies ran while one was open for 8% of the time, Pallas kernels for 13%

profile of v2, /device:TPU:0, one launch (start us, length us, event | category | flops | bytes accessed | tf_op | source)
XLA Modules:
  0.0 478.7 jit_solution(4285899450516135271)
XLA Ops:
  0.7 2.8 dynamic-slice_bitcast_fusion.1
  3.5 3.0 collective-permute-start
  6.5 2.6 collective-permute-start.1
  12.1 17.0 %collective-permute-done = bf16[8,256,128]{2,1,0:T(8,128)(2,1)S(1)} collective-permute-done((bf16[8,256,128]{2,1,0:T(8,128)(2,1)}, bf16[8,256,128]{2,1,0:T(8,128)(2,1)S(1)}, u32[]{:S(2)}, u32[]{:S(2)}) %collective-permute-start) | collective-permute-done | bytes 524320 | tf_op jit(solution)/shard_map/ppermute | solution.py:286
  29.2 15.8 %collective-permute-done.1 = bf16[8,256,128]{2,1,0:T(8,128)(2,1)S(1)} collective-permute-done((bf16[8,256,128]{2,1,0:T(8,128)(2,1)}, bf16[8,256,128]{2,1,0:T(8,128)(2,1)S(1)}, u32[]{:S(2)}, u32[]{:S(2)}) %collective-permute-start.1) | collective-permute-done | bytes 524320 | tf_op jit(solution)/shard_map/ppermute | solution.py:286
  46.4 4.7 shard_map.110
  51.2 4.4 all-to-all-start
  55.6 2.6 dynamic-slice_bitcast_fusion
  58.1 10.3 %collective-permute-start.6 = (bf16[8,256,128]{2,1,0:T(8,128)(2,1)S(1)}, bf16[8,256,128]{2,1,0:T(8,128)(2,1)S(1)}, u32[]{:S(2)}, u32[]{:S(2)}) collective-permute-start(bf16[8,256,128]{2,1,0:T(8,128)(2,1)S(1)} %get-tuple-element.36), channel_id=1, source_target_pairs={{0,8},{1,9},{2,10},{3,11},{4,12},{5,13},{6,14},{7,15},{8,0},{9,1},... | collective-permute-start | bytes 1572872 | tf_op jit(solution)/shard_map/ppermute | solution.py:286
  73.7 18.0 %collective-permute-done.6 = bf16[8,256,128]{2,1,0:T(8,128)(2,1)S(1)} collective-permute-done((bf16[8,256,128]{2,1,0:T(8,128)(2,1)S(1)}, bf16[8,256,128]{2,1,0:T(8,128)(2,1)S(1)}, u32[]{:S(2)}, u32[]{:S(2)}) %collective-permute-start.6) | collective-permute-done | bytes 524320 | tf_op jit(solution)/shard_map/ppermute | solution.py:286
  91.7 14.9 %collective-permute-done.7 = bf16[8,256,128]{2,1,0:T(8,128)(2,1)S(1)} collective-permute-done((bf16[8,256,128]{2,1,0:T(8,128)(2,1)S(1)}, bf16[8,256,128]{2,1,0:T(8,128)(2,1)S(1)}, u32[]{:S(2)}, u32[]{:S(2)}) %collective-permute-start.7) | collective-permute-done | bytes 524320 | tf_op jit(solution)/shard_map/ppermute | solution.py:286
  108.1 4.6 shard_map.116
  112.7 4.5 all-to-all-start.4
  117.2 11.9 %collective-permute-start.12 = (bf16[8,256,128]{2,1,0:T(8,128)(2,1)S(1)}, bf16[8,256,128]{2,1,0:T(8,128)(2,1)S(1)}, u32[]{:S(2)}, u32[]{:S(2)}) collective-permute-start(bf16[8,256,128]{2,1,0:T(8,128)(2,1)S(1)} %copy-done.19), channel_id=1, source_target_pairs={{0,16},{1,17},{2,18},{3,19},{4,20},{5,21},{6,22},{7,23},{8,24},{9,... | collective-permute-start | bytes 1572872 | tf_op jit(solution)/shard_map/ppermute | solution.py:286
  129.9 22.9 %collective-permute-done.12 = bf16[8,256,128]{2,1,0:T(8,128)(2,1)S(1)} collective-permute-done((bf16[8,256,128]{2,1,0:T(8,128)(2,1)S(1)}, bf16[8,256,128]{2,1,0:T(8,128)(2,1)S(1)}, u32[]{:S(2)}, u32[]{:S(2)}) %collective-permute-start.12) | collective-permute-done | bytes 524320 | tf_op jit(solution)/shard_map/ppermute | solution.py:286
  153.8 4.2 shard_map.113
  158.1 4.1 all-to-all-start.2
  164.3 24.4 %collective-permute-done.14 = bf16[8,256,128]{2,1,0:T(8,128)(2,1)S(1)} collective-permute-done((bf16[8,256,128]{2,1,0:T(8,128)(2,1)S(1)}, bf16[8,256,128]{2,1,0:T(8,128)(2,1)S(1)}, u32[]{:S(2)}, u32[]{:S(2)}) %collective-permute-start.14) | collective-permute-done | bytes 524320 | tf_op jit(solution)/shard_map/ppermute | solution.py:286
  189.8 4.1 shard_map.118
  193.8 4.5 all-to-all-start.5
  204.6 2.0 collective-permute-start.4
  208.9 26.1 %collective-permute-done.3 = bf16[8,256,128]{2,1,0:T(8,128)(2,1)} collective-permute-done((bf16[8,256,128]{2,1,0:T(8,128)(2,1)}, bf16[8,256,128]{2,1,0:T(8,128)(2,1)}, u32[]{:S(2)}, u32[]{:S(2)}) %collective-permute-start.3) | collective-permute-done | bytes 524320 | tf_op jit(solution)/shard_map/ppermute | solution.py:286
  237.2 10.4 %collective-permute-done.5 = bf16[8,256,128]{2,1,0:T(8,128)(2,1)S(1)} collective-permute-done((bf16[8,256,128]{2,1,0:T(8,128)(2,1)}, bf16[8,256,128]{2,1,0:T(8,128)(2,1)S(1)}, u32[]{:S(2)}, u32[]{:S(2)}) %collective-permute-start.5) | collective-permute-done | bytes 524320 | tf_op jit(solution)/shard_map/ppermute | solution.py:286
  249.0 9.6 %shard_map.111 = (bf16[32,256,128]{2,1,0:T(8,128)(2,1)}, bf16[8,32,32,128]{3,2,1,0:T(8,128)(2,1)}) custom-call(bf16[256,32,128]{2,1,0:T(8,128)(2,1)} %bitcast.7.m_ref.g_ref, bf16[32,256,128]{2,1,0:T(8,128)(2,1)} %copy-done.2, bf16[256,256]{1,0:T(8,128)(2,1)} %copy.26.o_ref, bf16[256,256]{1,0:T(8,128)(2,1)} %bitcast.120), custom_call_target="tpu_custom_call" | custom-call | flops 1073741824 | bytes 8388608 | tf_op jit(solution)/shard_map/pallas_call | solution.py:110
  258.6 3.8 all-to-all-start.1
  262.5 13.6 %shard_map.117 = (bf16[8,32,32,128]{3,2,1,0:T(8,128)(2,1)}, f32[256,256]{1,0:T(8,128)}, f32[256,256]{1,0:T(8,128)}) custom-call(bf16[256,32,128]{2,1,0:T(8,128)(2,1)} %bitcast.51.f_ref, bf16[256,32,128]{2,1,0:T(8,128)(2,1)} %bitcast.7.m_ref.g_ref, bf16[32,256,128]{2,1,0:T(8,128)(2,1)} %copy-done.2, bf16[32,256,128]{2,1,0:T(8,128)(2,1)} %get-tuple-element.25.gw_ref, ...), custom_call_target="tpu_custom_call" | custom-call | flops 2147483648 | bytes 10485760 | tf_op jit(solution)/shard_map/pallas_call | solution.py:160
  276.1 12.9 %all-to-all-done.1.g_ref = bf16[8,32,32,128]{3,2,1,0:T(8,128)(2,1)S(1)} async-done(((bf16[8,32,32,128]{3,2,1,0:T(8,128)(2,1)}), bf16[8,32,32,128]{3,2,1,0:T(8,128)(2,1)S(1)}, u32[]{:S(2)}, u32[]{:S(2)}) %all-to-all-start.1) | async-done | bytes 2097184 | tf_op jit(solution)/shard_map/all_to_all | solution.py:292
  290.3 4.4 all-to-all-start.6
  294.6 6.6 %collective-permute-start.13 = (bf16[8,256,128]{2,1,0:T(8,128)(2,1)}, bf16[8,256,128]{2,1,0:T(8,128)(2,1)S(1)}, u32[]{:S(2)}, u32[]{:S(2)}) collective-permute-start(bf16[8,256,128]{2,1,0:T(8,128)(2,1)} %get-tuple-element.39), channel_id=1, source_target_pairs={{0,16},{1,17},{2,18},{3,19},{4,20},{5,21},{6,22},{7,23},{8,24},{9,... | collective-permute-start | bytes 1572872 | tf_op jit(solution)/shard_map/ppermute | solution.py:286
  302.7 22.4 %collective-permute-done.13 = bf16[8,256,128]{2,1,0:T(8,128)(2,1)S(1)} collective-permute-done((bf16[8,256,128]{2,1,0:T(8,128)(2,1)}, bf16[8,256,128]{2,1,0:T(8,128)(2,1)S(1)}, u32[]{:S(2)}, u32[]{:S(2)}) %collective-permute-start.13) | collective-permute-done | bytes 524320 | tf_op jit(solution)/shard_map/ppermute | solution.py:286
  326.2 4.4 shard_map.114
  330.6 4.0 all-to-all-start.3
  334.6 5.7 %shard_map.119 = (bf16[16,16,16,128]{3,2,1,0:T(8,128)(2,1)}, f32[256,256]{1,0:T(8,128)}, f32[256,256]{1,0:T(8,128)}) custom-call(bf16[256,16,128]{2,1,0:T(8,128)(2,1)} %bitcast.56.f_ref, bf16[256,16,128]{2,1,0:T(8,128)(2,1)} %bitcast.118, bf16[16,256,128]{2,1,0:T(8,128)(2,1)} %copy-done.6, bf16[16,256,128]{2,1,0:T(8,128)(2,1)} %get-tuple-element.27.gw_ref, ...), custom_call_target="tpu_custom_call" | custom-call | flops 1073741824 | bytes 5242880 | tf_op jit(solution)/shard_map/pallas_call | solution.py:160
  340.3 10.5 %all-to-all-done.3.g_ref = bf16[16,16,16,128]{3,2,1,0:T(8,128)(2,1)S(1)} async-done(((bf16[16,16,16,128]{3,2,1,0:T(8,128)(2,1)}), bf16[16,16,16,128]{3,2,1,0:T(8,128)(2,1)S(1)}, u32[]{:S(2)}, u32[]{:S(2)}) %all-to-all-start.3) | async-done | bytes 1048608 | tf_op jit(solution)/shard_map/all_to_all | solution.py:292
  350.8 3.7 all-to-all-start.7
  358.7 5.8 %shard_map.112 = (bf16[32,256,128]{2,1,0:T(8,128)(2,1)}, f32[256,256]{1,0:T(8,128)}) custom-call(bf16[8,32,32,128]{3,2,1,0:T(8,128)(2,1)} %copy-done.11, bf16[32,256,128]{2,1,0:T(8,128)(2,1)} %copy-done.1, bf16[256,256]{1,0:T(8,128)(2,1)} %bitcast.123), custom_call_target="tpu_custom_call" | custom-call | flops 1073741824 | bytes 6291456 | tf_op jit(solution)/shard_map/pallas_call | solution.py:194
  366.3 4.5 shard_map.120
  372.5 4.6 shard_map.115
  379.8 3.8 shard_map.121
  388.4 4.0 all-to-all-start.8
  395.1 7.0 %all-to-all-done.8 = bf16[8,32,1024]{2,1,0:T(8,128)(2,1)S(1)} async-done(((bf16[8,32,1024]{2,1,0:T(8,128)(2,1)}), bf16[8,32,1024]{2,1,0:T(8,128)(2,1)S(1)}, u32[]{:S(2)}, u32[]{:S(2)}) %all-to-all-start.8) | async-done | bytes 524320 | tf_op jit(solution)/shard_map/all_to_all | solution.py:292
  402.2 2.0 collective-permute-start.16
  405.2 18.2 %collective-permute-done.16 = f32[32,1024]{1,0:T(8,128)S(1)} collective-permute-done((f32[32,1024]{1,0:T(8,128)S(1)}, f32[32,1024]{1,0:T(8,128)S(1)}, u32[]{:S(2)}, u32[]{:S(2)}) %collective-permute-start.16) | collective-permute-done | bytes 131104 | tf_op jit(solution)/shard_map/ppermute | solution.py:286
  426.4 3.0 collective-permute-start.11
  430.0 4.8 collective-permute-done.17
  435.9 3.6 all-to-all-start.9
  441.4 16.2 %collective-permute-done.10 = bf16[8,256,128]{2,1,0:T(8,128)(2,1)} collective-permute-done((bf16[8,256,128]{2,1,0:T(8,128)(2,1)}, bf16[8,256,128]{2,1,0:T(8,128)(2,1)}, u32[]{:S(2)}, u32[]{:S(2)}) %collective-permute-start.10) | collective-permute-done | bytes 524320 | tf_op jit(solution)/shard_map/ppermute | solution.py:286
  462.1 14.7 %collective-permute-done.15 = bf16[8,256,128]{2,1,0:T(8,128)(2,1)S(1)} collective-permute-done((bf16[8,256,128]{2,1,0:T(8,128)(2,1)S(1)}, bf16[8,256,128]{2,1,0:T(8,128)(2,1)S(1)}, u32[]{:S(2)}, u32[]{:S(2)}) %collective-permute-start.15) | collective-permute-done | bytes 524320 | tf_op jit(solution)/shard_map/ppermute | solution.py:286
  (145 shorter events, 64.1 us)
Async XLA Ops:
  0.7 8.4 %copy-start.23 = (bf16[256,256]{1,0:T(8,128)(2,1)S(1)}, bf16[256,256]{1,0:T(8,128)(2,1)}, u32[]{:S(2)}) copy-start(bf16[256,256]{1,0:T(8,128)(2,1)} %param.13) | copy-start | bytes 393220
  3.5 25.6 %collective-permute-start = (bf16[8,256,128]{2,1,0:T(8,128)(2,1)}, bf16[8,256,128]{2,1,0:T(8,128)(2,1)S(1)}, u32[]{:S(2)}, u32[]{:S(2)}) collective-permute-start(bf16[8,256,128]{2,1,0:T(8,128)(2,1)} %get-tuple-element.48), channel_id=1, source_target_pairs={{0,8},{1,9},{2,10},{3,11},{4,12},{5,13},{6,14},{7,15},{8,0},{9,1},... | collective-permute-start | bytes 1572872 | tf_op jit(solution)/shard_map/ppermute | solution.py:286
  6.5 38.4 %collective-permute-start.1 = (bf16[8,256,128]{2,1,0:T(8,128)(2,1)}, bf16[8,256,128]{2,1,0:T(8,128)(2,1)S(1)}, u32[]{:S(2)}, u32[]{:S(2)}) collective-permute-start(bf16[8,256,128]{2,1,0:T(8,128)(2,1)} %get-tuple-element.47), channel_id=1, source_target_pairs={{0,16},{1,17},{2,18},{3,19},{4,20},{5,21},{6,22},{7,23},{8,24},{9,... | collective-permute-start | bytes 1572872 | tf_op jit(solution)/shard_map/ppermute | solution.py:286
  9.1 35.9 %collective-permute-start.2 = (bf16[8,256,128]{2,1,0:T(8,128)(2,1)S(1)}, bf16[8,256,128]{2,1,0:T(8,128)(2,1)S(1)}, u32[]{:S(2)}, u32[]{:S(2)}) collective-permute-start(bf16[8,256,128]{2,1,0:T(8,128)(2,1)S(1)} %get-tuple-element.46), channel_id=1, source_target_pairs={{0,24},{1,25},{2,26},{3,27},{4,28},{5,29},{6,30},{7,31},{8,16},{9,... | collective-permute-start | bytes 1572872 | tf_op jit(solution)/shard_map/ppermute | solution.py:286
  45.1 1.3 copy-start
  51.2 61.6 %all-to-all-start = ((bf16[8,32,32,128]{3,2,1,0:T(8,128)(2,1)}), bf16[8,32,32,128]{3,2,1,0:T(8,128)(2,1)}, u32[]{:S(2)}, u32[]{:S(2)}) async-start(bf16[8,32,32,128]{3,2,1,0:T(8,128)(2,1)} %shard_map.110), calls=%async_computation | async-start | bytes 4194304 | tf_op jit(solution)/shard_map/all_to_all | solution.py:292
  55.5 15.4 %copy-start.17 = (bf16[256,256]{1,0:T(8,128)(2,1)S(1)}, bf16[256,256]{1,0:T(8,128)(2,1)}, u32[]{:S(2)}) copy-start(bf16[256,256]{1,0:T(8,128)(2,1)} %param.10) | copy-start | bytes 393220
  58.1 33.5 %collective-permute-start.6 = (bf16[8,256,128]{2,1,0:T(8,128)(2,1)S(1)}, bf16[8,256,128]{2,1,0:T(8,128)(2,1)S(1)}, u32[]{:S(2)}, u32[]{:S(2)}) collective-permute-start(bf16[8,256,128]{2,1,0:T(8,128)(2,1)S(1)} %get-tuple-element.36), channel_id=1, source_target_pairs={{0,8},{1,9},{2,10},{3,11},{4,12},{5,13},{6,14},{7,15},{8,0},{9,1},... | collective-permute-start | bytes 1572872 | tf_op jit(solution)/shard_map/ppermute | solution.py:286
  68.4 38.2 %collective-permute-start.7 = (bf16[8,256,128]{2,1,0:T(8,128)(2,1)S(1)}, bf16[8,256,128]{2,1,0:T(8,128)(2,1)S(1)}, u32[]{:S(2)}, u32[]{:S(2)}) collective-permute-start(bf16[8,256,128]{2,1,0:T(8,128)(2,1)S(1)} %get-tuple-element.35), channel_id=1, source_target_pairs={{0,16},{1,17},{2,18},{3,19},{4,20},{5,21},{6,22},{7,23},{8,24},{9,... | collective-permute-start | bytes 1572872 | tf_op jit(solution)/shard_map/ppermute | solution.py:286
  69.4 37.3 %collective-permute-start.8 = (bf16[8,256,128]{2,1,0:T(8,128)(2,1)S(1)}, bf16[8,256,128]{2,1,0:T(8,128)(2,1)S(1)}, u32[]{:S(2)}, u32[]{:S(2)}) collective-permute-start(bf16[8,256,128]{2,1,0:T(8,128)(2,1)S(1)} %get-tuple-element.34), channel_id=1, source_target_pairs={{0,24},{1,25},{2,26},{3,27},{4,28},{5,29},{6,30},{7,31},{8,16},{9,... | collective-permute-start | bytes 1572872 | tf_op jit(solution)/shard_map/ppermute | solution.py:286
  73.6 33.1 %copy-start.8 = (bf16[16,256,128]{2,1,0:T(8,128)(2,1)}, bf16[16,256,128]{2,1,0:T(8,128)(2,1)S(1)}, u32[]{:S(2)}) copy-start(bf16[16,256,128]{2,1,0:T(8,128)(2,1)S(1)} %get-tuple-element.37) | copy-start | bytes 3145732
  106.8 1.3 copy-start.1
  112.7 4.5 copy-start.19
  112.7 45.3 %all-to-all-start.4 = ((bf16[8,32,32,128]{3,2,1,0:T(8,128)(2,1)}), bf16[8,32,32,128]{3,2,1,0:T(8,128)(2,1)}, u32[]{:S(2)}, u32[]{:S(2)}) async-start(bf16[8,32,32,128]{3,2,1,0:T(8,128)(2,1)} %shard_map.116), calls=%async_computation.4 | async-start | bytes 4194304 | tf_op jit(solution)/shard_map/all_to_all | solution.py:292
  117.2 35.5 %collective-permute-start.12 = (bf16[8,256,128]{2,1,0:T(8,128)(2,1)S(1)}, bf16[8,256,128]{2,1,0:T(8,128)(2,1)S(1)}, u32[]{:S(2)}, u32[]{:S(2)}) collective-permute-start(bf16[8,256,128]{2,1,0:T(8,128)(2,1)S(1)} %copy-done.19), channel_id=1, source_target_pairs={{0,16},{1,17},{2,18},{3,19},{4,20},{5,21},{6,22},{7,23},{8,24},{9,... | collective-permute-start | bytes 1572872 | tf_op jit(solution)/shard_map/ppermute | solution.py:286
  153.8 34.9 %copy-start.9 = (bf16[16,256,128]{2,1,0:T(8,128)(2,1)S(1)}, bf16[16,256,128]{2,1,0:T(8,128)(2,1)}, u32[]{:S(2)}) copy-start(bf16[16,256,128]{2,1,0:T(8,128)(2,1)} %copy-done.8) | copy-start | bytes 3145732
  158.1 4.1 copy-start.20
  158.1 35.8 %all-to-all-start.2 = ((bf16[16,16,16,128]{3,2,1,0:T(8,128)(2,1)}), bf16[16,16,16,128]{3,2,1,0:T(8,128)(2,1)S(1)}, u32[]{:S(2)}, u32[]{:S(2)}) async-start(bf16[16,16,16,128]{3,2,1,0:T(8,128)(2,1)} %shard_map.113), calls=%async_computation.2 | async-start | bytes 2097152 | tf_op jit(solution)/shard_map/all_to_all | solution.py:292
  162.2 26.5 %collective-permute-start.14 = (bf16[8,256,128]{2,1,0:T(8,128)(2,1)S(1)}, bf16[8,256,128]{2,1,0:T(8,128)(2,1)S(1)}, u32[]{:S(2)}, u32[]{:S(2)}) collective-permute-start(bf16[8,256,128]{2,1,0:T(8,128)(2,1)S(1)} %copy-done.20), channel_id=1, source_target_pairs={{0,16},{1,17},{2,18},{3,19},{4,20},{5,21},{6,22},{7,23},{8,24},{9,... | collective-permute-start | bytes 1572872 | tf_op jit(solution)/shard_map/ppermute | solution.py:286
  193.8 5.0 %copy-start.3 = (bf16[16,16,16,128]{3,2,1,0:T(8,128)(2,1)}, bf16[16,16,16,128]{3,2,1,0:T(8,128)(2,1)S(1)}, u32[]{:S(2)}) copy-start(bf16[16,16,16,128]{3,2,1,0:T(8,128)(2,1)S(1)} %all-to-all-done.2) | copy-start | bytes 3145732
  193.8 64.8 %all-to-all-start.5 = ((bf16[16,16,16,128]{3,2,1,0:T(8,128)(2,1)}), bf16[16,16,16,128]{3,2,1,0:T(8,128)(2,1)}, u32[]{:S(2)}, u32[]{:S(2)}) async-start(bf16[16,16,16,128]{3,2,1,0:T(8,128)(2,1)} %shard_map.118), calls=%async_computation.5 | async-start | bytes 2097152 | tf_op jit(solution)/shard_map/all_to_all | solution.py:292
  198.4 1.9 copy-start.14
  200.2 7.1 %copy-start.24 = (bf16[256,256]{1,0:T(8,128)(2,1)S(1)}, bf16[256,256]{1,0:T(8,128)(2,1)}, u32[]{:S(2)}) copy-start(bf16[256,256]{1,0:T(8,128)(2,1)} %param.11) | copy-start | bytes 393220
  200.2 8.0 %copy-start.18 = (bf16[256,256]{1,0:T(8,128)(2,1)S(1)}, bf16[256,256]{1,0:T(8,128)(2,1)}, u32[]{:S(2)}) copy-start(bf16[256,256]{1,0:T(8,128)(2,1)} %param.12) | copy-start | bytes 393220
  203.0 32.0 %collective-permute-start.3 = (bf16[8,256,128]{2,1,0:T(8,128)(2,1)}, bf16[8,256,128]{2,1,0:T(8,128)(2,1)}, u32[]{:S(2)}, u32[]{:S(2)}) collective-permute-start(bf16[8,256,128]{2,1,0:T(8,128)(2,1)} %get-tuple-element.42), channel_id=1, source_target_pairs={{0,8},{1,9},{2,10},{3,11},{4,12},{5,13},{6,14},{7,15},{8,0},{9,1},... | collective-permute-start | bytes 1572872 | tf_op jit(solution)/shard_map/ppermute | solution.py:286
  204.6 31.5 %collective-permute-start.4 = (bf16[8,256,128]{2,1,0:T(8,128)(2,1)}, bf16[8,256,128]{2,1,0:T(8,128)(2,1)}, u32[]{:S(2)}, u32[]{:S(2)}) collective-permute-start(bf16[8,256,128]{2,1,0:T(8,128)(2,1)} %get-tuple-element.41), channel_id=1, source_target_pairs={{0,16},{1,17},{2,18},{3,19},{4,20},{5,21},{6,22},{7,23},{8,24},{9,... | collective-permute-start | bytes 1572872 | tf_op jit(solution)/shard_map/ppermute | solution.py:286
  206.6 41.0 %collective-permute-start.5 = (bf16[8,256,128]{2,1,0:T(8,128)(2,1)}, bf16[8,256,128]{2,1,0:T(8,128)(2,1)S(1)}, u32[]{:S(2)}, u32[]{:S(2)}) collective-permute-start(bf16[8,256,128]{2,1,0:T(8,128)(2,1)} %get-tuple-element.40), channel_id=1, source_target_pairs={{0,24},{1,25},{2,26},{3,27},{4,28},{5,29},{6,30},{7,31},{8,16},{9,... | collective-permute-start | bytes 1572872 | tf_op jit(solution)/shard_map/ppermute | solution.py:286
  247.7 1.3 copy-start.2
  258.6 30.3 %all-to-all-start.1 = ((bf16[8,32,32,128]{3,2,1,0:T(8,128)(2,1)}), bf16[8,32,32,128]{3,2,1,0:T(8,128)(2,1)S(1)}, u32[]{:S(2)}, u32[]{:S(2)}) async-start(bf16[8,32,32,128]{3,2,1,0:T(8,128)(2,1)} %get-tuple-element.19), calls=%async_computation.1 | async-start | bytes 4194304 | tf_op jit(solution)/shard_map/all_to_all | solution.py:292
  288.9 1.3 copy-start.11
  288.9 36.2 %copy-start.5 = (bf16[16,256,128]{2,1,0:T(8,128)(2,1)S(1)}, bf16[16,256,128]{2,1,0:T(8,128)(2,1)}, u32[]{:S(2)}) copy-start(bf16[16,256,128]{2,1,0:T(8,128)(2,1)} %copy-done.4) | copy-start | bytes 3145732
  290.3 40.3 %all-to-all-start.6 = ((bf16[8,32,32,128]{3,2,1,0:T(8,128)(2,1)}), bf16[8,32,32,128]{3,2,1,0:T(8,128)(2,1)}, u32[]{:S(2)}, u32[]{:S(2)}) async-start(bf16[8,32,32,128]{3,2,1,0:T(8,128)(2,1)} %get-tuple-element.31), calls=%async_computation.6 | async-start | bytes 4194304 | tf_op jit(solution)/shard_map/all_to_all | solution.py:292
  294.6 30.5 %collective-permute-start.13 = (bf16[8,256,128]{2,1,0:T(8,128)(2,1)}, bf16[8,256,128]{2,1,0:T(8,128)(2,1)S(1)}, u32[]{:S(2)}, u32[]{:S(2)}) collective-permute-start(bf16[8,256,128]{2,1,0:T(8,128)(2,1)} %get-tuple-element.39), channel_id=1, source_target_pairs={{0,16},{1,17},{2,18},{3,19},{4,20},{5,21},{6,22},{7,23},{8,24},{9,... | collective-permute-start | bytes 1572872 | tf_op jit(solution)/shard_map/ppermute | solution.py:286
  330.6 20.2 %all-to-all-start.3 = ((bf16[16,16,16,128]{3,2,1,0:T(8,128)(2,1)}), bf16[16,16,16,128]{3,2,1,0:T(8,128)(2,1)S(1)}, u32[]{:S(2)}, u32[]{:S(2)}) async-start(bf16[16,16,16,128]{3,2,1,0:T(8,128)(2,1)} %get-tuple-element.21), calls=%async_computation.3 | async-start | bytes 2097152 | tf_op jit(solution)/shard_map/all_to_all | solution.py:292
  340.3 14.1 %copy-start.21 = (f32[256,256]{1,0:T(8,128)S(1)}, f32[256,256]{1,0:T(8,128)}, u32[]{:S(2)}) copy-start(f32[256,256]{1,0:T(8,128)} %get-tuple-element.26) | copy-start | bytes 786436
  350.8 4.1 copy-start.12
  350.8 28.0 %all-to-all-start.7 = ((bf16[16,16,16,128]{3,2,1,0:T(8,128)(2,1)}), bf16[16,16,16,128]{3,2,1,0:T(8,128)(2,1)S(1)}, u32[]{:S(2)}, u32[]{:S(2)}) async-start(bf16[16,16,16,128]{3,2,1,0:T(8,128)(2,1)} %get-tuple-element.32), calls=%async_computation.7 | async-start | bytes 2097152 | tf_op jit(solution)/shard_map/all_to_all | solution.py:292
  355.2 2.8 copy-start.22
  385.3 7.1 %copy-start.15 = (bf16[32,256,128]{2,1,0:T(8,128)(2,1)S(1)}, bf16[32,256,128]{2,1,0:T(8,128)(2,1)}, u32[]{:S(2)}) copy-start(bf16[32,256,128]{2,1,0:T(8,128)(2,1)} %get-tuple-element.20) | copy-start | bytes 6291460
  388.4 13.8 %all-to-all-start.8 = ((bf16[8,32,1024]{2,1,0:T(8,128)(2,1)}), bf16[8,32,1024]{2,1,0:T(8,128)(2,1)S(1)}, u32[]{:S(2)}, u32[]{:S(2)}) async-start(bf16[8,32,1024]{2,1,0:T(8,128)(2,1)} %pad_maximum_fusion), calls=%async_computation.8 | async-start | bytes 1048576 | tf_op jit(solution)/shard_map/all_to_all | solution.py:292
  393.6 45.9 %collective-permute-start.9 = (bf16[8,256,128]{2,1,0:T(8,128)(2,1)}, bf16[8,256,128]{2,1,0:T(8,128)(2,1)}, u32[]{:S(2)}, u32[]{:S(2)}) collective-permute-start(bf16[8,256,128]{2,1,0:T(8,128)(2,1)} %get-tuple-element.53), channel_id=1, source_target_pairs={{0,8},{1,9},{2,10},{3,11},{4,12},{5,13},{6,14},{7,15},{8,0},{9,1},... | collective-permute-start | bytes 1572872 | tf_op jit(solution)/shard_map/ppermute | solution.py:286
  402.2 21.2 %collective-permute-start.16 = (f32[32,1024]{1,0:T(8,128)S(1)}, f32[32,1024]{1,0:T(8,128)S(1)}, u32[]{:S(2)}, u32[]{:S(2)}) collective-permute-start(f32[32,1024]{1,0:T(8,128)S(1)} %convert_reduce_fusion), channel_id=1, source_target_pairs={{0,16},{1,17},{2,18},{3,19},{4,20},{5,21},{6,22},{7,23},{8,24},{9,... | collective-permute-start | bytes 393224 | tf_op jit(solution)/shard_map/ppermute | solution.py:286
  404.2 53.3 %collective-permute-start.10 = (bf16[8,256,128]{2,1,0:T(8,128)(2,1)}, bf16[8,256,128]{2,1,0:T(8,128)(2,1)}, u32[]{:S(2)}, u32[]{:S(2)}) collective-permute-start(bf16[8,256,128]{2,1,0:T(8,128)(2,1)} %get-tuple-element.52), channel_id=1, source_target_pairs={{0,16},{1,17},{2,18},{3,19},{4,20},{5,21},{6,22},{7,23},{8,24},{9,... | collective-permute-start | bytes 1572872 | tf_op jit(solution)/shard_map/ppermute | solution.py:286
  423.4 5.9 %copy-start.16 = (bf16[16,256,128]{2,1,0:T(8,128)(2,1)S(1)}, bf16[16,256,128]{2,1,0:T(8,128)(2,1)}, u32[]{:S(2)}) copy-start(bf16[16,256,128]{2,1,0:T(8,128)(2,1)} %get-tuple-element.22) | copy-start | bytes 3145732
  423.4 11.3 %collective-permute-start.17 = (f32[32,1024]{1,0:T(8,128)S(1)}, f32[32,1024]{1,0:T(8,128)S(1)}, u32[]{:S(2)}, u32[]{:S(2)}) collective-permute-start(f32[32,1024]{1,0:T(8,128)S(1)} %add.130), channel_id=1, source_target_pairs={{0,8},{1,9},{2,10},{3,11},{4,12},{5,13},{6,14},{7,15},{8,0},{9,1},... | collective-permute-start | bytes 393224 | tf_op jit(solution)/shard_map/ppermute | solution.py:286
  426.4 33.0 %collective-permute-start.11 = (bf16[8,256,128]{2,1,0:T(8,128)(2,1)}, bf16[8,256,128]{2,1,0:T(8,128)(2,1)}, u32[]{:S(2)}, u32[]{:S(2)}) collective-permute-start(bf16[8,256,128]{2,1,0:T(8,128)(2,1)} %get-tuple-element.51), channel_id=1, source_target_pairs={{0,24},{1,25},{2,26},{3,27},{4,28},{5,29},{6,30},{7,31},{8,16},{9,... | collective-permute-start | bytes 1572872 | tf_op jit(solution)/shard_map/ppermute | solution.py:286
  429.4 47.4 %collective-permute-start.15 = (bf16[8,256,128]{2,1,0:T(8,128)(2,1)S(1)}, bf16[8,256,128]{2,1,0:T(8,128)(2,1)S(1)}, u32[]{:S(2)}, u32[]{:S(2)}) collective-permute-start(bf16[8,256,128]{2,1,0:T(8,128)(2,1)S(1)} %constant_dynamic-slice_fusion.7), channel_id=1, source_target_pairs={{0,16},{1,17},{2,18},{3,19},{4,20},{5,21},{6,22},{7,23},{8,24},{9,... | collective-permute-start | bytes 1572872 | tf_op jit(solution)/shard_map/ppermute | solution.py:286
  435.9 41.7 %all-to-all-start.9 = ((f32[8,32,1024]{2,1,0:T(8,128)}), f32[8,32,1024]{2,1,0:T(8,128)S(1)}, u32[]{:S(2)}, u32[]{:S(2)}) async-start(f32[8,32,1024]{2,1,0:T(8,128)} %broadcast_in_dim.29), calls=%async_computation.9 | async-start | bytes 2097152 | tf_op jit(solution)/shard_map/all_to_all | solution.py:292
  (5 other events, 4.9 us)

commit v3 on v1

--- a/solution.py
+++ b/solution.py
@@ -10,7 +10,7 @@
 F32 = jnp.float32
 BF16 = jnp.bfloat16
 LANES = 128
-VMEM = 56 * 2**20
+VMEM = 63 * 2**20
 
 
 def dot(x, y, dims):
@@ -39,7 +39,7 @@
 def apply_inner(x, factor, side, members):
     rows, order, channels = x.shape
     part = order // members
-    step = max(1, rows // 4)
+    step = max(1, rows // 2)
 
     def body(x_ref, f_ref, o_ref):
         for r in range(step):
@@ -178,7 +178,7 @@
 def finish_values(grad_first, values, inner):
     members, rows, part, channels = grad_first.shape
     order = members * part
-    step = max(1, rows // 4)
+    step = max(1, rows // 2)
 
     def body(g_ref, v_ref, f_ref, gv_ref, gi_ref):
         @pl.when(pl.program_id(0) == 0)
@@ -208,7 +208,7 @@
 def finish_return(returned, cotangent):
     members, rows, part, channels = returned.shape
     order = members * part
-    step = max(1, rows // 4)
+    step = max(1, rows // 2)
 
     def body(r_ref, c_ref, o_ref):
         @pl.when(pl.program_id(0) == 0)
@@ -281,24 +281,47 @@
     )
 
 
-def swap(x, bit):
+def swap(x, bits):
     size = lax.axis_size("seq")
-    return lax.ppermute(x, "seq", [(i, i ^ bit) for i in range(size)])
-
-
-def total(x):
+    return lax.ppermute(x, "seq", [(i, i ^ bits) for i in range(size)])
+
+
+def move(x):
+    return lax.all_to_all(x, "seq", 0, 0, tiled=True)
+
+
+def halves(x, bit):
+    mine = (lax.axis_index("seq") // bit) % 2
+    pair = x.reshape(2, x.shape[0] // 2, x.shape[1])
+    return (
+        lax.dynamic_index_in_dim(pair, mine, 0, keepdims=False),
+        lax.dynamic_index_in_dim(pair, 1 - mine, 0, keepdims=False),
+    )
+
+
+def join(mine, other, bit):
+    first = (lax.axis_index("seq") // bit) % 2 == 0
+    return jnp.concatenate((jnp.where(first, mine, other), jnp.where(first, other, mine)), axis=0)
+
+
+def early_sum(x):
+    for bit in (1, 2, 4):
+        keep, give = halves(x, bit)
+        x = keep + swap(give, bit)
+    for bit in (16, 8):
+        x = x.astype(BF16)
+        x = x.astype(F32) + swap(x, bit).astype(F32)
+    for bit in (4, 2, 1):
+        x = join(x, swap(x, bit), bit)
+    return x
+
+
+def late_sum(x):
     size = lax.axis_size("seq")
-    plane = [[z * 8 + p for p in range(8)] for z in range(size // 8)]
     rows, columns = x.shape
-    parts = lax.all_to_all(
-        x.astype(BF16).reshape(8, rows // 8, columns), "seq", 0, 0, axis_index_groups=plane, tiled=True
-    )
-    held = jnp.sum(parts.astype(F32), axis=0).astype(BF16)
-    sent = sum(swap(held, 8 * d).astype(F32) for d in (2,)) + held.astype(F32)
-    sent = sent.astype(BF16)
-    part = sent.astype(F32) + swap(sent, 8).astype(F32)
-    out = jnp.broadcast_to(part.astype(BF16)[None], (8, rows // 8, columns))
-    return lax.all_to_all(out, "seq", 0, 0, axis_index_groups=plane, tiled=True).reshape(rows, columns)
+    parts = move(x.astype(BF16).reshape(size, rows // size, columns))
+    held = jnp.sum(parts.astype(F32), axis=0)
+    return move(jnp.broadcast_to(held[None], parts.shape)).reshape(rows, columns)
 
 
 def per_device(values, kernel, cotangent, inner_factor, outer_factor, return_outer, return_inner):
@@ -318,9 +341,6 @@
         )
     scale = 1.0 / math.sqrt(order * channels)
 
-    def move(x):
-        return lax.all_to_all(x, "seq", 0, 0, tiled=True)
-
     grad_ret = move(apply_inner(cotangent[0], return_inner, 0, members))
     sent = apply_inner(values[0], inner_factor, 1, members)
     sent, grad_ret = lax.optimization_barrier((sent, grad_ret))
@@ -336,10 +356,10 @@
     sent, grad_first = lax.optimization_barrier((sent, grad_first))
     returned = move(sent)
     grad_values, grad_inner = finish_values(grad_first, values[0], inner_factor)
-    grad_last = finish_return(returned, cotangent[0])
-    grads = total(jnp.concatenate((grad_inner, grad_outer, grad_back, grad_last), axis=1))
-    grads = jnp.split(grads.astype(F32) * scale, 4, axis=1)
-    return (grad_values[None], *grads)
+    early = early_sum(jnp.concatenate((grad_inner, grad_outer, grad_back), axis=1)) * scale
+    returned, early = lax.optimization_barrier((returned, early))
+    grad_last = late_sum(finish_return(returned, cotangent[0])) * scale
+    return (grad_values[None], *jnp.split(early, 3, axis=1), grad_last)
 
 
 def solution(mesh):

time: 357 us -> 361 us (1.011)
  blocking collectives: 25.1 us -> 11.9 us
  waiting for transfers between devices: 264 us -> 276 us
  starting transfers between devices: 19.5 us -> 31.3 us
  Pallas kernels: 39.3 us -> 35.3 us
    ppermute x2 -> x8, waiting for transfers between devices: 9.4 us -> 74.1 us  [swap(): return lax.ppermute(x, 'seq', [(i, i ^ bits) for i in range(size)])]
    all_to_all x4 -> x5, waiting for transfers between devices: 254 us -> 202 us  [move(): return lax.all_to_all(x, 'seq', 0, 0, tiled=True)]
    all_to_all x2 -> x1, blocking collectives: 25.1 us -> 11.9 us  [move(): return lax.all_to_all(x, 'seq', 0, 0, tiled=True)]
    ppermute x2 -> x8, starting transfers between devices: 0.14 us -> 9.2 us  [swap(): return lax.ppermute(x, 'seq', [(i, i ^ bits) for i in range(size)])]
    all_to_all x4 -> x5, starting transfers between devices: 19.3 us -> 22.1 us  [move(): return lax.all_to_all(x, 'seq', 0, 0, tiled=True)]
  transfers between devices with their start and end apart: 6 -> 13, of which waited for: 6 -> 12; matrix products, arithmetic and copies ran while one was open for 1% -> 1% of each run, Pallas kernels for 8% -> 8%
where the time goes in v3:
time: 361 us; the launch traced here: 360 us
  waiting for transfers between devices  276 us (76%)
  Pallas kernels  35.3 us (10%)
  starting transfers between devices  31.3 us (9%)
  blocking collectives  11.9 us (3%)
    all_to_all x5, waiting for transfers between devices, move(): return lax.all_to_all(x, 'seq', 0, 0, tiled=True)  202 us
    ppermute x8, waiting for transfers between devices, swap(): return lax.ppermute(x, 'seq', [(i, i ^ bits) for i in range(size)])  74.1 us
    all_to_all x5, starting transfers between devices, move(): return lax.all_to_all(x, 'seq', 0, 0, tiled=True)  22.1 us
    all_to_all x1, blocking collectives, move(): return lax.all_to_all(x, 'seq', 0, 0, tiled=True)  11.9 us
    pallas_call x1, Pallas kernels, forward_mixed(): call(body, (channels // width,), [moved, moved, mine, mine, square(order)...  10.5 us
    ppermute x8, starting transfers between devices, swap(): return lax.ppermute(x, 'seq', [(i, i ^ bits) for i in range(size)])  9.2 us
    pallas_call x1, Pallas kernels, backward_mixed(): call(body, (channels // width,), [pl.BlockSpec((order, part, width), lamb...  7.8 us
    pallas_call x2, Pallas kernels, apply_inner(): call(body, (rows // step,), [pl.BlockSpec((step, order, channels), lambda...  7.54 us
  transfers between devices with their start and end apart: 13, of which 12 were waited for; matrix products, arithmetic and copies ran while one was open for 1% of the time, Pallas kernels for 8%

profile of v3, /device:TPU:0, one launch (start us, length us, event | category | flops | bytes accessed | tf_op | source)
XLA Modules:
  0.0 360.2 jit_solution(2957056202339981014)
XLA Ops:
  0.6 3.8 %shard_map.111 = bf16[32,8,8,768]{3,2,1,0:T(8,128)(2,1)} custom-call(bf16[8,256,768]{2,1,0:T(8,128)(2,1)} %bitcast.28, bf16[256,256]{1,0:T(8,128)(2,1)} %f_ref.4), custom_call_target="tpu_custom_call" | custom-call | flops 805306368 | bytes 6291456 | tf_op jit(solution)/shard_map/pallas_call | solution.py:49
  4.4 7.4 %all-to-all-start = ((bf16[32,8,8,768]{3,2,1,0:T(8,128)(2,1)}), bf16[32,8,8,768]{3,2,1,0:T(8,128)(2,1)}, u32[]{:S(2)}, u32[]{:S(2)}) async-start(bf16[32,8,8,768]{3,2,1,0:T(8,128)(2,1)} %shard_map.111), calls=%async_computation | async-start | bytes 6291456 | tf_op jit(solution)/shard_map/all_to_all | solution.py:290
  11.8 3.8 %shard_map.110 = bf16[32,8,8,768]{3,2,1,0:T(8,128)(2,1)} custom-call(bf16[8,256,768]{2,1,0:T(8,128)(2,1)} %bitcast.26, bf16[256,256]{1,0:T(8,128)(2,1)} %f_ref.5), custom_call_target="tpu_custom_call" | custom-call | flops 805306368 | bytes 6291456 | tf_op jit(solution)/shard_map/pallas_call | solution.py:49
  15.6 67.7 %all-to-all-done = bf16[32,8,8,768]{3,2,1,0:T(8,128)(2,1)} async-done(((bf16[32,8,8,768]{3,2,1,0:T(8,128)(2,1)}), bf16[32,8,8,768]{3,2,1,0:T(8,128)(2,1)}, u32[]{:S(2)}, u32[]{:S(2)}) %all-to-all-start) | async-done | bytes 3145760 | tf_op jit(solution)/shard_map/all_to_all | solution.py:290
  83.3 4.0 %all-to-all-start.1 = ((bf16[32,8,8,768]{3,2,1,0:T(8,128)(2,1)}), bf16[32,8,8,768]{3,2,1,0:T(8,128)(2,1)}, u32[]{:S(2)}, u32[]{:S(2)}) async-start(bf16[32,8,8,768]{3,2,1,0:T(8,128)(2,1)} %shard_map.110), calls=%async_computation.1 | async-start | bytes 6291456 | tf_op jit(solution)/shard_map/all_to_all | solution.py:290
  87.3 7.8 %shard_map.112 = (bf16[8,256,768]{2,1,0:T(8,128)(2,1)}, bf16[32,8,8,768]{3,2,1,0:T(8,128)(2,1)}) custom-call(bf16[256,8,768]{2,1,0:T(8,128)(2,1)} %bitcast.2.m_ref.g_ref, bf16[8,256,768]{2,1,0:T(8,128)(2,1)} %k_ref.3, bf16[256,256]{1,0:T(8,128)(2,1)} %o_ref.3, bf16[256,256]{1,0:T(8,128)(2,1)} %b_ref.3), custom_call_target="tpu_custom_call" | custom-call | flops 1610612736 | bytes 12582912 | tf_op jit(solution)/shard_map/pallas_call | solution.py:110
  95.1 63.7 %all-to-all-done.1 = bf16[32,8,8,768]{3,2,1,0:T(8,128)(2,1)} async-done(((bf16[32,8,8,768]{3,2,1,0:T(8,128)(2,1)}), bf16[32,8,8,768]{3,2,1,0:T(8,128)(2,1)}, u32[]{:S(2)}, u32[]{:S(2)}) %all-to-all-start.1) | async-done | bytes 3145760 | tf_op jit(solution)/shard_map/all_to_all | solution.py:290
  158.8 4.0 %all-to-all-start.2 = ((bf16[32,8,8,768]{3,2,1,0:T(8,128)(2,1)}), bf16[32,8,8,768]{3,2,1,0:T(8,128)(2,1)}, u32[]{:S(2)}, u32[]{:S(2)}) async-start(bf16[32,8,8,768]{3,2,1,0:T(8,128)(2,1)} %get-tuple-element.26), calls=%async_computation.2 | async-start | bytes 6291456 | tf_op jit(solution)/shard_map/all_to_all | solution.py:290
  162.8 10.5 %shard_map.113 = (bf16[32,8,8,768]{3,2,1,0:T(8,128)(2,1)}, f32[256,256]{1,0:T(8,128)}, f32[256,256]{1,0:T(8,128)}) custom-call(bf16[256,8,768]{2,1,0:T(8,128)(2,1)} %bitcast.3.f_ref, bf16[256,8,768]{2,1,0:T(8,128)(2,1)} %bitcast.2.m_ref.g_ref, bf16[8,256,768]{2,1,0:T(8,128)(2,1)} %k_ref.3, bf16[8,256,768]{2,1,0:T(8,128)(2,1)} %get-tuple-element.24.gw_ref, ...), custom_call_target="tpu_custom_call" | custom-call | flops 3221225472 | bytes 15728640 | tf_op jit(solution)/shard_map/pallas_call | solution.py:160
  173.3 60.9 %all-to-all-done.2.g_ref = bf16[32,8,8,768]{3,2,1,0:T(8,128)(2,1)} async-done(((bf16[32,8,8,768]{3,2,1,0:T(8,128)(2,1)}), bf16[32,8,8,768]{3,2,1,0:T(8,128)(2,1)}, u32[]{:S(2)}, u32[]{:S(2)}) %all-to-all-start.2) | async-done | bytes 3145760 | tf_op jit(solution)/shard_map/all_to_all | solution.py:290
  234.3 4.0 %all-to-all-start.3 = ((bf16[32,8,8,768]{3,2,1,0:T(8,128)(2,1)}), bf16[32,8,8,768]{3,2,1,0:T(8,128)(2,1)}, u32[]{:S(2)}, u32[]{:S(2)}) async-start(bf16[32,8,8,768]{3,2,1,0:T(8,128)(2,1)} %get-tuple-element.29), calls=%async_computation.3 | async-start | bytes 6291456 | tf_op jit(solution)/shard_map/all_to_all | solution.py:290
  238.4 0.0 copy-start
  238.4 0.0 copy-start.1
  238.4 5.3 %shard_map.114 = (bf16[8,256,768]{2,1,0:T(8,128)(2,1)}, f32[256,256]{1,0:T(8,128)}) custom-call(bf16[32,8,8,768]{3,2,1,0:T(8,128)(2,1)} %all-to-all-done.2.g_ref, bf16[8,256,768]{2,1,0:T(8,128)(2,1)} %bitcast.27, bf16[256,256]{1,0:T(8,128)(2,1)} %f_ref.5), custom_call_target="tpu_custom_call" | custom-call | flops 1610612736 | bytes 9437184 | tf_op jit(solution)/shard_map/pallas_call | solution.py:194
  243.7 0.0 copy-done
  243.7 0.0 copy-done.1
  243.7 1.0 pad_maximum_fusion
  244.7 0.3 collective-permute-start
  245.0 1.5 collective-permute-done
  246.6 1.8 collective-permute-start.1
  248.4 16.9 %collective-permute-done.1 = f32[64,768]{1,0:T(8,128)S(1)} collective-permute-done((f32[64,768]{1,0:T(8,128)S(1)}, f32[64,768]{1,0:T(8,128)S(1)}, u32[]{:S(2)}, u32[]{:S(2)}) %collective-permute-start.1) | collective-permute-done | bytes 196640 | tf_op jit(solution)/shard_map/ppermute | solution.py:286
  265.3 1.1 collective-permute-start.2
  266.4 5.4 %collective-permute-done.2 = f32[32,768]{1,0:T(8,128)S(1)} collective-permute-done((f32[32,768]{1,0:T(8,128)S(1)}, f32[32,768]{1,0:T(8,128)S(1)}, u32[]{:S(2)}, u32[]{:S(2)}) %collective-permute-start.2) | collective-permute-done | bytes 98336 | tf_op jit(solution)/shard_map/ppermute | solution.py:286
  271.8 3.5 collective-permute-start.3
  275.3 36.6 %collective-permute-done.3 = bf16[32,768]{1,0:T(8,128)(2,1)S(1)} collective-permute-done((bf16[32,768]{1,0:T(8,128)(2,1)S(1)}, bf16[32,768]{1,0:T(8,128)(2,1)S(1)}, u32[]{:S(2)}, u32[]{:S(2)}) %collective-permute-start.3) | collective-permute-done | bytes 49184 | tf_op jit(solution)/shard_map/ppermute | solution.py:286
  311.9 0.1 collective-permute-start.4
  312.0 4.1 %collective-permute-done.4 = bf16[32,768]{1,0:T(8,128)(2,1)S(1)} collective-permute-done((bf16[32,768]{1,0:T(8,128)(2,1)S(1)}, bf16[32,768]{1,0:T(8,128)(2,1)S(1)}, u32[]{:S(2)}, u32[]{:S(2)}) %collective-permute-start.4) | collective-permute-done | bytes 49184 | tf_op jit(solution)/shard_map/ppermute | solution.py:286
  316.1 1.2 collective-permute-start.5
  317.3 3.5 collective-permute-done.5
  320.8 1.2 collective-permute-start.6
  322.0 4.5 %collective-permute-done.6 = f32[64,768]{1,0:T(8,128)S(1)} collective-permute-done((f32[64,768]{1,0:T(8,128)S(1)}, f32[64,768]{1,0:T(8,128)S(1)}, u32[]{:S(2)}, u32[]{:S(2)}) %collective-permute-start.6) | collective-permute-done | bytes 196640 | tf_op jit(solution)/shard_map/ppermute | solution.py:286
  326.6 0.1 collective-permute-start.7
  326.7 1.7 collective-permute-done.7
  328.4 0.1 broadcast_select_fusion.1
  328.4 0.1 maximum_multiply_fusion
  328.5 0.0 all-to-all-done.3.r_ref
  328.5 4.2 %shard_map.115 = f32[256,256]{1,0:T(8,128)} custom-call(bf16[32,8,8,768]{3,2,1,0:T(8,128)(2,1)} %all-to-all-done.3.r_ref, bf16[8,256,768]{2,1,0:T(8,128)(2,1)} %bitcast.29), custom_call_target="tpu_custom_call" | custom-call | flops 805306368 | bytes 6291456 | tf_op jit(solution)/shard_map/pallas_call | solution.py:222
  332.7 1.0 convert_bitcast_fusion
  333.7 11.9 %all_to_all.30 = bf16[32,8,256]{2,1,0:T(8,128)(2,1)S(1)} all-to-all(bf16[32,8,256]{2,1,0:T(8,128)(2,1)S(1)} %convert_bitcast_fusion), channel_id=1, replica_groups=mesh['groups'=1,'seq'=32,'dp'=1] {'seq'}, dimensions={0} | all-to-all | bytes 262144 | tf_op jit(solution)/shard_map/all_to_all | solution.py:290
  345.6 0.7 broadcast_in_dim.10
  346.3 2.6 all-to-all-start.5
  348.9 0.9 fusion.1
  349.8 9.7 %all-to-all-done.5 = f32[32,8,256]{2,1,0:T(8,128)S(1)} async-done(((f32[32,8,256]{2,1,0:T(8,128)}), f32[32,8,256]{2,1,0:T(8,128)S(1)}, u32[]{:S(2)}, u32[]{:S(2)}) %all-to-all-start.5) | async-done | bytes 262176 | tf_op jit(solution)/shard_map/all_to_all | solution.py:290
  359.5 0.7 multiply_bitcast_fusion
  (13 shorter events, 0.3 us)
Async XLA Ops:
  4.4 78.9 %all-to-all-start = ((bf16[32,8,8,768]{3,2,1,0:T(8,128)(2,1)}), bf16[32,8,8,768]{3,2,1,0:T(8,128)(2,1)}, u32[]{:S(2)}, u32[]{:S(2)}) async-start(bf16[32,8,8,768]{3,2,1,0:T(8,128)(2,1)} %shard_map.111), calls=%async_computation | async-start | bytes 6291456 | tf_op jit(solution)/shard_map/all_to_all | solution.py:290
  83.3 75.5 %all-to-all-start.1 = ((bf16[32,8,8,768]{3,2,1,0:T(8,128)(2,1)}), bf16[32,8,8,768]{3,2,1,0:T(8,128)(2,1)}, u32[]{:S(2)}, u32[]{:S(2)}) async-start(bf16[32,8,8,768]{3,2,1,0:T(8,128)(2,1)} %shard_map.110), calls=%async_computation.1 | async-start | bytes 6291456 | tf_op jit(solution)/shard_map/all_to_all | solution.py:290
  158.8 75.5 %all-to-all-start.2 = ((bf16[32,8,8,768]{3,2,1,0:T(8,128)(2,1)}), bf16[32,8,8,768]{3,2,1,0:T(8,128)(2,1)}, u32[]{:S(2)}, u32[]{:S(2)}) async-start(bf16[32,8,8,768]{3,2,1,0:T(8,128)(2,1)} %get-tuple-element.26), calls=%async_computation.2 | async-start | bytes 6291456 | tf_op jit(solution)/shard_map/all_to_all | solution.py:290
  234.3 94.2 %all-to-all-start.3 = ((bf16[32,8,8,768]{3,2,1,0:T(8,128)(2,1)}), bf16[32,8,8,768]{3,2,1,0:T(8,128)(2,1)}, u32[]{:S(2)}, u32[]{:S(2)}) async-start(bf16[32,8,8,768]{3,2,1,0:T(8,128)(2,1)} %get-tuple-element.29), calls=%async_computation.3 | async-start | bytes 6291456 | tf_op jit(solution)/shard_map/all_to_all | solution.py:290
  238.4 5.3 %copy-start = (f32[256,256]{1,0:T(8,128)S(1)}, f32[256,256]{1,0:T(8,128)}, u32[]{:S(2)}) copy-start(f32[256,256]{1,0:T(8,128)} %get-tuple-element.31) | copy-start | bytes 786436
  238.4 5.3 %copy-start.1 = (f32[256,256]{1,0:T(8,128)S(1)}, f32[256,256]{1,0:T(8,128)}, u32[]{:S(2)}) copy-start(f32[256,256]{1,0:T(8,128)} %get-tuple-element.32) | copy-start | bytes 786436
  244.7 1.8 collective-permute-start
  246.6 18.6 %collective-permute-start.1 = (f32[64,768]{1,0:T(8,128)S(1)}, f32[64,768]{1,0:T(8,128)S(1)}, u32[]{:S(2)}, u32[]{:S(2)}) collective-permute-start(f32[64,768]{1,0:T(8,128)S(1)} %dynamic-slice_bitcast_fusion.1), channel_id=1, source_target_pairs={{0,2},{1,3},{2,0},{3,1},{4,6},{5,7},{6,4},{7,5},{8,10},{9,11},{10,... | collective-permute-start | bytes 589832 | tf_op jit(solution)/shard_map/ppermute | solution.py:286
  265.3 6.5 %collective-permute-start.2 = (f32[32,768]{1,0:T(8,128)S(1)}, f32[32,768]{1,0:T(8,128)S(1)}, u32[]{:S(2)}, u32[]{:S(2)}) collective-permute-start(f32[32,768]{1,0:T(8,128)S(1)} %dynamic-slice_bitcast_fusion.2), channel_id=1, source_target_pairs={{0,4},{1,5},{2,6},{3,7},{4,0},{5,1},{6,2},{7,3},{8,12},{9,13},{10,... | collective-permute-start | bytes 294920 | tf_op jit(solution)/shard_map/ppermute | solution.py:286
  271.8 40.1 %collective-permute-start.3 = (bf16[32,768]{1,0:T(8,128)(2,1)S(1)}, bf16[32,768]{1,0:T(8,128)(2,1)S(1)}, u32[]{:S(2)}, u32[]{:S(2)}) collective-permute-start(bf16[32,768]{1,0:T(8,128)(2,1)S(1)} %fusion), channel_id=1, source_target_pairs={{0,16},{1,17},{2,18},{3,19},{4,20},{5,21},{6,22},{7,23},{8,24},{9,... | collective-permute-start | bytes 147464 | tf_op jit(solution)/shard_map/ppermute | solution.py:286
  311.9 4.2 %collective-permute-start.4 = (bf16[32,768]{1,0:T(8,128)(2,1)S(1)}, bf16[32,768]{1,0:T(8,128)(2,1)S(1)}, u32[]{:S(2)}, u32[]{:S(2)}) collective-permute-start(bf16[32,768]{1,0:T(8,128)(2,1)S(1)} %add_convert_fusion), channel_id=1, source_target_pairs={{0,8},{1,9},{2,10},{3,11},{4,12},{5,13},{6,14},{7,15},{8,0},{9,1},... | collective-permute-start | bytes 147464 | tf_op jit(solution)/shard_map/ppermute | solution.py:286
  316.1 4.7 %collective-permute-start.5 = (f32[32,768]{1,0:T(8,128)S(1)}, f32[32,768]{1,0:T(8,128)S(1)}, u32[]{:S(2)}, u32[]{:S(2)}) collective-permute-start(f32[32,768]{1,0:T(8,128)S(1)} %convert_add_fusion), channel_id=1, source_target_pairs={{0,4},{1,5},{2,6},{3,7},{4,0},{5,1},{6,2},{7,3},{8,12},{9,13},{10,... | collective-permute-start | bytes 294920 | tf_op jit(solution)/shard_map/ppermute | solution.py:286
  320.8 5.7 %collective-permute-start.6 = (f32[64,768]{1,0:T(8,128)S(1)}, f32[64,768]{1,0:T(8,128)S(1)}, u32[]{:S(2)}, u32[]{:S(2)}) collective-permute-start(f32[64,768]{1,0:T(8,128)S(1)} %pad_maximum_fusion.2), channel_id=1, source_target_pairs={{0,2},{1,3},{2,0},{3,1},{4,6},{5,7},{6,4},{7,5},{8,10},{9,11},{10,... | collective-permute-start | bytes 589832 | tf_op jit(solution)/shard_map/ppermute | solution.py:286
  326.6 1.8 collective-permute-start.7
  346.3 13.2 %all-to-all-start.5 = ((f32[32,8,256]{2,1,0:T(8,128)}), f32[32,8,256]{2,1,0:T(8,128)S(1)}, u32[]{:S(2)}, u32[]{:S(2)}) async-start(f32[32,8,256]{2,1,0:T(8,128)} %broadcast_in_dim.10), calls=%async_computation.5 | async-start | bytes 524288 | tf_op jit(solution)/shard_map/all_to_all | solution.py:290

commit v4 on v3

--- a/solution.py
+++ b/solution.py
@@ -209,25 +209,30 @@
     members, rows, part, channels = returned.shape
     order = members * part
     step = max(1, rows // 2)
-
-    def body(r_ref, c_ref, o_ref):
+    steps = rows // step
+
+    def body(r_ref, c_ref, o_ref, acc):
         @pl.when(pl.program_id(0) == 0)
         def _():
-            o_ref[...] = jnp.zeros_like(o_ref)
+            acc[...] = jnp.zeros_like(acc)
 
         for r in range(step):
             ret = r_ref[:, r].astype(F32).reshape(order, channels).astype(BF16)
-            o_ref[...] += dot(c_ref[r], ret, (1, 1))
+            acc[...] += dot(c_ref[r], ret, (1, 1))
+
+        @pl.when(pl.program_id(0) == steps - 1)
+        def _():
+            o_ref[...] = acc[...].astype(BF16)
 
     return call(
         body,
-        (rows // step,),
+        (steps,),
         [
             pl.BlockSpec((members, step, part, channels), lambda g: (0, g, 0, 0)),
             pl.BlockSpec((step, order, channels), lambda g: (g, 0, 0)),
         ],
-        [(square(order), jax.ShapeDtypeStruct((order, order), F32))],
-        [],
+        [(square(order), jax.ShapeDtypeStruct((order, order), BF16))],
+        [pltpu.VMEM((order, order), F32)],
         2 * order * cotangent.size,
         4 * cotangent.size,
     )(returned, cotangent)[0]
@@ -304,13 +309,20 @@
     return jnp.concatenate((jnp.where(first, mine, other), jnp.where(first, other, mine)), axis=0)
 
 
-def early_sum(x):
+def plane_sum(x):
     for bit in (1, 2, 4):
         keep, give = halves(x, bit)
         x = keep + swap(give, bit)
-    for bit in (16, 8):
-        x = x.astype(BF16)
-        x = x.astype(F32) + swap(x, bit).astype(F32)
+    return x
+
+
+def across(x):
+    x = x.astype(BF16)
+    near, *far = [swap(x, bits) for bits in (8, 16, 24)]
+    return x, near, *far
+
+
+def joined(x):
     for bit in (4, 2, 1):
         x = join(x, swap(x, bit), bit)
     return x
@@ -319,9 +331,9 @@
 def late_sum(x):
     size = lax.axis_size("seq")
     rows, columns = x.shape
-    parts = move(x.astype(BF16).reshape(size, rows // size, columns))
-    held = jnp.sum(parts.astype(F32), axis=0)
-    return move(jnp.broadcast_to(held[None], parts.shape)).reshape(rows, columns)
+    parts = move(x.reshape(size, rows // size, columns))
+    held = jnp.sum(parts.astype(F32), axis=0).astype(BF16)
+    return move(jnp.broadcast_to(held[None], parts.shape)).reshape(rows, columns).astype(F32)
 
 
 def per_device(values, kernel, cotangent, inner_factor, outer_factor, return_outer, return_inner):
@@ -356,9 +368,14 @@
     sent, grad_first = lax.optimization_barrier((sent, grad_first))
     returned = move(sent)
     grad_values, grad_inner = finish_values(grad_first, values[0], inner_factor)
-    early = early_sum(jnp.concatenate((grad_inner, grad_outer, grad_back), axis=1)) * scale
+    early = plane_sum(jnp.concatenate((grad_inner, grad_outer, grad_back), axis=1))
     returned, early = lax.optimization_barrier((returned, early))
-    grad_last = late_sum(finish_return(returned, cotangent[0])) * scale
+    quarters = across(early)
+    grad_last = finish_return(returned, cotangent[0])
+    (a, b, c, d), grad_last = lax.optimization_barrier((quarters, grad_last))
+    early = (a.astype(F32) + b.astype(F32)) + (c.astype(F32) + d.astype(F32))
+    early = joined(early) * scale
+    grad_last = late_sum(grad_last) * scale
     return (grad_values[None], *jnp.split(early, 3, axis=1), grad_last)
 
 

time: 361 us -> 345 us (0.956)
  blocking collectives: 11.9 us -> 0 us
  waiting for transfers between devices: 276 us -> 269 us
  starting transfers between devices: 31.3 us -> 36 us
    ppermute x8 -> x9, waiting for transfers between devices: 74.1 us -> 24 us  [swap(): return lax.ppermute(x, 'seq', [(i, i ^ bits) for i in range(size)])]
    all_to_all x5 -> x6, waiting for transfers between devices: 202 us -> 245 us  [move(): return lax.all_to_all(x, 'seq', 0, 0, tiled=True)]
    all_to_all x1 -> x0, blocking collectives: 11.9 us -> none  [move(): return lax.all_to_all(x, 'seq', 0, 0, tiled=True)]
    all_to_all x5 -> x6, starting transfers between devices: 22.1 us -> 25.4 us  [move(): return lax.all_to_all(x, 'seq', 0, 0, tiled=True)]
    ppermute x8 -> x9, starting transfers between devices: 9.2 us -> 10.6 us  [swap(): return lax.ppermute(x, 'seq', [(i, i ^ bits) for i in range(size)])]
  transfers between devices with their start and end apart: 13 -> 15, of which waited for: 12 -> 10; matrix products, arithmetic and copies ran while one was open for 1% -> 1% of each run, Pallas kernels for 8% -> 9%
where the time goes in v4:
time: 345 us; the launch traced here: 344 us
  waiting for transfers between devices  269 us (78%)
  starting transfers between devices  36 us (10%)
  Pallas kernels  35.3 us (10%)
    all_to_all x6, waiting for transfers between devices, move(): return lax.all_to_all(x, 'seq', 0, 0, tiled=True)  245 us
    all_to_all x6, starting transfers between devices, move(): return lax.all_to_all(x, 'seq', 0, 0, tiled=True)  25.4 us
    ppermute x9, waiting for transfers between devices, swap(): return lax.ppermute(x, 'seq', [(i, i ^ bits) for i in range(size)])  24 us
    ppermute x9, starting transfers between devices, swap(): return lax.ppermute(x, 'seq', [(i, i ^ bits) for i in range(size)])  10.6 us
    pallas_call x1, Pallas kernels, forward_mixed(): call(body, (channels // width,), [moved, moved, mine, mine, square(order)...  10.5 us
    pallas_call x1, Pallas kernels, backward_mixed(): call(body, (channels // width,), [pl.BlockSpec((order, part, width), lamb...  7.8 us
    pallas_call x2, Pallas kernels, apply_inner(): call(body, (rows // step,), [pl.BlockSpec((step, order, channels), lambda...  7.62 us
  transfers between devices with their start and end apart: 15, of which 10 were waited for; matrix products, arithmetic and copies ran while one was open for 1% of the time, Pallas kernels for 9%

profile of v4, /device:TPU:0, one launch (start us, length us, event | category | flops | bytes accessed | tf_op | source)
XLA Modules:
  0.0 344.4 jit_solution(1136370161116414091)
XLA Ops:
  0.6 3.8 %shard_map.111 = bf16[32,8,8,768]{3,2,1,0:T(8,128)(2,1)} custom-call(bf16[8,256,768]{2,1,0:T(8,128)(2,1)} %bitcast.25, bf16[256,256]{1,0:T(8,128)(2,1)} %f_ref.4), custom_call_target="tpu_custom_call" | custom-call | flops 805306368 | bytes 6291456 | tf_op jit(solution)/shard_map/pallas_call | solution.py:49
  4.4 7.4 %all-to-all-start = ((bf16[32,8,8,768]{3,2,1,0:T(8,128)(2,1)}), bf16[32,8,8,768]{3,2,1,0:T(8,128)(2,1)}, u32[]{:S(2)}, u32[]{:S(2)}) async-start(bf16[32,8,8,768]{3,2,1,0:T(8,128)(2,1)} %shard_map.111), calls=%async_computation | async-start | bytes 6291456 | tf_op jit(solution)/shard_map/all_to_all | solution.py:295
  11.8 3.8 %shard_map.110 = bf16[32,8,8,768]{3,2,1,0:T(8,128)(2,1)} custom-call(bf16[8,256,768]{2,1,0:T(8,128)(2,1)} %bitcast.23, bf16[256,256]{1,0:T(8,128)(2,1)} %f_ref.5), custom_call_target="tpu_custom_call" | custom-call | flops 805306368 | bytes 6291456 | tf_op jit(solution)/shard_map/pallas_call | solution.py:49
  15.7 67.6 %all-to-all-done = bf16[32,8,8,768]{3,2,1,0:T(8,128)(2,1)} async-done(((bf16[32,8,8,768]{3,2,1,0:T(8,128)(2,1)}), bf16[32,8,8,768]{3,2,1,0:T(8,128)(2,1)}, u32[]{:S(2)}, u32[]{:S(2)}) %all-to-all-start) | async-done | bytes 3145760 | tf_op jit(solution)/shard_map/all_to_all | solution.py:295
  83.3 4.0 %all-to-all-start.1 = ((bf16[32,8,8,768]{3,2,1,0:T(8,128)(2,1)}), bf16[32,8,8,768]{3,2,1,0:T(8,128)(2,1)}, u32[]{:S(2)}, u32[]{:S(2)}) async-start(bf16[32,8,8,768]{3,2,1,0:T(8,128)(2,1)} %shard_map.110), calls=%async_computation.1 | async-start | bytes 6291456 | tf_op jit(solution)/shard_map/all_to_all | solution.py:295
  87.3 7.8 %shard_map.112 = (bf16[8,256,768]{2,1,0:T(8,128)(2,1)}, bf16[32,8,8,768]{3,2,1,0:T(8,128)(2,1)}) custom-call(bf16[256,8,768]{2,1,0:T(8,128)(2,1)} %bitcast.2.m_ref.g_ref, bf16[8,256,768]{2,1,0:T(8,128)(2,1)} %k_ref.3, bf16[256,256]{1,0:T(8,128)(2,1)} %o_ref.3, bf16[256,256]{1,0:T(8,128)(2,1)} %b_ref.3), custom_call_target="tpu_custom_call" | custom-call | flops 1610612736 | bytes 12582912 | tf_op jit(solution)/shard_map/pallas_call | solution.py:110
  95.1 63.7 %all-to-all-done.1 = bf16[32,8,8,768]{3,2,1,0:T(8,128)(2,1)} async-done(((bf16[32,8,8,768]{3,2,1,0:T(8,128)(2,1)}), bf16[32,8,8,768]{3,2,1,0:T(8,128)(2,1)}, u32[]{:S(2)}, u32[]{:S(2)}) %all-to-all-start.1) | async-done | bytes 3145760 | tf_op jit(solution)/shard_map/all_to_all | solution.py:295
  158.8 4.0 %all-to-all-start.2 = ((bf16[32,8,8,768]{3,2,1,0:T(8,128)(2,1)}), bf16[32,8,8,768]{3,2,1,0:T(8,128)(2,1)}, u32[]{:S(2)}, u32[]{:S(2)}) async-start(bf16[32,8,8,768]{3,2,1,0:T(8,128)(2,1)} %get-tuple-element.31), calls=%async_computation.2 | async-start | bytes 6291456 | tf_op jit(solution)/shard_map/all_to_all | solution.py:295
  162.8 10.5 %shard_map.113 = (bf16[32,8,8,768]{3,2,1,0:T(8,128)(2,1)}, f32[256,256]{1,0:T(8,128)}, f32[256,256]{1,0:T(8,128)}) custom-call(bf16[256,8,768]{2,1,0:T(8,128)(2,1)} %bitcast.3.f_ref, bf16[256,8,768]{2,1,0:T(8,128)(2,1)} %bitcast.2.m_ref.g_ref, bf16[8,256,768]{2,1,0:T(8,128)(2,1)} %k_ref.3, bf16[8,256,768]{2,1,0:T(8,128)(2,1)} %get-tuple-element.29.gw_ref, ...), custom_call_target="tpu_custom_call" | custom-call | flops 3221225472 | bytes 15728640 | tf_op jit(solution)/shard_map/pallas_call | solution.py:160
  173.3 60.9 %all-to-all-done.2.g_ref = bf16[32,8,8,768]{3,2,1,0:T(8,128)(2,1)} async-done(((bf16[32,8,8,768]{3,2,1,0:T(8,128)(2,1)}), bf16[32,8,8,768]{3,2,1,0:T(8,128)(2,1)}, u32[]{:S(2)}, u32[]{:S(2)}) %all-to-all-start.2) | async-done | bytes 3145760 | tf_op jit(solution)/shard_map/all_to_all | solution.py:295
  234.3 4.0 %all-to-all-start.3 = ((bf16[32,8,8,768]{3,2,1,0:T(8,128)(2,1)}), bf16[32,8,8,768]{3,2,1,0:T(8,128)(2,1)}, u32[]{:S(2)}, u32[]{:S(2)}) async-start(bf16[32,8,8,768]{3,2,1,0:T(8,128)(2,1)} %get-tuple-element.34), calls=%async_computation.3 | async-start | bytes 6291456 | tf_op jit(solution)/shard_map/all_to_all | solution.py:295
  238.4 0.0 copy-start
  238.4 0.0 copy-start.1
  238.4 5.3 %shard_map.114 = (bf16[8,256,768]{2,1,0:T(8,128)(2,1)}, f32[256,256]{1,0:T(8,128)}) custom-call(bf16[32,8,8,768]{3,2,1,0:T(8,128)(2,1)} %all-to-all-done.2.g_ref, bf16[8,256,768]{2,1,0:T(8,128)(2,1)} %bitcast.24, bf16[256,256]{1,0:T(8,128)(2,1)} %f_ref.5), custom_call_target="tpu_custom_call" | custom-call | flops 1610612736 | bytes 9437184 | tf_op jit(solution)/shard_map/pallas_call | solution.py:194
  243.7 0.0 copy-done
  243.7 0.0 copy-done.1
  243.7 1.0 pad_maximum_fusion
  244.7 0.3 collective-permute-start
  245.0 1.5 collective-permute-done
  246.6 1.8 collective-permute-start.1
  248.4 16.9 %collective-permute-done.1 = f32[64,768]{1,0:T(8,128)S(1)} collective-permute-done((f32[64,768]{1,0:T(8,128)S(1)}, f32[64,768]{1,0:T(8,128)S(1)}, u32[]{:S(2)}, u32[]{:S(2)}) %collective-permute-start.1) | collective-permute-done | bytes 196640 | tf_op jit(solution)/shard_map/ppermute | solution.py:291
  265.3 1.1 collective-permute-start.2
  266.4 5.4 %collective-permute-done.2 = f32[32,768]{1,0:T(8,128)S(1)} collective-permute-done((f32[32,768]{1,0:T(8,128)S(1)}, f32[32,768]{1,0:T(8,128)S(1)}, u32[]{:S(2)}, u32[]{:S(2)}) %collective-permute-start.2) | collective-permute-done | bytes 98336 | tf_op jit(solution)/shard_map/ppermute | solution.py:291
  271.8 38.1 %all-to-all-done.3.r_ref = bf16[32,8,8,768]{3,2,1,0:T(8,128)(2,1)} async-done(((bf16[32,8,8,768]{3,2,1,0:T(8,128)(2,1)}), bf16[32,8,8,768]{3,2,1,0:T(8,128)(2,1)}, u32[]{:S(2)}, u32[]{:S(2)}) %all-to-all-start.3) | async-done | bytes 3145760 | tf_op jit(solution)/shard_map/all_to_all | solution.py:295
  309.9 0.0 collective-permute-start.3
  309.9 2.5 collective-permute-start.4
  312.3 1.9 collective-permute-start.5
  314.3 4.1 %shard_map.115 = bf16[256,256]{1,0:T(8,128)(2,1)} custom-call(bf16[32,8,8,768]{3,2,1,0:T(8,128)(2,1)} %all-to-all-done.3.r_ref, bf16[8,256,768]{2,1,0:T(8,128)(2,1)} %bitcast.26), custom_call_target="tpu_custom_call" | custom-call | flops 805306368 | bytes 6291456 | tf_op jit(solution)/shard_map/pallas_call | solution.py:227
  318.4 0.0 collective-permute-done.3
  318.4 0.0 collective-permute-done.4
  318.4 0.0 collective-permute-done.5
  318.4 1.3 collective-permute-start.6
  319.7 3.2 all-to-all-start.4
  322.9 0.2 collective-permute-done.6
  323.1 1.7 collective-permute-start.7
  324.8 6.3 %all-to-all-done.4 = bf16[32,8,256]{2,1,0:T(8,128)(2,1)S(1)} async-done(((bf16[32,8,256]{2,1,0:T(8,128)(2,1)}), bf16[32,8,256]{2,1,0:T(8,128)(2,1)S(1)}, u32[]{:S(2)}, u32[]{:S(2)}) %all-to-all-start.4) | async-done | bytes 131104 | tf_op jit(solution)/shard_map/all_to_all | solution.py:295
  331.2 0.7 broadcast_in_dim.10
  331.9 2.6 all-to-all-start.5
  334.4 0.0 collective-permute-done.7
  334.5 0.2 collective-permute-start.8
  334.7 8.0 %all-to-all-done.5 = bf16[32,8,256]{2,1,0:T(8,128)(2,1)S(1)} async-done(((bf16[32,8,256]{2,1,0:T(8,128)(2,1)}), bf16[32,8,256]{2,1,0:T(8,128)(2,1)S(1)}, u32[]{:S(2)}, u32[]{:S(2)}) %all-to-all-start.5) | async-done | bytes 131104 | tf_op jit(solution)/shard_map/all_to_all | solution.py:295
  342.7 0.7 multiply_bitcast_fusion
  343.4 0.0 collective-permute-done.8
  343.4 0.1 broadcast_select_fusion.1
  343.5 0.1 maximum_multiply_fusion
  343.5 0.9 fusion
  (12 shorter events, 0.3 us)
Async XLA Ops:
  4.4 78.9 %all-to-all-start = ((bf16[32,8,8,768]{3,2,1,0:T(8,128)(2,1)}), bf16[32,8,8,768]{3,2,1,0:T(8,128)(2,1)}, u32[]{:S(2)}, u32[]{:S(2)}) async-start(bf16[32,8,8,768]{3,2,1,0:T(8,128)(2,1)} %shard_map.111), calls=%async_computation | async-start | bytes 6291456 | tf_op jit(solution)/shard_map/all_to_all | solution.py:295
  83.3 75.5 %all-to-all-start.1 = ((bf16[32,8,8,768]{3,2,1,0:T(8,128)(2,1)}), bf16[32,8,8,768]{3,2,1,0:T(8,128)(2,1)}, u32[]{:S(2)}, u32[]{:S(2)}) async-start(bf16[32,8,8,768]{3,2,1,0:T(8,128)(2,1)} %shard_map.110), calls=%async_computation.1 | async-start | bytes 6291456 | tf_op jit(solution)/shard_map/all_to_all | solution.py:295
  158.8 75.5 %all-to-all-start.2 = ((bf16[32,8,8,768]{3,2,1,0:T(8,128)(2,1)}), bf16[32,8,8,768]{3,2,1,0:T(8,128)(2,1)}, u32[]{:S(2)}, u32[]{:S(2)}) async-start(bf16[32,8,8,768]{3,2,1,0:T(8,128)(2,1)} %get-tuple-element.31), calls=%async_computation.2 | async-start | bytes 6291456 | tf_op jit(solution)/shard_map/all_to_all | solution.py:295
  234.3 75.6 %all-to-all-start.3 = ((bf16[32,8,8,768]{3,2,1,0:T(8,128)(2,1)}), bf16[32,8,8,768]{3,2,1,0:T(8,128)(2,1)}, u32[]{:S(2)}, u32[]{:S(2)}) async-start(bf16[32,8,8,768]{3,2,1,0:T(8,128)(2,1)} %get-tuple-element.34), calls=%async_computation.3 | async-start | bytes 6291456 | tf_op jit(solution)/shard_map/all_to_all | solution.py:295
  238.4 5.3 %copy-start = (f32[256,256]{1,0:T(8,128)S(1)}, f32[256,256]{1,0:T(8,128)}, u32[]{:S(2)}) copy-start(f32[256,256]{1,0:T(8,128)} %get-tuple-element.36) | copy-start | bytes 786436
  238.4 5.3 %copy-start.1 = (f32[256,256]{1,0:T(8,128)S(1)}, f32[256,256]{1,0:T(8,128)}, u32[]{:S(2)}) copy-start(f32[256,256]{1,0:T(8,128)} %get-tuple-element.37) | copy-start | bytes 786436
  244.7 1.8 collective-permute-start
  246.6 18.6 %collective-permute-start.1 = (f32[64,768]{1,0:T(8,128)S(1)}, f32[64,768]{1,0:T(8,128)S(1)}, u32[]{:S(2)}, u32[]{:S(2)}) collective-permute-start(f32[64,768]{1,0:T(8,128)S(1)} %dynamic-slice_bitcast_fusion.1), channel_id=1, source_target_pairs={{0,2},{1,3},{2,0},{3,1},{4,6},{5,7},{6,4},{7,5},{8,10},{9,11},{10,... | collective-permute-start | bytes 589832 | tf_op jit(solution)/shard_map/ppermute | solution.py:291
  265.3 6.5 %collective-permute-start.2 = (f32[32,768]{1,0:T(8,128)S(1)}, f32[32,768]{1,0:T(8,128)S(1)}, u32[]{:S(2)}, u32[]{:S(2)}) collective-permute-start(f32[32,768]{1,0:T(8,128)S(1)} %dynamic-slice_bitcast_fusion.2), channel_id=1, source_target_pairs={{0,4},{1,5},{2,6},{3,7},{4,0},{5,1},{6,2},{7,3},{8,12},{9,13},{10,... | collective-permute-start | bytes 294920 | tf_op jit(solution)/shard_map/ppermute | solution.py:291
  309.9 8.5 %collective-permute-start.3 = (bf16[32,768]{1,0:T(8,128)(2,1)S(1)}, bf16[32,768]{1,0:T(8,128)(2,1)S(1)}, u32[]{:S(2)}, u32[]{:S(2)}) collective-permute-start(bf16[32,768]{1,0:T(8,128)(2,1)S(1)} %bitcast_add_fusion.2), channel_id=1, source_target_pairs={{0,8},{1,9},{2,10},{3,11},{4,12},{5,13},{6,14},{7,15},{8,0},{9,1},... | collective-permute-start | bytes 147464 | tf_op jit(solution)/shard_map/ppermute | solution.py:291
  309.9 8.5 %collective-permute-start.4 = (bf16[32,768]{1,0:T(8,128)(2,1)S(1)}, bf16[32,768]{1,0:T(8,128)(2,1)S(1)}, u32[]{:S(2)}, u32[]{:S(2)}) collective-permute-start(bf16[32,768]{1,0:T(8,128)(2,1)S(1)} %bitcast_add_fusion.2), channel_id=1, source_target_pairs={{0,16},{1,17},{2,18},{3,19},{4,20},{5,21},{6,22},{7,23},{8,24},{9,... | collective-permute-start | bytes 147464 | tf_op jit(solution)/shard_map/ppermute | solution.py:291
  312.3 6.0 %collective-permute-start.5 = (bf16[32,768]{1,0:T(8,128)(2,1)S(1)}, bf16[32,768]{1,0:T(8,128)(2,1)S(1)}, u32[]{:S(2)}, u32[]{:S(2)}) collective-permute-start(bf16[32,768]{1,0:T(8,128)(2,1)S(1)} %bitcast_add_fusion.2), channel_id=1, source_target_pairs={{0,24},{1,25},{2,26},{3,27},{4,28},{5,29},{6,30},{7,31},{8,16},{9,... | collective-permute-start | bytes 147464 | tf_op jit(solution)/shard_map/ppermute | solution.py:291
  318.4 4.7 %collective-permute-start.6 = (f32[32,768]{1,0:T(8,128)S(1)}, f32[32,768]{1,0:T(8,128)S(1)}, u32[]{:S(2)}, u32[]{:S(2)}) collective-permute-start(f32[32,768]{1,0:T(8,128)S(1)} %add_add_fusion), channel_id=1, source_target_pairs={{0,4},{1,5},{2,6},{3,7},{4,0},{5,1},{6,2},{7,3},{8,12},{9,13},{10,... | collective-permute-start | bytes 294920 | tf_op jit(solution)/shard_map/ppermute | solution.py:291
  319.7 11.5 %all-to-all-start.4 = ((bf16[32,8,256]{2,1,0:T(8,128)(2,1)}), bf16[32,8,256]{2,1,0:T(8,128)(2,1)S(1)}, u32[]{:S(2)}, u32[]{:S(2)}) async-start(bf16[32,8,256]{2,1,0:T(8,128)(2,1)} %bitcast.33), calls=%async_computation.4 | async-start | bytes 262144 | tf_op jit(solution)/shard_map/all_to_all | solution.py:295
  323.1 11.3 %collective-permute-start.7 = (f32[64,768]{1,0:T(8,128)S(1)}, f32[64,768]{1,0:T(8,128)S(1)}, u32[]{:S(2)}, u32[]{:S(2)}) collective-permute-start(f32[64,768]{1,0:T(8,128)S(1)} %pad_maximum_fusion.2), channel_id=1, source_target_pairs={{0,2},{1,3},{2,0},{3,1},{4,6},{5,7},{6,4},{7,5},{8,10},{9,11},{10,... | collective-permute-start | bytes 589832 | tf_op jit(solution)/shard_map/ppermute | solution.py:291
  331.9 10.8 %all-to-all-start.5 = ((bf16[32,8,256]{2,1,0:T(8,128)(2,1)}), bf16[32,8,256]{2,1,0:T(8,128)(2,1)S(1)}, u32[]{:S(2)}, u32[]{:S(2)}) async-start(bf16[32,8,256]{2,1,0:T(8,128)(2,1)} %broadcast_in_dim.10), calls=%async_computation.5 | async-start | bytes 262144 | tf_op jit(solution)/shard_map/all_to_all | solution.py:295
  334.5 8.9 %collective-permute-start.8 = (f32[128,768]{1,0:T(8,128)S(1)}, f32[128,768]{1,0:T(8,128)S(1)}, u32[]{:S(2)}, u32[]{:S(2)}) collective-permute-start(f32[128,768]{1,0:T(8,128)S(1)} %pad_maximum_fusion.1), channel_id=1, source_target_pairs={{0,1},{1,0},{2,3},{3,2},{4,5},{5,4},{6,7},{7,6},{8,9},{9,8},{10,11... | collective-permute-start | bytes 1179656 | tf_op jit(solution)/shard_map/ppermute | solution.py:291

commit v5 on v4

--- a/solution.py
+++ b/solution.py
@@ -369,7 +369,6 @@
     returned = move(sent)
     grad_values, grad_inner = finish_values(grad_first, values[0], inner_factor)
     early = plane_sum(jnp.concatenate((grad_inner, grad_outer, grad_back), axis=1))
-    returned, early = lax.optimization_barrier((returned, early))
     quarters = across(early)
     grad_last = finish_return(returned, cotangent[0])
     (a, b, c, d), grad_last = lax.optimization_barrier((quarters, grad_last))

time: 345 us -> 343 us (level)
  waiting for transfers between devices: 269 us -> 263 us
    all_to_all x6, waiting for transfers between devices: 245 us -> 239 us  [move(): return lax.all_to_all(x, 'seq', 0, 0, tiled=True)]
where the time goes in v5:
time: 343 us; the launch traced here: 342 us
  waiting for transfers between devices  263 us (77%)
  starting transfers between devices  39 us (11%)
  Pallas kernels  35.3 us (10%)
    all_to_all x6, waiting for transfers between devices, move(): return lax.all_to_all(x, 'seq', 0, 0, tiled=True)  239 us
    all_to_all x6, starting transfers between devices, move(): return lax.all_to_all(x, 'seq', 0, 0, tiled=True)  25.2 us
    ppermute x9, waiting for transfers between devices, swap(): return lax.ppermute(x, 'seq', [(i, i ^ bits) for i in range(size)])  24.3 us
    ppermute x9, starting transfers between devices, swap(): return lax.ppermute(x, 'seq', [(i, i ^ bits) for i in range(size)])  13.8 us
    pallas_call x1, Pallas kernels, forward_mixed(): call(body, (channels // width,), [moved, moved, mine, mine, square(order)...  10.5 us
    pallas_call x1, Pallas kernels, backward_mixed(): call(body, (channels // width,), [pl.BlockSpec((order, part, width), lamb...  7.8 us
    pallas_call x2, Pallas kernels, apply_inner(): call(body, (rows // step,), [pl.BlockSpec((step, order, channels), lambda...  7.62 us
  transfers between devices with their start and end apart: 15, of which 10 were waited for; matrix products, arithmetic and copies ran while one was open for 1% of the time, Pallas kernels for 9%

profile of v5, /device:TPU:0, one launch (start us, length us, event | category | flops | bytes accessed | tf_op | source)
XLA Modules:
  0.0 342.3 jit_solution(5398715310807863659)
XLA Ops:
  0.6 3.8 %shard_map.111 = bf16[32,8,8,768]{3,2,1,0:T(8,128)(2,1)} custom-call(bf16[8,256,768]{2,1,0:T(8,128)(2,1)} %bitcast.27, bf16[256,256]{1,0:T(8,128)(2,1)} %f_ref.4), custom_call_target="tpu_custom_call" | custom-call | flops 805306368 | bytes 6291456 | tf_op jit(solution)/shard_map/pallas_call | solution.py:49
  4.4 7.4 %all-to-all-start = ((bf16[32,8,8,768]{3,2,1,0:T(8,128)(2,1)}), bf16[32,8,8,768]{3,2,1,0:T(8,128)(2,1)}, u32[]{:S(2)}, u32[]{:S(2)}) async-start(bf16[32,8,8,768]{3,2,1,0:T(8,128)(2,1)} %shard_map.111), calls=%async_computation | async-start | bytes 6291456 | tf_op jit(solution)/shard_map/all_to_all | solution.py:295
  11.8 3.8 %shard_map.110 = bf16[32,8,8,768]{3,2,1,0:T(8,128)(2,1)} custom-call(bf16[8,256,768]{2,1,0:T(8,128)(2,1)} %bitcast.25, bf16[256,256]{1,0:T(8,128)(2,1)} %f_ref.5), custom_call_target="tpu_custom_call" | custom-call | flops 805306368 | bytes 6291456 | tf_op jit(solution)/shard_map/pallas_call | solution.py:49
  15.7 67.6 %all-to-all-done = bf16[32,8,8,768]{3,2,1,0:T(8,128)(2,1)} async-done(((bf16[32,8,8,768]{3,2,1,0:T(8,128)(2,1)}), bf16[32,8,8,768]{3,2,1,0:T(8,128)(2,1)}, u32[]{:S(2)}, u32[]{:S(2)}) %all-to-all-start) | async-done | bytes 3145760 | tf_op jit(solution)/shard_map/all_to_all | solution.py:295
  83.3 4.0 %all-to-all-start.1 = ((bf16[32,8,8,768]{3,2,1,0:T(8,128)(2,1)}), bf16[32,8,8,768]{3,2,1,0:T(8,128)(2,1)}, u32[]{:S(2)}, u32[]{:S(2)}) async-start(bf16[32,8,8,768]{3,2,1,0:T(8,128)(2,1)} %shard_map.110), calls=%async_computation.1 | async-start | bytes 6291456 | tf_op jit(solution)/shard_map/all_to_all | solution.py:295
  87.3 7.8 %shard_map.112 = (bf16[8,256,768]{2,1,0:T(8,128)(2,1)}, bf16[32,8,8,768]{3,2,1,0:T(8,128)(2,1)}) custom-call(bf16[256,8,768]{2,1,0:T(8,128)(2,1)} %bitcast.2.m_ref.g_ref, bf16[8,256,768]{2,1,0:T(8,128)(2,1)} %k_ref.3, bf16[256,256]{1,0:T(8,128)(2,1)} %o_ref.3, bf16[256,256]{1,0:T(8,128)(2,1)} %b_ref.3), custom_call_target="tpu_custom_call" | custom-call | flops 1610612736 | bytes 12582912 | tf_op jit(solution)/shard_map/pallas_call | solution.py:110
  95.1 63.7 %all-to-all-done.1 = bf16[32,8,8,768]{3,2,1,0:T(8,128)(2,1)} async-done(((bf16[32,8,8,768]{3,2,1,0:T(8,128)(2,1)}), bf16[32,8,8,768]{3,2,1,0:T(8,128)(2,1)}, u32[]{:S(2)}, u32[]{:S(2)}) %all-to-all-start.1) | async-done | bytes 3145760 | tf_op jit(solution)/shard_map/all_to_all | solution.py:295
  158.8 4.0 %all-to-all-start.2 = ((bf16[32,8,8,768]{3,2,1,0:T(8,128)(2,1)}), bf16[32,8,8,768]{3,2,1,0:T(8,128)(2,1)}, u32[]{:S(2)}, u32[]{:S(2)}) async-start(bf16[32,8,8,768]{3,2,1,0:T(8,128)(2,1)} %get-tuple-element.29), calls=%async_computation.2 | async-start | bytes 6291456 | tf_op jit(solution)/shard_map/all_to_all | solution.py:295
  162.8 10.5 %shard_map.113 = (bf16[32,8,8,768]{3,2,1,0:T(8,128)(2,1)}, f32[256,256]{1,0:T(8,128)}, f32[256,256]{1,0:T(8,128)}) custom-call(bf16[256,8,768]{2,1,0:T(8,128)(2,1)} %bitcast.3.f_ref, bf16[256,8,768]{2,1,0:T(8,128)(2,1)} %bitcast.2.m_ref.g_ref, bf16[8,256,768]{2,1,0:T(8,128)(2,1)} %k_ref.3, bf16[8,256,768]{2,1,0:T(8,128)(2,1)} %get-tuple-element.27.gw_ref, ...), custom_call_target="tpu_custom_call" | custom-call | flops 3221225472 | bytes 15728640 | tf_op jit(solution)/shard_map/pallas_call | solution.py:160
  173.3 60.9 %all-to-all-done.2.g_ref = bf16[32,8,8,768]{3,2,1,0:T(8,128)(2,1)} async-done(((bf16[32,8,8,768]{3,2,1,0:T(8,128)(2,1)}), bf16[32,8,8,768]{3,2,1,0:T(8,128)(2,1)}, u32[]{:S(2)}, u32[]{:S(2)}) %all-to-all-start.2) | async-done | bytes 3145760 | tf_op jit(solution)/shard_map/all_to_all | solution.py:295
  234.3 4.0 %all-to-all-start.3 = ((bf16[32,8,8,768]{3,2,1,0:T(8,128)(2,1)}), bf16[32,8,8,768]{3,2,1,0:T(8,128)(2,1)}, u32[]{:S(2)}, u32[]{:S(2)}) async-start(bf16[32,8,8,768]{3,2,1,0:T(8,128)(2,1)} %get-tuple-element.35), calls=%async_computation.3 | async-start | bytes 6291456 | tf_op jit(solution)/shard_map/all_to_all | solution.py:295
  238.4 0.0 copy-start
  238.4 0.0 copy-start.1
  238.4 5.3 %shard_map.114 = (bf16[8,256,768]{2,1,0:T(8,128)(2,1)}, f32[256,256]{1,0:T(8,128)}) custom-call(bf16[32,8,8,768]{3,2,1,0:T(8,128)(2,1)} %all-to-all-done.2.g_ref, bf16[8,256,768]{2,1,0:T(8,128)(2,1)} %bitcast.26, bf16[256,256]{1,0:T(8,128)(2,1)} %f_ref.5), custom_call_target="tpu_custom_call" | custom-call | flops 1610612736 | bytes 9437184 | tf_op jit(solution)/shard_map/pallas_call | solution.py:194
  243.7 0.0 copy-done
  243.7 0.0 copy-done.1
  243.7 1.0 pad_maximum_fusion
  244.7 0.3 collective-permute-start
  245.0 1.5 collective-permute-done
  246.6 1.8 collective-permute-start.1
  248.4 16.9 %collective-permute-done.1 = f32[64,768]{1,0:T(8,128)S(1)} collective-permute-done((f32[64,768]{1,0:T(8,128)S(1)}, f32[64,768]{1,0:T(8,128)S(1)}, u32[]{:S(2)}, u32[]{:S(2)}) %collective-permute-start.1) | collective-permute-done | bytes 196640 | tf_op jit(solution)/shard_map/ppermute | solution.py:291
  265.3 1.1 collective-permute-start.2
  266.4 5.4 %collective-permute-done.2 = f32[32,768]{1,0:T(8,128)S(1)} collective-permute-done((f32[32,768]{1,0:T(8,128)S(1)}, f32[32,768]{1,0:T(8,128)S(1)}, u32[]{:S(2)}, u32[]{:S(2)}) %collective-permute-start.2) | collective-permute-done | bytes 98336 | tf_op jit(solution)/shard_map/ppermute | solution.py:291
  271.8 0.1 collective-permute-start.3
  271.9 7.9 %collective-permute-start.4 = (bf16[32,768]{1,0:T(8,128)(2,1)S(1)}, bf16[32,768]{1,0:T(8,128)(2,1)S(1)}, u32[]{:S(2)}, u32[]{:S(2)}) collective-permute-start(bf16[32,768]{1,0:T(8,128)(2,1)S(1)} %fusion), channel_id=1, source_target_pairs={{0,16},{1,17},{2,18},{3,19},{4,20},{5,21},{6,22},{7,23},{8,24},{9,... | collective-permute-start | bytes 147464 | tf_op jit(solution)/shard_map/ppermute | solution.py:291
  279.8 0.0 collective-permute-start.5
  279.8 32.7 %all-to-all-done.3.r_ref = bf16[32,8,8,768]{3,2,1,0:T(8,128)(2,1)} async-done(((bf16[32,8,8,768]{3,2,1,0:T(8,128)(2,1)}), bf16[32,8,8,768]{3,2,1,0:T(8,128)(2,1)}, u32[]{:S(2)}, u32[]{:S(2)}) %all-to-all-start.3) | async-done | bytes 3145760 | tf_op jit(solution)/shard_map/all_to_all | solution.py:295
  312.4 4.1 %shard_map.115 = bf16[256,256]{1,0:T(8,128)(2,1)} custom-call(bf16[32,8,8,768]{3,2,1,0:T(8,128)(2,1)} %all-to-all-done.3.r_ref, bf16[8,256,768]{2,1,0:T(8,128)(2,1)} %bitcast.28), custom_call_target="tpu_custom_call" | custom-call | flops 805306368 | bytes 6291456 | tf_op jit(solution)/shard_map/pallas_call | solution.py:227
  316.6 0.0 collective-permute-done.3
  316.6 0.0 collective-permute-done.4
  316.6 0.0 collective-permute-done.5
  316.6 1.2 collective-permute-start.6
  317.8 3.0 all-to-all-start.4
  320.8 0.5 collective-permute-done.6
  321.3 1.4 collective-permute-start.7
  322.7 6.3 %all-to-all-done.4 = bf16[32,8,256]{2,1,0:T(8,128)(2,1)S(1)} async-done(((bf16[32,8,256]{2,1,0:T(8,128)(2,1)}), bf16[32,8,256]{2,1,0:T(8,128)(2,1)S(1)}, u32[]{:S(2)}, u32[]{:S(2)}) %all-to-all-start.4) | async-done | bytes 131104 | tf_op jit(solution)/shard_map/all_to_all | solution.py:295
  329.1 0.7 broadcast_in_dim.10
  329.8 2.6 all-to-all-start.5
  332.4 0.0 collective-permute-done.7
  332.4 0.2 collective-permute-start.8
  332.6 8.0 %all-to-all-done.5 = bf16[32,8,256]{2,1,0:T(8,128)(2,1)S(1)} async-done(((bf16[32,8,256]{2,1,0:T(8,128)(2,1)}), bf16[32,8,256]{2,1,0:T(8,128)(2,1)S(1)}, u32[]{:S(2)}, u32[]{:S(2)}) %all-to-all-start.5) | async-done | bytes 131104 | tf_op jit(solution)/shard_map/all_to_all | solution.py:295
  340.6 0.7 multiply_bitcast_fusion
  341.3 0.0 collective-permute-done.8
  341.3 0.1 broadcast_select_fusion.1
  341.4 0.1 maximum_multiply_fusion
  341.5 0.9 fusion.1
  (12 shorter events, 0.3 us)
Async XLA Ops:
  4.4 78.9 %all-to-all-start = ((bf16[32,8,8,768]{3,2,1,0:T(8,128)(2,1)}), bf16[32,8,8,768]{3,2,1,0:T(8,128)(2,1)}, u32[]{:S(2)}, u32[]{:S(2)}) async-start(bf16[32,8,8,768]{3,2,1,0:T(8,128)(2,1)} %shard_map.111), calls=%async_computation | async-start | bytes 6291456 | tf_op jit(solution)/shard_map/all_to_all | solution.py:295
  83.3 75.5 %all-to-all-start.1 = ((bf16[32,8,8,768]{3,2,1,0:T(8,128)(2,1)}), bf16[32,8,8,768]{3,2,1,0:T(8,128)(2,1)}, u32[]{:S(2)}, u32[]{:S(2)}) async-start(bf16[32,8,8,768]{3,2,1,0:T(8,128)(2,1)} %shard_map.110), calls=%async_computation.1 | async-start | bytes 6291456 | tf_op jit(solution)/shard_map/all_to_all | solution.py:295
  158.8 75.5 %all-to-all-start.2 = ((bf16[32,8,8,768]{3,2,1,0:T(8,128)(2,1)}), bf16[32,8,8,768]{3,2,1,0:T(8,128)(2,1)}, u32[]{:S(2)}, u32[]{:S(2)}) async-start(bf16[32,8,8,768]{3,2,1,0:T(8,128)(2,1)} %get-tuple-element.29), calls=%async_computation.2 | async-start | bytes 6291456 | tf_op jit(solution)/shard_map/all_to_all | solution.py:295
  234.3 78.2 %all-to-all-start.3 = ((bf16[32,8,8,768]{3,2,1,0:T(8,128)(2,1)}), bf16[32,8,8,768]{3,2,1,0:T(8,128)(2,1)}, u32[]{:S(2)}, u32[]{:S(2)}) async-start(bf16[32,8,8,768]{3,2,1,0:T(8,128)(2,1)} %get-tuple-element.35), calls=%async_computation.3 | async-start | bytes 6291456 | tf_op jit(solution)/shard_map/all_to_all | solution.py:295
  238.4 5.3 %copy-start = (f32[256,256]{1,0:T(8,128)S(1)}, f32[256,256]{1,0:T(8,128)}, u32[]{:S(2)}) copy-start(f32[256,256]{1,0:T(8,128)} %get-tuple-element.33) | copy-start | bytes 786436
  238.4 5.3 %copy-start.1 = (f32[256,256]{1,0:T(8,128)S(1)}, f32[256,256]{1,0:T(8,128)}, u32[]{:S(2)}) copy-start(f32[256,256]{1,0:T(8,128)} %get-tuple-element.34) | copy-start | bytes 786436
  244.7 1.8 collective-permute-start
  246.6 18.6 %collective-permute-start.1 = (f32[64,768]{1,0:T(8,128)S(1)}, f32[64,768]{1,0:T(8,128)S(1)}, u32[]{:S(2)}, u32[]{:S(2)}) collective-permute-start(f32[64,768]{1,0:T(8,128)S(1)} %dynamic-slice_bitcast_fusion.1), channel_id=1, source_target_pairs={{0,2},{1,3},{2,0},{3,1},{4,6},{5,7},{6,4},{7,5},{8,10},{9,11},{10,... | collective-permute-start | bytes 589832 | tf_op jit(solution)/shard_map/ppermute | solution.py:291
  265.3 6.5 %collective-permute-start.2 = (f32[32,768]{1,0:T(8,128)S(1)}, f32[32,768]{1,0:T(8,128)S(1)}, u32[]{:S(2)}, u32[]{:S(2)}) collective-permute-start(f32[32,768]{1,0:T(8,128)S(1)} %dynamic-slice_bitcast_fusion.2), channel_id=1, source_target_pairs={{0,4},{1,5},{2,6},{3,7},{4,0},{5,1},{6,2},{7,3},{8,12},{9,13},{10,... | collective-permute-start | bytes 294920 | tf_op jit(solution)/shard_map/ppermute | solution.py:291
  271.8 44.8 %collective-permute-start.3 = (bf16[32,768]{1,0:T(8,128)(2,1)S(1)}, bf16[32,768]{1,0:T(8,128)(2,1)S(1)}, u32[]{:S(2)}, u32[]{:S(2)}) collective-permute-start(bf16[32,768]{1,0:T(8,128)(2,1)S(1)} %fusion), channel_id=1, source_target_pairs={{0,8},{1,9},{2,10},{3,11},{4,12},{5,13},{6,14},{7,15},{8,0},{9,1},... | collective-permute-start | bytes 147464 | tf_op jit(solution)/shard_map/ppermute | solution.py:291
  271.9 44.7 %collective-permute-start.4 = (bf16[32,768]{1,0:T(8,128)(2,1)S(1)}, bf16[32,768]{1,0:T(8,128)(2,1)S(1)}, u32[]{:S(2)}, u32[]{:S(2)}) collective-permute-start(bf16[32,768]{1,0:T(8,128)(2,1)S(1)} %fusion), channel_id=1, source_target_pairs={{0,16},{1,17},{2,18},{3,19},{4,20},{5,21},{6,22},{7,23},{8,24},{9,... | collective-permute-start | bytes 147464 | tf_op jit(solution)/shard_map/ppermute | solution.py:291
  279.8 36.8 %collective-permute-start.5 = (bf16[32,768]{1,0:T(8,128)(2,1)S(1)}, bf16[32,768]{1,0:T(8,128)(2,1)S(1)}, u32[]{:S(2)}, u32[]{:S(2)}) collective-permute-start(bf16[32,768]{1,0:T(8,128)(2,1)S(1)} %fusion), channel_id=1, source_target_pairs={{0,24},{1,25},{2,26},{3,27},{4,28},{5,29},{6,30},{7,31},{8,16},{9,... | collective-permute-start | bytes 147464 | tf_op jit(solution)/shard_map/ppermute | solution.py:291
  316.6 4.7 %collective-permute-start.6 = (f32[32,768]{1,0:T(8,128)S(1)}, f32[32,768]{1,0:T(8,128)S(1)}, u32[]{:S(2)}, u32[]{:S(2)}) collective-permute-start(f32[32,768]{1,0:T(8,128)S(1)} %add_add_fusion), channel_id=1, source_target_pairs={{0,4},{1,5},{2,6},{3,7},{4,0},{5,1},{6,2},{7,3},{8,12},{9,13},{10,... | collective-permute-start | bytes 294920 | tf_op jit(solution)/shard_map/ppermute | solution.py:291
  317.8 11.3 %all-to-all-start.4 = ((bf16[32,8,256]{2,1,0:T(8,128)(2,1)}), bf16[32,8,256]{2,1,0:T(8,128)(2,1)S(1)}, u32[]{:S(2)}, u32[]{:S(2)}) async-start(bf16[32,8,256]{2,1,0:T(8,128)(2,1)} %bitcast.35), calls=%async_computation.4 | async-start | bytes 262144 | tf_op jit(solution)/shard_map/all_to_all | solution.py:295
  321.3 11.0 %collective-permute-start.7 = (f32[64,768]{1,0:T(8,128)S(1)}, f32[64,768]{1,0:T(8,128)S(1)}, u32[]{:S(2)}, u32[]{:S(2)}) collective-permute-start(f32[64,768]{1,0:T(8,128)S(1)} %pad_maximum_fusion.2), channel_id=1, source_target_pairs={{0,2},{1,3},{2,0},{3,1},{4,6},{5,7},{6,4},{7,5},{8,10},{9,11},{10,... | collective-permute-start | bytes 589832 | tf_op jit(solution)/shard_map/ppermute | solution.py:291
  329.8 10.8 %all-to-all-start.5 = ((bf16[32,8,256]{2,1,0:T(8,128)(2,1)}), bf16[32,8,256]{2,1,0:T(8,128)(2,1)S(1)}, u32[]{:S(2)}, u32[]{:S(2)}) async-start(bf16[32,8,256]{2,1,0:T(8,128)(2,1)} %broadcast_in_dim.10), calls=%async_computation.5 | async-start | bytes 262144 | tf_op jit(solution)/shard_map/all_to_all | solution.py:295
  332.4 8.9 %collective-permute-start.8 = (f32[128,768]{1,0:T(8,128)S(1)}, f32[128,768]{1,0:T(8,128)S(1)}, u32[]{:S(2)}, u32[]{:S(2)}) collective-permute-start(f32[128,768]{1,0:T(8,128)S(1)} %pad_maximum_fusion.1), channel_id=1, source_target_pairs={{0,1},{1,0},{2,3},{3,2},{4,5},{5,4},{6,7},{7,6},{8,9},{9,8},{10,11... | collective-permute-start | bytes 1179656 | tf_op jit(solution)/shard_map/ppermute | solution.py:291

commit v6 on v4

--- a/solution.py
+++ b/solution.py
@@ -316,12 +316,6 @@
     return x
 
 
-def across(x):
-    x = x.astype(BF16)
-    near, *far = [swap(x, bits) for bits in (8, 16, 24)]
-    return x, near, *far
-
-
 def joined(x):
     for bit in (4, 2, 1):
         x = join(x, swap(x, bit), bit)
@@ -369,11 +363,13 @@
     returned = move(sent)
     grad_values, grad_inner = finish_values(grad_first, values[0], inner_factor)
     early = plane_sum(jnp.concatenate((grad_inner, grad_outer, grad_back), axis=1))
+    early = early + swap(early, 8)
     returned, early = lax.optimization_barrier((returned, early))
-    quarters = across(early)
+    early = early.astype(BF16)
+    other = swap(early, 16)
     grad_last = finish_return(returned, cotangent[0])
-    (a, b, c, d), grad_last = lax.optimization_barrier((quarters, grad_last))
-    early = (a.astype(F32) + b.astype(F32)) + (c.astype(F32) + d.astype(F32))
+    other, grad_last = lax.optimization_barrier((other, grad_last))
+    early = early.astype(F32) + other.astype(F32)
     early = joined(early) * scale
     grad_last = late_sum(grad_last) * scale
     return (grad_values[None], *jnp.split(early, 3, axis=1), grad_last)

time: 345 us -> 341 us (0.988)
  starting transfers between devices: 36 us -> 31.8 us
    ppermute x9 -> x8, waiting for transfers between devices: 24 us -> 45.2 us  [swap(): return lax.ppermute(x, 'seq', [(i, i ^ bits) for i in range(size)])]
    all_to_all x6, waiting for transfers between devices: 245 us -> 224 us  [move(): return lax.all_to_all(x, 'seq', 0, 0, tiled=True)]
    ppermute x9 -> x8, starting transfers between devices: 10.6 us -> 6.28 us  [swap(): return lax.ppermute(x, 'seq', [(i, i ^ bits) for i in range(size)])]
  transfers between devices with their start and end apart: 15 -> 14, of which waited for: 10 -> 12; matrix products, arithmetic and copies ran while one was open for 1% -> 1% of each run, Pallas kernels for 9% -> 9%
where the time goes in v6:
time: 341 us
  waiting for transfers between devices  269 us (79%)
  Pallas kernels  35.2 us (10%)
  starting transfers between devices  31.8 us (9%)
    all_to_all x6, waiting for transfers between devices, move(): return lax.all_to_all(x, 'seq', 0, 0, tiled=True)  224 us
    ppermute x8, waiting for transfers between devices, swap(): return lax.ppermute(x, 'seq', [(i, i ^ bits) for i in range(size)])  45.2 us
    all_to_all x6, starting transfers between devices, move(): return lax.all_to_all(x, 'seq', 0, 0, tiled=True)  25.5 us
    pallas_call x1, Pallas kernels, forward_mixed(): call(body, (channels // width,), [moved, moved, mine, mine, square(order)...  10.5 us
    pallas_call x1, Pallas kernels, backward_mixed(): call(body, (channels // width,), [pl.BlockSpec((order, part, width), lamb...  7.72 us
    pallas_call x2, Pallas kernels, apply_inner(): call(body, (rows // step,), [pl.BlockSpec((step, order, channels), lambda...  7.62 us
  transfers between devices with their start and end apart: 14, of which 12 were waited for; matrix products, arithmetic and copies ran while one was open for 1% of the time, Pallas kernels for 9%

profile of v6, /device:TPU:0, one launch (start us, length us, event | category | flops | bytes accessed | tf_op | source)
XLA Modules:
  0.0 341.0 jit_solution(4569888905044239280)
XLA Ops:
  0.6 3.8 %shard_map.111 = bf16[32,8,8,768]{3,2,1,0:T(8,128)(2,1)} custom-call(bf16[8,256,768]{2,1,0:T(8,128)(2,1)} %bitcast.25, bf16[256,256]{1,0:T(8,128)(2,1)} %f_ref.4), custom_call_target="tpu_custom_call" | custom-call | flops 805306368 | bytes 6291456 | tf_op jit(solution)/shard_map/pallas_call | solution.py:49
  4.4 7.4 %all-to-all-start = ((bf16[32,8,8,768]{3,2,1,0:T(8,128)(2,1)}), bf16[32,8,8,768]{3,2,1,0:T(8,128)(2,1)}, u32[]{:S(2)}, u32[]{:S(2)}) async-start(bf16[32,8,8,768]{3,2,1,0:T(8,128)(2,1)} %shard_map.111), calls=%async_computation | async-start | bytes 6291456 | tf_op jit(solution)/shard_map/all_to_all | solution.py:295
  11.8 3.8 %shard_map.110 = bf16[32,8,8,768]{3,2,1,0:T(8,128)(2,1)} custom-call(bf16[8,256,768]{2,1,0:T(8,128)(2,1)} %bitcast.23, bf16[256,256]{1,0:T(8,128)(2,1)} %f_ref.5), custom_call_target="tpu_custom_call" | custom-call | flops 805306368 | bytes 6291456 | tf_op jit(solution)/shard_map/pallas_call | solution.py:49
  15.7 67.6 %all-to-all-done = bf16[32,8,8,768]{3,2,1,0:T(8,128)(2,1)} async-done(((bf16[32,8,8,768]{3,2,1,0:T(8,128)(2,1)}), bf16[32,8,8,768]{3,2,1,0:T(8,128)(2,1)}, u32[]{:S(2)}, u32[]{:S(2)}) %all-to-all-start) | async-done | bytes 3145760 | tf_op jit(solution)/shard_map/all_to_all | solution.py:295
  83.3 4.0 %all-to-all-start.1 = ((bf16[32,8,8,768]{3,2,1,0:T(8,128)(2,1)}), bf16[32,8,8,768]{3,2,1,0:T(8,128)(2,1)}, u32[]{:S(2)}, u32[]{:S(2)}) async-start(bf16[32,8,8,768]{3,2,1,0:T(8,128)(2,1)} %shard_map.110), calls=%async_computation.1 | async-start | bytes 6291456 | tf_op jit(solution)/shard_map/all_to_all | solution.py:295
  87.3 7.7 %shard_map.112 = (bf16[8,256,768]{2,1,0:T(8,128)(2,1)}, bf16[32,8,8,768]{3,2,1,0:T(8,128)(2,1)}) custom-call(bf16[256,8,768]{2,1,0:T(8,128)(2,1)} %bitcast.2.m_ref.g_ref, bf16[8,256,768]{2,1,0:T(8,128)(2,1)} %k_ref.3, bf16[256,256]{1,0:T(8,128)(2,1)} %o_ref.3, bf16[256,256]{1,0:T(8,128)(2,1)} %b_ref.3), custom_call_target="tpu_custom_call" | custom-call | flops 1610612736 | bytes 12582912 | tf_op jit(solution)/shard_map/pallas_call | solution.py:110
  95.1 63.7 %all-to-all-done.1 = bf16[32,8,8,768]{3,2,1,0:T(8,128)(2,1)} async-done(((bf16[32,8,8,768]{3,2,1,0:T(8,128)(2,1)}), bf16[32,8,8,768]{3,2,1,0:T(8,128)(2,1)}, u32[]{:S(2)}, u32[]{:S(2)}) %all-to-all-start.1) | async-done | bytes 3145760 | tf_op jit(solution)/shard_map/all_to_all | solution.py:295
  158.8 4.0 %all-to-all-start.2 = ((bf16[32,8,8,768]{3,2,1,0:T(8,128)(2,1)}), bf16[32,8,8,768]{3,2,1,0:T(8,128)(2,1)}, u32[]{:S(2)}, u32[]{:S(2)}) async-start(bf16[32,8,8,768]{3,2,1,0:T(8,128)(2,1)} %get-tuple-element.28), calls=%async_computation.2 | async-start | bytes 6291456 | tf_op jit(solution)/shard_map/all_to_all | solution.py:295
  162.8 10.5 %shard_map.113 = (bf16[32,8,8,768]{3,2,1,0:T(8,128)(2,1)}, f32[256,256]{1,0:T(8,128)}, f32[256,256]{1,0:T(8,128)}) custom-call(bf16[256,8,768]{2,1,0:T(8,128)(2,1)} %bitcast.3.f_ref, bf16[256,8,768]{2,1,0:T(8,128)(2,1)} %bitcast.2.m_ref.g_ref, bf16[8,256,768]{2,1,0:T(8,128)(2,1)} %k_ref.3, bf16[8,256,768]{2,1,0:T(8,128)(2,1)} %get-tuple-element.26.gw_ref, ...), custom_call_target="tpu_custom_call" | custom-call | flops 3221225472 | bytes 15728640 | tf_op jit(solution)/shard_map/pallas_call | solution.py:160
  173.3 60.9 %all-to-all-done.2.g_ref = bf16[32,8,8,768]{3,2,1,0:T(8,128)(2,1)} async-done(((bf16[32,8,8,768]{3,2,1,0:T(8,128)(2,1)}), bf16[32,8,8,768]{3,2,1,0:T(8,128)(2,1)}, u32[]{:S(2)}, u32[]{:S(2)}) %all-to-all-start.2) | async-done | bytes 3145760 | tf_op jit(solution)/shard_map/all_to_all | solution.py:295
  234.3 4.0 %all-to-all-start.3 = ((bf16[32,8,8,768]{3,2,1,0:T(8,128)(2,1)}), bf16[32,8,8,768]{3,2,1,0:T(8,128)(2,1)}, u32[]{:S(2)}, u32[]{:S(2)}) async-start(bf16[32,8,8,768]{3,2,1,0:T(8,128)(2,1)} %get-tuple-element.31), calls=%async_computation.3 | async-start | bytes 6291456 | tf_op jit(solution)/shard_map/all_to_all | solution.py:295
  238.4 0.0 copy-start
  238.4 0.0 copy-start.1
  238.4 5.3 %shard_map.114 = (bf16[8,256,768]{2,1,0:T(8,128)(2,1)}, f32[256,256]{1,0:T(8,128)}) custom-call(bf16[32,8,8,768]{3,2,1,0:T(8,128)(2,1)} %all-to-all-done.2.g_ref, bf16[8,256,768]{2,1,0:T(8,128)(2,1)} %bitcast.24, bf16[256,256]{1,0:T(8,128)(2,1)} %f_ref.5), custom_call_target="tpu_custom_call" | custom-call | flops 1610612736 | bytes 9437184 | tf_op jit(solution)/shard_map/pallas_call | solution.py:194
  243.7 0.0 copy-done
  243.7 0.0 copy-done.1
  243.7 1.0 pad_maximum_fusion
  244.7 0.3 collective-permute-start
  245.0 1.5 collective-permute-done
  246.6 1.8 collective-permute-start.1
  248.4 16.9 %collective-permute-done.1 = f32[64,768]{1,0:T(8,128)S(1)} collective-permute-done((f32[64,768]{1,0:T(8,128)S(1)}, f32[64,768]{1,0:T(8,128)S(1)}, u32[]{:S(2)}, u32[]{:S(2)}) %collective-permute-start.1) | collective-permute-done | bytes 196640 | tf_op jit(solution)/shard_map/ppermute | solution.py:291
  265.3 1.1 collective-permute-start.2
  266.4 5.4 %collective-permute-done.2 = f32[32,768]{1,0:T(8,128)S(1)} collective-permute-done((f32[32,768]{1,0:T(8,128)S(1)}, f32[32,768]{1,0:T(8,128)S(1)}, u32[]{:S(2)}, u32[]{:S(2)}) %collective-permute-start.2) | collective-permute-done | bytes 98336 | tf_op jit(solution)/shard_map/ppermute | solution.py:291
  271.8 0.1 collective-permute-start.3
  271.9 20.4 %collective-permute-done.3 = f32[32,768]{1,0:T(8,128)S(1)} collective-permute-done((f32[32,768]{1,0:T(8,128)S(1)}, f32[32,768]{1,0:T(8,128)S(1)}, u32[]{:S(2)}, u32[]{:S(2)}) %collective-permute-start.3) | collective-permute-done | bytes 98336 | tf_op jit(solution)/shard_map/ppermute | solution.py:291
  292.3 17.6 %all-to-all-done.3.r_ref = bf16[32,8,8,768]{3,2,1,0:T(8,128)(2,1)} async-done(((bf16[32,8,8,768]{3,2,1,0:T(8,128)(2,1)}), bf16[32,8,8,768]{3,2,1,0:T(8,128)(2,1)}, u32[]{:S(2)}, u32[]{:S(2)}) %all-to-all-start.3) | async-done | bytes 3145760 | tf_op jit(solution)/shard_map/all_to_all | solution.py:295
  309.9 0.0 collective-permute-start.4
  309.9 4.1 %shard_map.115 = bf16[256,256]{1,0:T(8,128)(2,1)} custom-call(bf16[32,8,8,768]{3,2,1,0:T(8,128)(2,1)} %all-to-all-done.3.r_ref, bf16[8,256,768]{2,1,0:T(8,128)(2,1)} %bitcast.26), custom_call_target="tpu_custom_call" | custom-call | flops 805306368 | bytes 6291456 | tf_op jit(solution)/shard_map/pallas_call | solution.py:227
  314.0 0.9 collective-permute-done.4
  314.9 1.2 collective-permute-start.5
  316.1 3.4 all-to-all-start.4
  319.4 0.1 collective-permute-done.5
  319.6 1.7 collective-permute-start.6
  321.3 6.3 %all-to-all-done.4 = bf16[32,8,256]{2,1,0:T(8,128)(2,1)S(1)} async-done(((bf16[32,8,256]{2,1,0:T(8,128)(2,1)}), bf16[32,8,256]{2,1,0:T(8,128)(2,1)S(1)}, u32[]{:S(2)}, u32[]{:S(2)}) %all-to-all-start.4) | async-done | bytes 131104 | tf_op jit(solution)/shard_map/all_to_all | solution.py:295
  327.7 0.7 broadcast_in_dim.10
  328.4 2.6 all-to-all-start.5
  331.0 0.0 collective-permute-done.6
  331.0 0.2 collective-permute-start.7
  331.2 8.0 %all-to-all-done.5 = bf16[32,8,256]{2,1,0:T(8,128)(2,1)S(1)} async-done(((bf16[32,8,256]{2,1,0:T(8,128)(2,1)}), bf16[32,8,256]{2,1,0:T(8,128)(2,1)S(1)}, u32[]{:S(2)}, u32[]{:S(2)}) %all-to-all-start.5) | async-done | bytes 131104 | tf_op jit(solution)/shard_map/all_to_all | solution.py:295
  339.2 0.7 multiply_bitcast_fusion
  339.9 0.0 collective-permute-done.7
  339.9 0.1 broadcast_select_fusion.1
  340.0 0.1 maximum_multiply_fusion
  340.1 0.9 fusion
  (13 shorter events, 0.3 us)
Async XLA Ops:
  4.4 78.9 %all-to-all-start = ((bf16[32,8,8,768]{3,2,1,0:T(8,128)(2,1)}), bf16[32,8,8,768]{3,2,1,0:T(8,128)(2,1)}, u32[]{:S(2)}, u32[]{:S(2)}) async-start(bf16[32,8,8,768]{3,2,1,0:T(8,128)(2,1)} %shard_map.111), calls=%async_computation | async-start | bytes 6291456 | tf_op jit(solution)/shard_map/all_to_all | solution.py:295
  83.3 75.5 %all-to-all-start.1 = ((bf16[32,8,8,768]{3,2,1,0:T(8,128)(2,1)}), bf16[32,8,8,768]{3,2,1,0:T(8,128)(2,1)}, u32[]{:S(2)}, u32[]{:S(2)}) async-start(bf16[32,8,8,768]{3,2,1,0:T(8,128)(2,1)} %shard_map.110), calls=%async_computation.1 | async-start | bytes 6291456 | tf_op jit(solution)/shard_map/all_to_all | solution.py:295
  158.8 75.5 %all-to-all-start.2 = ((bf16[32,8,8,768]{3,2,1,0:T(8,128)(2,1)}), bf16[32,8,8,768]{3,2,1,0:T(8,128)(2,1)}, u32[]{:S(2)}, u32[]{:S(2)}) async-start(bf16[32,8,8,768]{3,2,1,0:T(8,128)(2,1)} %get-tuple-element.28), calls=%async_computation.2 | async-start | bytes 6291456 | tf_op jit(solution)/shard_map/all_to_all | solution.py:295
  234.3 75.6 %all-to-all-start.3 = ((bf16[32,8,8,768]{3,2,1,0:T(8,128)(2,1)}), bf16[32,8,8,768]{3,2,1,0:T(8,128)(2,1)}, u32[]{:S(2)}, u32[]{:S(2)}) async-start(bf16[32,8,8,768]{3,2,1,0:T(8,128)(2,1)} %get-tuple-element.31), calls=%async_computation.3 | async-start | bytes 6291456 | tf_op jit(solution)/shard_map/all_to_all | solution.py:295
  238.4 5.3 %copy-start = (f32[256,256]{1,0:T(8,128)S(1)}, f32[256,256]{1,0:T(8,128)}, u32[]{:S(2)}) copy-start(f32[256,256]{1,0:T(8,128)} %get-tuple-element.33) | copy-start | bytes 786436
  238.4 5.3 %copy-start.1 = (f32[256,256]{1,0:T(8,128)S(1)}, f32[256,256]{1,0:T(8,128)}, u32[]{:S(2)}) copy-start(f32[256,256]{1,0:T(8,128)} %get-tuple-element.34) | copy-start | bytes 786436
  244.7 1.8 collective-permute-start
  246.6 18.6 %collective-permute-start.1 = (f32[64,768]{1,0:T(8,128)S(1)}, f32[64,768]{1,0:T(8,128)S(1)}, u32[]{:S(2)}, u32[]{:S(2)}) collective-permute-start(f32[64,768]{1,0:T(8,128)S(1)} %dynamic-slice_bitcast_fusion.1), channel_id=1, source_target_pairs={{0,2},{1,3},{2,0},{3,1},{4,6},{5,7},{6,4},{7,5},{8,10},{9,11},{10,... | collective-permute-start | bytes 589832 | tf_op jit(solution)/shard_map/ppermute | solution.py:291
  265.3 6.5 %collective-permute-start.2 = (f32[32,768]{1,0:T(8,128)S(1)}, f32[32,768]{1,0:T(8,128)S(1)}, u32[]{:S(2)}, u32[]{:S(2)}) collective-permute-start(f32[32,768]{1,0:T(8,128)S(1)} %dynamic-slice_bitcast_fusion.2), channel_id=1, source_target_pairs={{0,4},{1,5},{2,6},{3,7},{4,0},{5,1},{6,2},{7,3},{8,12},{9,13},{10,... | collective-permute-start | bytes 294920 | tf_op jit(solution)/shard_map/ppermute | solution.py:291
  271.8 20.5 %collective-permute-start.3 = (f32[32,768]{1,0:T(8,128)S(1)}, f32[32,768]{1,0:T(8,128)S(1)}, u32[]{:S(2)}, u32[]{:S(2)}) collective-permute-start(f32[32,768]{1,0:T(8,128)S(1)} %bitcast_add_fusion.2), channel_id=1, source_target_pairs={{0,8},{1,9},{2,10},{3,11},{4,12},{5,13},{6,14},{7,15},{8,0},{9,1},... | collective-permute-start | bytes 294920 | tf_op jit(solution)/shard_map/ppermute | solution.py:291
  309.9 5.0 %collective-permute-start.4 = (bf16[32,768]{1,0:T(8,128)(2,1)S(1)}, bf16[32,768]{1,0:T(8,128)(2,1)S(1)}, u32[]{:S(2)}, u32[]{:S(2)}) collective-permute-start(bf16[32,768]{1,0:T(8,128)(2,1)S(1)} %add.67), channel_id=1, source_target_pairs={{0,16},{1,17},{2,18},{3,19},{4,20},{5,21},{6,22},{7,23},{8,24},{9,... | collective-permute-start | bytes 147464 | tf_op jit(solution)/shard_map/ppermute | solution.py:291
  314.9 4.7 %collective-permute-start.5 = (f32[32,768]{1,0:T(8,128)S(1)}, f32[32,768]{1,0:T(8,128)S(1)}, u32[]{:S(2)}, u32[]{:S(2)}) collective-permute-start(f32[32,768]{1,0:T(8,128)S(1)} %convert_add_fusion), channel_id=1, source_target_pairs={{0,4},{1,5},{2,6},{3,7},{4,0},{5,1},{6,2},{7,3},{8,12},{9,13},{10,... | collective-permute-start | bytes 294920 | tf_op jit(solution)/shard_map/ppermute | solution.py:291
  316.1 11.6 %all-to-all-start.4 = ((bf16[32,8,256]{2,1,0:T(8,128)(2,1)}), bf16[32,8,256]{2,1,0:T(8,128)(2,1)S(1)}, u32[]{:S(2)}, u32[]{:S(2)}) async-start(bf16[32,8,256]{2,1,0:T(8,128)(2,1)} %bitcast.33), calls=%async_computation.4 | async-start | bytes 262144 | tf_op jit(solution)/shard_map/all_to_all | solution.py:295
  319.6 11.4 %collective-permute-start.6 = (f32[64,768]{1,0:T(8,128)S(1)}, f32[64,768]{1,0:T(8,128)S(1)}, u32[]{:S(2)}, u32[]{:S(2)}) collective-permute-start(f32[64,768]{1,0:T(8,128)S(1)} %pad_maximum_fusion.2), channel_id=1, source_target_pairs={{0,2},{1,3},{2,0},{3,1},{4,6},{5,7},{6,4},{7,5},{8,10},{9,11},{10,... | collective-permute-start | bytes 589832 | tf_op jit(solution)/shard_map/ppermute | solution.py:291
  328.4 10.8 %all-to-all-start.5 = ((bf16[32,8,256]{2,1,0:T(8,128)(2,1)}), bf16[32,8,256]{2,1,0:T(8,128)(2,1)S(1)}, u32[]{:S(2)}, u32[]{:S(2)}) async-start(bf16[32,8,256]{2,1,0:T(8,128)(2,1)} %broadcast_in_dim.10), calls=%async_computation.5 | async-start | bytes 262144 | tf_op jit(solution)/shard_map/all_to_all | solution.py:295
  331.0 8.9 %collective-permute-start.7 = (f32[128,768]{1,0:T(8,128)S(1)}, f32[128,768]{1,0:T(8,128)S(1)}, u32[]{:S(2)}, u32[]{:S(2)}) collective-permute-start(f32[128,768]{1,0:T(8,128)S(1)} %pad_maximum_fusion.1), channel_id=1, source_target_pairs={{0,1},{1,0},{2,3},{3,2},{4,5},{5,4},{6,7},{7,6},{8,9},{9,8},{10,11... | collective-permute-start | bytes 1179656 | tf_op jit(solution)/shard_map/ppermute | solution.py:291

commit v7 on v6

--- a/solution.py
+++ b/solution.py
@@ -208,34 +208,25 @@
 def finish_return(returned, cotangent):
     members, rows, part, channels = returned.shape
     order = members * part
-    step = max(1, rows // 2)
-    steps = rows // step
-
-    def body(r_ref, c_ref, o_ref, acc):
-        @pl.when(pl.program_id(0) == 0)
-        def _():
-            acc[...] = jnp.zeros_like(acc)
-
-        for r in range(step):
+
+    def body(r_ref, c_ref, o_ref):
+        acc = jnp.zeros((order, order), F32)
+        for r in range(rows):
             ret = r_ref[:, r].astype(F32).reshape(order, channels).astype(BF16)
-            acc[...] += dot(c_ref[r], ret, (1, 1))
-
-        @pl.when(pl.program_id(0) == steps - 1)
-        def _():
-            o_ref[...] = acc[...].astype(BF16)
-
-    return call(
-        body,
-        (steps,),
-        [
-            pl.BlockSpec((members, step, part, channels), lambda g: (0, g, 0, 0)),
-            pl.BlockSpec((step, order, channels), lambda g: (g, 0, 0)),
-        ],
-        [(square(order), jax.ShapeDtypeStruct((order, order), BF16))],
-        [pltpu.VMEM((order, order), F32)],
-        2 * order * cotangent.size,
-        4 * cotangent.size,
-    )(returned, cotangent)[0]
+            acc += dot(c_ref[r], ret, (1, 1))
+        o_ref[...] = acc.astype(BF16)
+
+    whole = pl.BlockSpec(memory_space=pltpu.VMEM)
+    return pl.pallas_call(
+        body,
+        in_specs=[whole, whole],
+        out_specs=whole,
+        out_shape=jax.ShapeDtypeStruct((order, order), BF16),
+        compiler_params=pltpu.CompilerParams(vmem_limit_bytes=24 * 2**20),
+        cost_estimate=pl.CostEstimate(
+            flops=2 * order * cotangent.size, bytes_accessed=4 * cotangent.size, transcendentals=0
+        ),
+    )(returned, cotangent)
 
 
 def plain(values, kernel, cotangent, inner_factor, outer_factor, return_outer, return_inner):
@@ -364,7 +355,6 @@
     grad_values, grad_inner = finish_values(grad_first, values[0], inner_factor)
     early = plane_sum(jnp.concatenate((grad_inner, grad_outer, grad_back), axis=1))
     early = early + swap(early, 8)
-    returned, early = lax.optimization_barrier((returned, early))
     early = early.astype(BF16)
     other = swap(early, 16)
     grad_last = finish_return(returned, cotangent[0])

time: 341 us -> 341 us (level)
  waiting for transfers between devices: 269 us -> 261 us
  starting transfers between devices: 31.8 us -> 35.3 us
    ppermute x8, waiting for transfers between devices: 45.2 us -> 39.5 us  [swap(): return lax.ppermute(x, 'seq', [(i, i ^ bits) for i in range(size)])]
    ppermute x8, starting transfers between devices: 6.28 us -> 10.2 us  [swap(): return lax.ppermute(x, 'seq', [(i, i ^ bits) for i in range(size)])]
  transfers between devices with their start and end apart: 14 -> 14, of which waited for: 12 -> 11; matrix products, arithmetic and copies ran while one was open for 1% -> 2% of each run, Pallas kernels for 9% -> 9%
where the time goes in v7:
time: 341 us
  waiting for transfers between devices  261 us (77%)
  starting transfers between devices  35.3 us (10%)
  Pallas kernels  34.7 us (10%)
  other arithmetic  5.25 us (2%)
  local copies, waits for them, and re-layouts  3.86 us (1%)
    all_to_all x6, waiting for transfers between devices, move(): return lax.all_to_all(x, 'seq', 0, 0, tiled=True)  221 us
    ppermute x8, waiting for transfers between devices, swap(): return lax.ppermute(x, 'seq', [(i, i ^ bits) for i in range(size)])  39.5 us
    all_to_all x6, starting transfers between devices, move(): return lax.all_to_all(x, 'seq', 0, 0, tiled=True)  25 us
    pallas_call x1, Pallas kernels, forward_mixed(): call(body, (channels // width,), [moved, moved, mine, mine, square(order)...  10.6 us
    ppermute x8, starting transfers between devices, swap(): return lax.ppermute(x, 'seq', [(i, i ^ bits) for i in range(size)])  10.2 us
    pallas_call x1, Pallas kernels, backward_mixed(): call(body, (channels // width,), [pl.BlockSpec((order, part, width), lamb...  7.77 us
    pallas_call x2, Pallas kernels, apply_inner(): call(body, (rows // step,), [pl.BlockSpec((step, order, channels), lambda...  7.56 us
  transfers between devices with their start and end apart: 14, of which 11 were waited for; matrix products, arithmetic and copies ran while one was open for 2% of the time, Pallas kernels for 9%

profile of v7, /device:TPU:0, one launch (start us, length us, event | category | flops | bytes accessed | tf_op | source)
XLA Modules:
  0.0 340.6 jit_solution(16721834855136190622)
XLA Ops:
  0.6 3.8 %shard_map.111 = bf16[32,8,8,768]{3,2,1,0:T(8,128)(2,1)} custom-call(bf16[8,256,768]{2,1,0:T(8,128)(2,1)} %bitcast.23, bf16[256,256]{1,0:T(8,128)(2,1)} %f_ref.4), custom_call_target="tpu_custom_call" | custom-call | flops 805306368 | bytes 6291456 | tf_op jit(solution)/shard_map/pallas_call | solution.py:49
  4.4 7.4 %all-to-all-start = ((bf16[32,8,8,768]{3,2,1,0:T(8,128)(2,1)}), bf16[32,8,8,768]{3,2,1,0:T(8,128)(2,1)}, u32[]{:S(2)}, u32[]{:S(2)}) async-start(bf16[32,8,8,768]{3,2,1,0:T(8,128)(2,1)} %shard_map.111), calls=%async_computation | async-start | bytes 6291456 | tf_op jit(solution)/shard_map/all_to_all | solution.py:286
  11.8 3.8 %shard_map.110 = bf16[32,8,8,768]{3,2,1,0:T(8,128)(2,1)} custom-call(bf16[8,256,768]{2,1,0:T(8,128)(2,1)} %bitcast.25, bf16[256,256]{1,0:T(8,128)(2,1)} %f_ref.5), custom_call_target="tpu_custom_call" | custom-call | flops 805306368 | bytes 6291456 | tf_op jit(solution)/shard_map/pallas_call | solution.py:49
  15.6 67.7 %all-to-all-done = bf16[32,8,8,768]{3,2,1,0:T(8,128)(2,1)} async-done(((bf16[32,8,8,768]{3,2,1,0:T(8,128)(2,1)}), bf16[32,8,8,768]{3,2,1,0:T(8,128)(2,1)}, u32[]{:S(2)}, u32[]{:S(2)}) %all-to-all-start) | async-done | bytes 3145760 | tf_op jit(solution)/shard_map/all_to_all | solution.py:286
  83.3 4.0 %all-to-all-start.1 = ((bf16[32,8,8,768]{3,2,1,0:T(8,128)(2,1)}), bf16[32,8,8,768]{3,2,1,0:T(8,128)(2,1)}, u32[]{:S(2)}, u32[]{:S(2)}) async-start(bf16[32,8,8,768]{3,2,1,0:T(8,128)(2,1)} %shard_map.110), calls=%async_computation.1 | async-start | bytes 6291456 | tf_op jit(solution)/shard_map/all_to_all | solution.py:286
  87.3 7.8 %shard_map.112 = (bf16[8,256,768]{2,1,0:T(8,128)(2,1)}, bf16[32,8,8,768]{3,2,1,0:T(8,128)(2,1)}) custom-call(bf16[256,8,768]{2,1,0:T(8,128)(2,1)} %bitcast.2.m_ref.g_ref, bf16[8,256,768]{2,1,0:T(8,128)(2,1)} %k_ref.3, bf16[256,256]{1,0:T(8,128)(2,1)} %o_ref.3, bf16[256,256]{1,0:T(8,128)(2,1)} %b_ref.3), custom_call_target="tpu_custom_call" | custom-call | flops 1610612736 | bytes 12582912 | tf_op jit(solution)/shard_map/pallas_call | solution.py:110
  95.1 63.7 %all-to-all-done.1 = bf16[32,8,8,768]{3,2,1,0:T(8,128)(2,1)} async-done(((bf16[32,8,8,768]{3,2,1,0:T(8,128)(2,1)}), bf16[32,8,8,768]{3,2,1,0:T(8,128)(2,1)}, u32[]{:S(2)}, u32[]{:S(2)}) %all-to-all-start.1) | async-done | bytes 3145760 | tf_op jit(solution)/shard_map/all_to_all | solution.py:286
  158.8 4.0 %all-to-all-start.2 = ((bf16[32,8,8,768]{3,2,1,0:T(8,128)(2,1)}), bf16[32,8,8,768]{3,2,1,0:T(8,128)(2,1)}, u32[]{:S(2)}, u32[]{:S(2)}) async-start(bf16[32,8,8,768]{3,2,1,0:T(8,128)(2,1)} %get-tuple-element.26), calls=%async_computation.2 | async-start | bytes 6291456 | tf_op jit(solution)/shard_map/all_to_all | solution.py:286
  162.8 10.6 %shard_map.113 = (bf16[32,8,8,768]{3,2,1,0:T(8,128)(2,1)}, f32[256,256]{1,0:T(8,128)}, f32[256,256]{1,0:T(8,128)}) custom-call(bf16[256,8,768]{2,1,0:T(8,128)(2,1)} %bitcast.3.f_ref, bf16[256,8,768]{2,1,0:T(8,128)(2,1)} %bitcast.2.m_ref.g_ref, bf16[8,256,768]{2,1,0:T(8,128)(2,1)} %k_ref.3, bf16[8,256,768]{2,1,0:T(8,128)(2,1)} %get-tuple-element.24.gw_ref, ...), custom_call_target="tpu_custom_call" | custom-call | flops 3221225472 | bytes 15728640 | tf_op jit(solution)/shard_map/pallas_call | solution.py:160
  173.4 60.9 %all-to-all-done.2.g_ref = bf16[32,8,8,768]{3,2,1,0:T(8,128)(2,1)} async-done(((bf16[32,8,8,768]{3,2,1,0:T(8,128)(2,1)}), bf16[32,8,8,768]{3,2,1,0:T(8,128)(2,1)}, u32[]{:S(2)}, u32[]{:S(2)}) %all-to-all-start.2) | async-done | bytes 3145760 | tf_op jit(solution)/shard_map/all_to_all | solution.py:286
  234.3 4.0 %all-to-all-start.3 = ((bf16[32,8,8,768]{3,2,1,0:T(8,128)(2,1)}), bf16[32,8,8,768]{3,2,1,0:T(8,128)(2,1)}, u32[]{:S(2)}, u32[]{:S(2)}) async-start(bf16[32,8,8,768]{3,2,1,0:T(8,128)(2,1)} %get-tuple-element.32), calls=%async_computation.3 | async-start | bytes 6291456 | tf_op jit(solution)/shard_map/all_to_all | solution.py:286
  238.4 0.0 copy-start.3
  238.4 5.2 %shard_map.114 = (bf16[8,256,768]{2,1,0:T(8,128)(2,1)}, f32[256,256]{1,0:T(8,128)}) custom-call(bf16[32,8,8,768]{3,2,1,0:T(8,128)(2,1)} %all-to-all-done.2.g_ref, bf16[8,256,768]{2,1,0:T(8,128)(2,1)} %bitcast.26, bf16[256,256]{1,0:T(8,128)(2,1)} %f_ref.5), custom_call_target="tpu_custom_call" | custom-call | flops 1610612736 | bytes 9437184 | tf_op jit(solution)/shard_map/pallas_call | solution.py:194
  243.6 1.2 pad_maximum_fusion
  244.9 0.9 copy-done.1
  245.8 0.3 collective-permute-start
  246.0 1.7 collective-permute-done
  247.7 1.2 bitcast_add_fusion
  248.9 0.7 dynamic-slice_bitcast_fusion.1
  249.6 1.7 collective-permute-start.1
  251.3 14.1 %collective-permute-done.1 = f32[64,768]{1,0:T(8,128)} collective-permute-done((f32[64,768]{1,0:T(8,128)}, f32[64,768]{1,0:T(8,128)}, u32[]{:S(2)}, u32[]{:S(2)}) %collective-permute-start.1) | collective-permute-done | bytes 196640 | tf_op jit(solution)/shard_map/ppermute | solution.py:282
  265.3 0.9 bitcast_add_fusion.1
  266.3 0.0 copy-start.2
  266.3 0.7 copy-done.2
  267.0 1.1 collective-permute-start.2
  268.1 8.1 %collective-permute-done.2 = f32[32,768]{1,0:T(8,128)S(1)} collective-permute-done((f32[32,768]{1,0:T(8,128)S(1)}, f32[32,768]{1,0:T(8,128)S(1)}, u32[]{:S(2)}, u32[]{:S(2)}) %collective-permute-start.2) | collective-permute-done | bytes 98336 | tf_op jit(solution)/shard_map/ppermute | solution.py:282
  276.1 0.9 bitcast_add_fusion.2
  277.0 0.1 collective-permute-start.3
  277.1 15.2 %collective-permute-done.3 = f32[32,768]{1,0:T(8,128)S(1)} collective-permute-done((f32[32,768]{1,0:T(8,128)S(1)}, f32[32,768]{1,0:T(8,128)S(1)}, u32[]{:S(2)}, u32[]{:S(2)}) %collective-permute-start.3) | collective-permute-done | bytes 98336 | tf_op jit(solution)/shard_map/ppermute | solution.py:282
  292.3 4.4 %collective-permute-start.4 = (bf16[32,768]{1,0:T(8,128)(2,1)S(1)}, bf16[32,768]{1,0:T(8,128)(2,1)S(1)}, u32[]{:S(2)}, u32[]{:S(2)}) collective-permute-start(bf16[32,768]{1,0:T(8,128)(2,1)S(1)} %add_convert_fusion), channel_id=1, source_target_pairs={{0,16},{1,17},{2,18},{3,19},{4,20},{5,21},{6,22},{7,23},{8,24},{9,... | collective-permute-start | bytes 147464 | tf_op jit(solution)/shard_map/ppermute | solution.py:282
  296.7 14.7 %all-to-all-done.3.r_ref = bf16[32,8,8,768]{3,2,1,0:T(8,128)(2,1)} async-done(((bf16[32,8,8,768]{3,2,1,0:T(8,128)(2,1)}), bf16[32,8,8,768]{3,2,1,0:T(8,128)(2,1)}, u32[]{:S(2)}, u32[]{:S(2)}) %all-to-all-start.3) | async-done | bytes 3145760 | tf_op jit(solution)/shard_map/all_to_all | solution.py:286
  311.4 3.6 %shard_map.115 = bf16[256,256]{1,0:T(8,128)(2,1)} custom-call(bf16[32,8,8,768]{3,2,1,0:T(8,128)(2,1)} %all-to-all-done.3.r_ref, bf16[8,256,768]{2,1,0:T(8,128)(2,1)S(1)} %bitcast.24), custom_call_target="tpu_custom_call" | custom-call | flops 805306368 | bytes 6291456 | tf_op jit(solution)/shard_map/pallas_call | solution.py:220
  315.0 0.0 collective-permute-done.4
  315.0 1.2 collective-permute-start.5
  316.2 2.9 all-to-all-start.4
  319.1 0.5 collective-permute-done.5
  319.7 1.3 collective-permute-start.6
  321.0 6.3 %all-to-all-done.4 = bf16[32,8,256]{2,1,0:T(8,128)(2,1)S(1)} async-done(((bf16[32,8,256]{2,1,0:T(8,128)(2,1)}), bf16[32,8,256]{2,1,0:T(8,128)(2,1)S(1)}, u32[]{:S(2)}, u32[]{:S(2)}) %all-to-all-start.4) | async-done | bytes 131104 | tf_op jit(solution)/shard_map/all_to_all | solution.py:286
  327.4 0.7 broadcast_in_dim.10
  328.1 2.6 all-to-all-start.5
  330.7 0.0 collective-permute-done.6
  330.7 0.2 collective-permute-start.7
  330.9 8.0 %all-to-all-done.5 = bf16[32,8,256]{2,1,0:T(8,128)(2,1)S(1)} async-done(((bf16[32,8,256]{2,1,0:T(8,128)(2,1)}), bf16[32,8,256]{2,1,0:T(8,128)(2,1)S(1)}, u32[]{:S(2)}, u32[]{:S(2)}) %all-to-all-start.5) | async-done | bytes 131104 | tf_op jit(solution)/shard_map/all_to_all | solution.py:286
  338.9 0.7 multiply_bitcast_fusion
  339.6 0.0 collective-permute-done.7
  339.6 0.1 broadcast_select_fusion.1
  339.7 0.1 maximum_multiply_fusion
  339.7 0.9 fusion
  (13 shorter events, 0.2 us)
Async XLA Ops:
  4.4 78.9 %all-to-all-start = ((bf16[32,8,8,768]{3,2,1,0:T(8,128)(2,1)}), bf16[32,8,8,768]{3,2,1,0:T(8,128)(2,1)}, u32[]{:S(2)}, u32[]{:S(2)}) async-start(bf16[32,8,8,768]{3,2,1,0:T(8,128)(2,1)} %shard_map.111), calls=%async_computation | async-start | bytes 6291456 | tf_op jit(solution)/shard_map/all_to_all | solution.py:286
  83.3 75.5 %all-to-all-start.1 = ((bf16[32,8,8,768]{3,2,1,0:T(8,128)(2,1)}), bf16[32,8,8,768]{3,2,1,0:T(8,128)(2,1)}, u32[]{:S(2)}, u32[]{:S(2)}) async-start(bf16[32,8,8,768]{3,2,1,0:T(8,128)(2,1)} %shard_map.110), calls=%async_computation.1 | async-start | bytes 6291456 | tf_op jit(solution)/shard_map/all_to_all | solution.py:286
  158.8 75.5 %all-to-all-start.2 = ((bf16[32,8,8,768]{3,2,1,0:T(8,128)(2,1)}), bf16[32,8,8,768]{3,2,1,0:T(8,128)(2,1)}, u32[]{:S(2)}, u32[]{:S(2)}) async-start(bf16[32,8,8,768]{3,2,1,0:T(8,128)(2,1)} %get-tuple-element.26), calls=%async_computation.2 | async-start | bytes 6291456 | tf_op jit(solution)/shard_map/all_to_all | solution.py:286
  234.3 77.1 %all-to-all-start.3 = ((bf16[32,8,8,768]{3,2,1,0:T(8,128)(2,1)}), bf16[32,8,8,768]{3,2,1,0:T(8,128)(2,1)}, u32[]{:S(2)}, u32[]{:S(2)}) async-start(bf16[32,8,8,768]{3,2,1,0:T(8,128)(2,1)} %get-tuple-element.32), calls=%async_computation.3 | async-start | bytes 6291456 | tf_op jit(solution)/shard_map/all_to_all | solution.py:286
  238.4 5.2 %copy-start.3 = (f32[256,256]{1,0:T(8,128)S(1)}, f32[256,256]{1,0:T(8,128)}, u32[]{:S(2)}) copy-start(f32[256,256]{1,0:T(8,128)} %get-tuple-element.30) | copy-start | bytes 786436
  243.6 67.8 %copy-start = (bf16[1,8,256,768]{3,2,1,0:T(8,128)(2,1)S(1)}, bf16[1,8,256,768]{3,2,1,0:T(8,128)(2,1)}, u32[]{:S(2)}) copy-start(bf16[1,8,256,768]{3,2,1,0:T(8,128)(2,1)} %param.9) | copy-start | bytes 9437188
  244.9 0.9 copy-start.1
  245.8 1.9 collective-permute-start
  249.6 15.8 %collective-permute-start.1 = (f32[64,768]{1,0:T(8,128)}, f32[64,768]{1,0:T(8,128)}, u32[]{:S(2)}, u32[]{:S(2)}) collective-permute-start(f32[64,768]{1,0:T(8,128)} %dynamic-slice_bitcast_fusion.1), channel_id=1, source_target_pairs={{0,2},{1,3},{2,0},{3,1},{4,6},{5,7},{6,4},{7,5},{8,10},{9,11},{10,... | collective-permute-start | bytes 589832 | tf_op jit(solution)/shard_map/ppermute | solution.py:282
  266.3 0.7 copy-start.2
  267.0 9.1 %collective-permute-start.2 = (f32[32,768]{1,0:T(8,128)S(1)}, f32[32,768]{1,0:T(8,128)S(1)}, u32[]{:S(2)}, u32[]{:S(2)}) collective-permute-start(f32[32,768]{1,0:T(8,128)S(1)} %dynamic-slice_bitcast_fusion.2), channel_id=1, source_target_pairs={{0,4},{1,5},{2,6},{3,7},{4,0},{5,1},{6,2},{7,3},{8,12},{9,13},{10,... | collective-permute-start | bytes 294920 | tf_op jit(solution)/shard_map/ppermute | solution.py:282
  277.0 15.2 %collective-permute-start.3 = (f32[32,768]{1,0:T(8,128)S(1)}, f32[32,768]{1,0:T(8,128)S(1)}, u32[]{:S(2)}, u32[]{:S(2)}) collective-permute-start(f32[32,768]{1,0:T(8,128)S(1)} %bitcast_add_fusion.2), channel_id=1, source_target_pairs={{0,8},{1,9},{2,10},{3,11},{4,12},{5,13},{6,14},{7,15},{8,0},{9,1},... | collective-permute-start | bytes 294920 | tf_op jit(solution)/shard_map/ppermute | solution.py:282
  292.3 22.7 %collective-permute-start.4 = (bf16[32,768]{1,0:T(8,128)(2,1)S(1)}, bf16[32,768]{1,0:T(8,128)(2,1)S(1)}, u32[]{:S(2)}, u32[]{:S(2)}) collective-permute-start(bf16[32,768]{1,0:T(8,128)(2,1)S(1)} %add_convert_fusion), channel_id=1, source_target_pairs={{0,16},{1,17},{2,18},{3,19},{4,20},{5,21},{6,22},{7,23},{8,24},{9,... | collective-permute-start | bytes 147464 | tf_op jit(solution)/shard_map/ppermute | solution.py:282
  315.0 4.7 %collective-permute-start.5 = (f32[32,768]{1,0:T(8,128)S(1)}, f32[32,768]{1,0:T(8,128)S(1)}, u32[]{:S(2)}, u32[]{:S(2)}) collective-permute-start(f32[32,768]{1,0:T(8,128)S(1)} %convert_add_fusion), channel_id=1, source_target_pairs={{0,4},{1,5},{2,6},{3,7},{4,0},{5,1},{6,2},{7,3},{8,12},{9,13},{10,... | collective-permute-start | bytes 294920 | tf_op jit(solution)/shard_map/ppermute | solution.py:282
  316.2 11.2 %all-to-all-start.4 = ((bf16[32,8,256]{2,1,0:T(8,128)(2,1)}), bf16[32,8,256]{2,1,0:T(8,128)(2,1)S(1)}, u32[]{:S(2)}, u32[]{:S(2)}) async-start(bf16[32,8,256]{2,1,0:T(8,128)(2,1)} %bitcast.14), calls=%async_computation.4 | async-start | bytes 262144 | tf_op jit(solution)/shard_map/all_to_all | solution.py:286
  319.7 11.0 %collective-permute-start.6 = (f32[64,768]{1,0:T(8,128)S(1)}, f32[64,768]{1,0:T(8,128)S(1)}, u32[]{:S(2)}, u32[]{:S(2)}) collective-permute-start(f32[64,768]{1,0:T(8,128)S(1)} %pad_maximum_fusion.2), channel_id=1, source_target_pairs={{0,2},{1,3},{2,0},{3,1},{4,6},{5,7},{6,4},{7,5},{8,10},{9,11},{10,... | collective-permute-start | bytes 589832 | tf_op jit(solution)/shard_map/ppermute | solution.py:282
  328.1 10.8 %all-to-all-start.5 = ((bf16[32,8,256]{2,1,0:T(8,128)(2,1)}), bf16[32,8,256]{2,1,0:T(8,128)(2,1)S(1)}, u32[]{:S(2)}, u32[]{:S(2)}) async-start(bf16[32,8,256]{2,1,0:T(8,128)(2,1)} %broadcast_in_dim.10), calls=%async_computation.5 | async-start | bytes 262144 | tf_op jit(solution)/shard_map/all_to_all | solution.py:286
  330.7 8.9 %collective-permute-start.7 = (f32[128,768]{1,0:T(8,128)S(1)}, f32[128,768]{1,0:T(8,128)S(1)}, u32[]{:S(2)}, u32[]{:S(2)}) collective-permute-start(f32[128,768]{1,0:T(8,128)S(1)} %pad_maximum_fusion.1), channel_id=1, source_target_pairs={{0,1},{1,0},{2,3},{3,2},{4,5},{5,4},{6,7},{7,6},{8,9},{9,8},{10,11... | collective-permute-start | bytes 1179656 | tf_op jit(solution)/shard_map/ppermute | solution.py:282
